TPU v7x, 32 devices: a whole 2x2x4 slice. The times are simulated.
32 devices in a mesh: blk: 8 (over z, x), mp: 4 (over y, core).
Axes of the slice: x: 2, y: 2, z: 4, core: 2. Of those that a mesh axis runs over, the one named last changes fastest.
Arguments:
- tokens_in: bfloat16 [2048, 2048], P('blk'), may hold values from -17 to 17
- w_qkv: bfloat16 [3, 2048, 2048], P(None, None, 'mp'), may hold values from -0.125 to 0.125
- w_out: bfloat16 [2048, 2048], P('mp'), may hold values from -0.125 to 0.125
- grad_y: bfloat16 [2048, 2048], P('blk'), may hold values from -6 to 6
- block_cols: int32 [16, 2], replicated, may hold values from 0 to 15, as said below
- block_count: int32 [16], replicated, may hold values from 1 to 2, as said below
Outputs:
- grad_x: bfloat16 [2048, 2048], P('blk', 'mp')
- grad_qkv: bfloat16 [3, 2048, 2048], P(None, 'blk', 'mp')
- grad_out: bfloat16 [2048, 2048], P('mp', 'blk')
Inputs may be any that keep to these rules, and one draw needn't show every extreme that they name: `block_cols`: slot 0 of row r is r itself; the first block_count[r] slots of a row are distinct blocks; later slots repeat r. `block_count`: some rows use all 2 slots.
All inputs are finite; a program needn't handle non-finite values.
Results may differ from a plain program's by a relative error of at most 0.02.
Values may be sent and summed in bfloat16 or wider, within the bound.
No kernel may reach another device: no remote copies, remote signals or barrier semaphores. Data moves between devices by JAX's collectives and lax.ppermute only.
A program may use at most 64 MiB of HBM per device.

v0:
```python
import math

import jax
import jax.numpy as jnp
from jax import lax
from jax.sharding import PartitionSpec as P

HEAD = 128
BLOCK = 128


NEG_FILL = -1e30


def local(tokens_in, w_qkv, w_out, grad_y, block_cols, block_count):
    tok_rows = tokens_in.shape[0]
    heads_dev = w_out.shape[0] // HEAD
    local_blocks = tok_rows // BLOCK
    block_total = block_cols.shape[0]
    slot_total = block_cols.shape[1]
    score_scale = 1.0 / math.sqrt(HEAD)
    projected = jnp.einsum(
        "td,cde->cte", tokens_in, w_qkv, preferred_element_type=jnp.float32
    ).astype(jnp.bfloat16)
    heads_view = projected.reshape(3, tok_rows, heads_dev, HEAD)
    queries, keys_loc, values_loc = (heads_view[0], heads_view[1], heads_view[2])
    keys_all, values_all = (
        lax.all_gather(keys_loc, "blk", axis=0, tiled=True),
        lax.all_gather(values_loc, "blk", axis=0, tiled=True),
    )
    key_blocks = keys_all.reshape(block_total, BLOCK, heads_dev, HEAD)
    value_blocks = values_all.reshape(block_total, BLOCK, heads_dev, HEAD)
    row_ids = lax.axis_index("blk") * local_blocks + jnp.arange(local_blocks, dtype=jnp.int32)
    my_cols = jnp.take(block_cols, row_ids, axis=0)
    my_counts = jnp.take(block_count, row_ids, axis=0)
    q_blocks = queries.reshape(local_blocks, BLOCK, heads_dev, HEAD)

    def slot_operands(slot):
        col_ids = lax.dynamic_index_in_dim(my_cols, slot, 1, keepdims=False)
        live_rows = slot < my_counts
        k_part = jnp.take(key_blocks, col_ids, axis=0)
        v_part = jnp.take(value_blocks, col_ids, axis=0)
        raw_scores = (
            jnp.einsum("bqhe,bkhe->bhqk", q_blocks, k_part, preferred_element_type=jnp.float32)
            * score_scale
        )
        return (col_ids, live_rows, k_part, v_part, raw_scores)

    def stats_slot(slot, carried):
        run_max, run_sum = carried
        col_ids, live_rows, k_part, v_part, raw_scores = slot_operands(slot)
        live_wide = live_rows[:, None, None, None]
        masked = jnp.where(live_wide, raw_scores, NEG_FILL)
        new_max = jnp.maximum(run_max, jnp.max(masked, axis=3))
        exps = jnp.where(live_wide, jnp.exp(masked - new_max[..., None]), 0.0)
        run_sum = run_sum * jnp.exp(run_max - new_max) + jnp.sum(exps, axis=3)
        return (new_max, run_sum)

    start_max = jnp.full((local_blocks, heads_dev, BLOCK), NEG_FILL, jnp.float32)
    start_sum = jnp.zeros((local_blocks, heads_dev, BLOCK), jnp.float32)
    run_max, run_sum = lax.fori_loop(0, slot_total, stats_slot, (start_max, start_sum))
    log_sum = run_max + jnp.log(run_sum)

    def value_slot(slot, accumulated):
        col_ids, live_rows, k_part, v_part, raw_scores = slot_operands(slot)
        live_wide = live_rows[:, None, None, None]
        weights = jnp.where(live_wide, jnp.exp(raw_scores - log_sum[..., None]), 0.0).astype(
            jnp.bfloat16
        )
        return accumulated + jnp.einsum(
            "bhqk,bkhe->bhqe", weights, v_part, preferred_element_type=jnp.float32
        )

    start_acc = jnp.zeros((local_blocks, heads_dev, BLOCK, HEAD), jnp.float32)
    accumulated = lax.fori_loop(0, slot_total, value_slot, start_acc)
    attended_blk = accumulated.astype(jnp.bfloat16)
    attended = attended_blk.transpose(0, 2, 1, 3).reshape(tok_rows, heads_dev, HEAD)
    o_flat = attended.reshape(tok_rows, heads_dev * HEAD)
    grad_heads = (
        jnp.dot(grad_y, w_out.T, preferred_element_type=jnp.float32)
        .astype(jnp.bfloat16)
        .reshape(tok_rows, heads_dev, HEAD)
    )
    g_blocks = grad_heads.reshape(local_blocks, BLOCK, heads_dev, HEAD)
    delta_blk = jnp.einsum(
        "bhqe,bqhe->bhq", attended_blk.astype(jnp.float32), g_blocks.astype(jnp.float32)
    )
    block_range = jnp.arange(block_total, dtype=jnp.int32)

    def backward_slot(slot, carried):
        col_ids, live_rows, k_part, v_part, raw_scores = slot_operands(slot)
        live_wide = live_rows[:, None, None, None]
        prob_rows = jnp.where(live_wide, jnp.exp(raw_scores - log_sum[..., None]), 0.0)
        dprobs = jnp.einsum("bqhe,bkhe->bhqk", g_blocks, v_part, preferred_element_type=jnp.float32)
        dscores = (prob_rows * (dprobs - delta_blk[..., None])).astype(jnp.bfloat16)
        dq_acc = carried[0] + jnp.einsum(
            "bhqk,bkhe->bqhe", dscores, k_part, preferred_element_type=jnp.float32
        )
        owner = ((col_ids[:, None] == block_range[None, :]) & live_rows[:, None]).astype(
            jnp.float32
        )
        dk_term = (
            jnp.einsum("bhqk,bqhe->bkhe", dscores, q_blocks, preferred_element_type=jnp.float32)
            * score_scale
        )
        dv_term = jnp.einsum(
            "bhqk,bqhe->bkhe",
            prob_rows.astype(jnp.bfloat16),
            g_blocks,
            preferred_element_type=jnp.float32,
        )
        dk_full = carried[1] + jnp.einsum(
            "bn,bkhe->nkhe", owner, dk_term, precision=lax.Precision.HIGHEST
        )
        dv_full = carried[2] + jnp.einsum(
            "bn,bkhe->nkhe", owner, dv_term, precision=lax.Precision.HIGHEST
        )
        return (dq_acc, dk_full, dv_full)

    dq_start = jnp.zeros((local_blocks, BLOCK, heads_dev, HEAD), jnp.float32)
    full_zero = jnp.zeros((block_total, BLOCK, heads_dev, HEAD), jnp.float32)
    back_start = (dq_start, full_zero, full_zero)
    back_out = lax.fori_loop(0, slot_total, backward_slot, back_start)
    grad_q = (back_out[0] * score_scale).astype(jnp.bfloat16).reshape(tok_rows, heads_dev, HEAD)
    stacked = jnp.stack(
        [
            back_out[1].reshape(block_total * BLOCK, heads_dev, HEAD),
            back_out[2].reshape(block_total * BLOCK, heads_dev, HEAD),
        ],
        axis=1,
    )
    key_grads = lax.psum_scatter(stacked, "blk", scatter_dimension=0, tiled=True)
    grad_k = key_grads[:, 0].astype(jnp.bfloat16)
    grad_v = key_grads[:, 1].astype(jnp.bfloat16)
    grads_stack = jnp.stack([grad_q, grad_k, grad_v]).reshape(3, tok_rows, heads_dev * HEAD)
    dx_term = jnp.einsum("cte,cde->td", grads_stack, w_qkv, preferred_element_type=jnp.float32)
    grad_x = lax.psum_scatter(dx_term, "mp", scatter_dimension=1, tiled=True).astype(jnp.bfloat16)
    qkv_term = jnp.einsum("td,cte->cde", tokens_in, grads_stack, preferred_element_type=jnp.float32)
    out_term = jnp.dot(o_flat.T, grad_y, preferred_element_type=jnp.float32)
    grad_qkv, grad_out = (
        lax.psum_scatter(qkv_term, "blk", scatter_dimension=1, tiled=True),
        lax.psum_scatter(out_term, "blk", scatter_dimension=1, tiled=True),
    )
    return (grad_x, grad_qkv.astype(jnp.bfloat16), grad_out.astype(jnp.bfloat16))


def solution(mesh):
    in_specs = (P("blk", None), P(None, None, "mp"), P("mp", None), P("blk", None), P(), P())
    out_specs = (P("blk", "mp"), P(None, "blk", "mp"), P("mp", "blk"))
    return jax.shard_map(local, mesh=mesh, in_specs=in_specs, out_specs=out_specs, check_vma=False)
```

profile of v0, /device:TPU:0, one launch (start us, length us, event | category | flops | bytes accessed | tf_op | source)
XLA Modules:
  0.0 675.0 jit_solution(446797628690224736)
XLA Ops:
  7.2 5.0 fusion.40
  18.1 49.0 %all-gather.3.cloned.1.call-done = bf16[2048,4,128]{0,2,1:T(8,128)(2,1)} async-done(((bf16[256,4,128]{0,2,1:T(8,128)(2,1)}), bf16[2048,4,128]{0,2,1:T(8,128)(2,1)}) %all-gather.3.cloned.1.call-update) | async-done | bytes 2097168 | tf_op jit(solution)/shard_map/all_gather | solution.py:28
  67.1 4.3 copy.39
  71.4 6.3 while.48
  71.4 2.4 gather_fusion
  74.6 2.5 gather_fusion
  77.7 41.2 %all-gather.5.cloned.1.call-done = bf16[2048,4,128]{0,2,1:T(8,128)(2,1)} async-done(((bf16[256,4,128]{0,2,1:T(8,128)(2,1)}), bf16[2048,4,128]{0,2,1:T(8,128)(2,1)}) %all-gather.5.cloned.1.call-update) | async-done | bytes 2097168 | tf_op jit(solution)/shard_map/all_gather | solution.py:29
  119.0 4.3 copy.42
  123.3 11.2 %while.49 = (s32[]{:T(128)}, f32[2,4,128,128]{3,2,1,0:T(8,128)S(1)}, s32[2]{0:T(128)S(1)}, s32[2,2]{0,1:T(2,128)S(1)}, bf16[16,128,4,128]{3,2,1,0:T(4,128)(2,1)}...) while((s32[]{:T(128)}, ...), condition=%wide.region_5.7_spmd.clone, body=%wide.region_4.6_spmd.clone.sunk | while | flops 68158480 | bytes 3941551 | solution.py:75
  137.0 33.5 %while.50 = (s32[]{:T(128)}, f32[2,128,4,128]{1,3,2,0:T(8,128)S(1)}, f32[16,128,4,128]{3,0,2,1:T(8,128)}, f32[16,128,4,128]{3,0,2,1:T(8,128)}, s32[2,2]{0,1:T(2,...) while((s32[]{:T(128)}, ...), condition=%wide.region_7.9_spmd.clone, body=%wide.region_6.8_spmd.clone.sunk | while | flops 223872144 | bytes 93861216 | solution.py:123
  144.6 3.6 select_add_fusion.4
  148.2 3.6 select_add_fusion.5
  161.3 3.6 select_add_fusion.4
  164.9 3.6 select_add_fusion.5
  170.4 4.8 copy.50
  175.2 2.4 copy.49
  177.7 3.8 pad_maximum_fusion
  182.7 2.7 fusion.43
  185.8 143.0 %reduce-scatter.5.cloned.1.call-done = f32[256,2,4,128]{3,0,2,1:T(8,128)} async-done(((f32[2048,2,4,128]{3,0,2,1:T(8,128)}), f32[256,2,4,128]{3,0,2,1:T(8,128)}) %reduce-scatter.5.cloned.1.call-update) | async-done | bytes 1048592 | tf_op jit(solution)/shard_map/reduce_scatter | solution.py:132
  330.9 6.0 convolution_bitcast_fusion.2
  337.0 6.4 convolution_bitcast_fusion.1
  343.4 76.8 %reduce-scatter.11.cloned.1.call-done = f32[512,256]{1,0:T(8,128)} async-done(((f32[512,2048]{1,0:T(8,128)}), f32[512,256]{1,0:T(8,128)}) %reduce-scatter.11.cloned.1.call-update) | async-done | bytes 524304 | tf_op jit(solution)/shard_map/reduce_scatter | solution.py:142
  422.0 31.9 %reduce-scatter.7.cloned.1.call-done = f32[256,512]{1,0:T(8,128)} async-done(((f32[256,2048]{1,0:T(8,128)}), f32[256,512]{1,0:T(8,128)}) %reduce-scatter.7.cloned.1.call-update) | async-done | bytes 524304 | tf_op jit(solution)/shard_map/reduce_scatter | solution.py:137
  455.7 209.9 %reduce-scatter.9.cloned.1.call-done = f32[3,256,512]{1,2,0:T(8,128)} async-done(((f32[3,2048,512]{1,2,0:T(8,128)}), f32[3,256,512]{1,2,0:T(8,128)}) %reduce-scatter.9.cloned.1.call-update) | async-done | bytes 1572880 | tf_op jit(solution)/shard_map/reduce_scatter | solution.py:141
  (141 shorter events, 49.4 us)
Async XLA Ops:
  7.2 8.8 %copy-start = (bf16[512,2048]{1,0:T(8,128)(2,1)S(1)}, bf16[512,2048]{1,0:T(8,128)(2,1)}, u32[]{:S(2)}) copy-start(bf16[512,2048]{1,0:T(8,128)(2,1)} %param.16) | copy-start | bytes 6291460
  7.2 6.8 %copy-start.12 = (s32[16,2]{0,1:T(2,128)S(1)}, s32[16,2]{0,1:T(2,128)}, u32[]{:S(2)}) copy-start(s32[16,2]{0,1:T(2,128)} %param.18) | copy-start | bytes 388
  7.2 8.0 %copy-start.2 = (s32[16]{0:T(128)S(1)}, s32[16]{0:T(128)}, u32[]{:S(2)}) copy-start(s32[16]{0:T(128)} %param.19) | copy-start | bytes 196
  7.2 59.9 %all-gather.3.cloned.1.call-start = ((), (), s32[]{:S(2)}) async-start(), calls=%async_computation.4 | async-start | bytes 2359296 | tf_op jit(solution)/shard_map/all_gather | solution.py:28
  13.1 105.8 %all-gather.5.cloned.1.call-start = ((), (), s32[]{:S(2)}) async-start(), calls=%async_computation.5 | async-start | bytes 2359296 | tf_op jit(solution)/shard_map/all_gather | solution.py:29
  13.9 314.9 %reduce-scatter.5.cloned.1.call-start = ((), (), s32[]{:S(2)}) async-start(), calls=%async_computation.6 | async-start | bytes 9437184 | tf_op jit(solution)/shard_map/reduce_scatter | solution.py:132
  77.7 45.6 %copy-start.10 = (f32[2,4,128,128]{3,2,1,0:T(8,128)S(1)}, f32[2,4,128,128]{3,2,1,0:T(8,128)}, u32[]{:S(2)}) copy-start(f32[2,4,128,128]{3,2,1,0:T(8,128)} %custom-call.2) | copy-start | bytes 1572868
  134.5 0.8 copy-start.11
  142.4 2.2 copy-start.5
  144.6 3.6 copy-start.3
  148.2 3.6 copy-start.6
  151.8 2.0 copy-start.4
  159.1 2.2 copy-start.5
  161.3 3.6 copy-start.3
  164.9 3.6 copy-start.6
  168.4 2.0 copy-start.4
  170.4 4.8 copy-start.7
  181.5 1.2 copy-start.9
  181.5 238.8 %reduce-scatter.11.cloned.1.call-start = ((), (), s32[]{:S(2)}) async-start(), calls=%async_computation.9 | async-start | bytes 4718592 | tf_op jit(solution)/shard_map/reduce_scatter | solution.py:142
  185.4 268.5 %reduce-scatter.7.cloned.1.call-start = ((), (), s32[]{:S(2)}) async-start(), calls=%async_computation.7 | async-start | bytes 2621440 | tf_op jit(solution)/shard_map/reduce_scatter | solution.py:137
  330.9 6.1 copy-start.8
  337.0 328.6 %reduce-scatter.9.cloned.1.call-start = ((), (), s32[]{:S(2)}) async-start(), calls=%async_computation.8 | async-start | bytes 14155776 | tf_op jit(solution)/shard_map/reduce_scatter | solution.py:141
  343.4 324.8 %copy-start.1 = (bf16[512,2048]{1,0:T(8,128)(2,1)S(1)}, bf16[512,2048]{1,0:T(8,128)(2,1)}, u32[]{:S(2)}) copy-start(bf16[512,2048]{1,0:T(8,128)(2,1)} %param.16) | copy-start | bytes 6291460
Sparse Core Ops, SparseCore 0:
  13.3 53.7 all-gather.2
  69.7 49.2 all-gather.4
  181.6 147.1 reduce-scatter.4
  332.8 87.4 reduce-scatter.10
  422.6 31.2 reduce-scatter.6
  457.8 207.7 reduce-scatter.8
where the time goes:
time: 676 us; the launch traced here: 675 us
  waiting for transfers between devices  553 us (82%)
  local copies, waits for them, and re-layouts  52.7 us (8%)
  matrix products  40.6 us (6%)
  between operations  14.4 us (2%)
  other arithmetic  13.8 us (2%)
    reduce_scatter x1, waiting for transfers between devices, local(): lax.psum_scatter(qkv_term, 'blk', scatter_dimension=1, tiled=True)  210 us
    reduce_scatter x1, waiting for transfers between devices, local(): lax.psum_scatter(stacked, 'blk', scatter_dimension=0, tiled=True)  143 us
    reduce_scatter x1, waiting for transfers between devices, local(): lax.psum_scatter(out_term, 'blk', scatter_dimension=1, tiled=True)  76.8 us
    all_gather x1, waiting for transfers between devices, local(): lax.all_gather(keys_loc, 'blk', axis=0, tiled=True)  49 us
    all_gather x1, waiting for transfers between devices, local(): lax.all_gather(values_loc, 'blk', axis=0, tiled=True)  41.2 us
    reduce_scatter x1, waiting for transfers between devices, local(): lax.psum_scatter(dx_term, 'mp', scatter_dimension=1, tiled=True)  31.9 us
    gather x6, local copies, waits for them, and re-layouts, slot_operands(): k_part = jnp.take(key_blocks, col_ids, axis=0)  14.3 us
  transfers between devices with their start and end apart: 6, of which 6 were waited for; matrix products, arithmetic and copies ran while one was open for 5% of the time, Pallas kernels for 0%

commit v1 on v0

v1 whole, which is shorter than its diff:
```python
import functools
import math

import jax
import jax.numpy as jnp
from jax import lax
from jax.experimental import pallas as pl
from jax.experimental.pallas import tpu as pltpu
from jax.sharding import Mesh
from jax.sharding import PartitionSpec as P

HEAD = 128
BLOCK = 128
NEG_FILL = -1e30
BF16 = jnp.bfloat16
F32 = jnp.float32


def dot(a, b, dims):
    return lax.dot_general(a, b, (dims, ((), ())), preferred_element_type=F32)


def attention_kernel(cols_ref, count_ref, qkv_ref, g_ref, grads_ref, att_ref, dk_ref, dv_ref):
    row_blocks, slots = cols_ref.shape
    heads = g_ref.shape[1] // HEAD
    scale = 1.0 / math.sqrt(HEAD)
    dk_ref[...] = jnp.zeros_like(dk_ref)
    dv_ref[...] = jnp.zeros_like(dv_ref)

    def row(r, carry):
        rows = pl.ds(pl.multiple_of(r * BLOCK, BLOCK), BLOCK)
        at = [pl.ds(pl.multiple_of(cols_ref[r, s] * BLOCK, BLOCK), BLOCK) for s in range(slots)]
        live = count_ref[r]
        for h in range(heads):
            lanes = slice(h * HEAD, (h + 1) * HEAD)
            q = qkv_ref[0, rows, lanes]
            g = g_ref[rows, lanes]
            k = jnp.concatenate([qkv_ref[1, a, lanes] for a in at], axis=0)
            v = jnp.concatenate([qkv_ref[2, a, lanes] for a in at], axis=0)
            s = dot(k, q, ((1,), (1,))) * scale
            slot_of = lax.broadcasted_iota(jnp.int32, s.shape, 0) // BLOCK
            s = jnp.where(slot_of < live, s, NEG_FILL)
            e = jnp.exp(s - jnp.max(s, axis=0, keepdims=True))
            p = e * (1.0 / jnp.sum(e, axis=0, keepdims=True))
            p16 = p.astype(BF16)
            att_ref[rows, lanes] = dot(p16, v, ((0,), (0,))).astype(BF16)
            dp = dot(v, g, ((1,), (1,)))
            delta = jnp.sum(p * dp, axis=0, keepdims=True)
            ds16 = (p * (dp - delta)).astype(BF16)
            grads_ref[0, rows, lanes] = (dot(ds16, k, ((0,), (0,))) * scale).astype(BF16)
            dk = dot(ds16, q, ((1,), (0,)))
            dv = dot(p16, g, ((1,), (0,)))
            for i, a in enumerate(at):
                part = slice(i * BLOCK, (i + 1) * BLOCK)
                dk_ref[a, lanes] += dk[part]
                dv_ref[a, lanes] += dv[part]
        return carry

    lax.fori_loop(0, row_blocks, row, 0)
    grads_ref[1] = (dk_ref[...] * scale).astype(BF16)
    grads_ref[2] = dv_ref[...].astype(BF16)


def attention(cols, count, qkv, g):
    tokens, width = g.shape
    whole = pl.BlockSpec(memory_space=pltpu.VMEM)
    table = pl.BlockSpec(memory_space=pltpu.SMEM)
    return pl.pallas_call(
        attention_kernel,
        out_shape=(
            jax.ShapeDtypeStruct((3, tokens, width), BF16),
            jax.ShapeDtypeStruct((tokens, width), BF16),
        ),
        in_specs=[table, table, whole, whole],
        out_specs=(whole, whole),
        scratch_shapes=[pltpu.VMEM((tokens, width), F32), pltpu.VMEM((tokens, width), F32)],
        compiler_params=pltpu.CompilerParams(vmem_limit_bytes=48 * 2**20),
        name="attention",
    )(cols, count, qkv, g)


def local(sizes, tokens_in, w_qkv, w_out, grad_y, block_cols, block_count):
    nz, nx, ny, nc = sizes
    chunks, pieces = nz * nx, ny * nc
    tok, width = tokens_in.shape
    piece = tok // pieces
    out_cols = width // chunks
    blocks = tok // BLOCK
    chunk = lax.axis_index("z") * nx + lax.axis_index("x")
    quarter = lax.axis_index("y") * nc + lax.axis_index("c")
    quarter_block = quarter * blocks // pieces

    def swap(a, axis, k):
        n = math.prod(mesh_size[i] for i in axis)
        return lax.ppermute(a, axis, [(i, i ^ k) for i in range(n)])

    mesh_size = dict(z=nz, x=nx, y=ny, c=nc)

    def my_piece(a, k):
        return lax.dynamic_slice_in_dim(a, (quarter ^ k) * piece, piece, 0)

    def spread(parts):
        by_y = [[p] + [swap(p, "y", k) for k in range(1, ny)] for p in parts]
        whole = []
        for ys in by_y:
            mine = jnp.concatenate(ys, axis=0)
            cs = [mine] + [swap(mine, "c", j) for j in range(1, nc)]
            whole.append(
                jnp.concatenate(
                    [cs[j][k * piece : (k + 1) * piece] for k in range(ny) for j in range(nc)], axis=0
                )
            )
        return whole

    own = my_piece(tokens_in, 0)
    along_z = [own] + [swap(own, "z", k) for k in range(1, nz)]
    along_x = [p if j == 0 else swap(p, "x", j) for p in along_z for j in range(nx)]
    all_tokens = [tokens_in] + spread(along_x[1:])

    g_own = dot(grad_y, w_out, ((1,), (1,))).astype(BF16)
    g_sent = jnp.concatenate([my_piece(g_own, k) for k in range(pieces)], axis=0)
    g_z = [g_sent] + [swap(g_sent, "z", k) for k in range(1, nz)]
    g_x = [p if j == 0 else swap(p, "x", j) for p in g_z for j in range(nx)]
    g_all = jnp.concatenate([g_own] + g_x[1:], axis=0)

    y_mine = my_piece(grad_y, 0)

    def columns(a, k):
        return lax.dynamic_slice_in_dim(a, (chunk ^ k) * out_cols, out_cols, 1)

    y_parts = [swap(columns(y_mine, k), ("z", "x"), k) for k in range(1, chunks)]
    y_rows = jnp.stack(y_parts)
    y_by_y = jnp.stack([y_rows] + [swap(y_rows, "y", k) for k in range(1, ny)], axis=1)
    y_by_c = jnp.stack([y_by_y] + [swap(y_by_y, "c", j) for j in range(1, nc)], axis=2)
    y_all = jnp.concatenate([columns(grad_y, 0), y_by_c.reshape((chunks - 1) * tok, out_cols)], axis=0)

    qkv = jnp.concatenate(
        [
            jnp.einsum("td,cde->cte", t, w_qkv, preferred_element_type=F32).astype(BF16)
            for t in all_tokens
        ],
        axis=1,
    )

    place = jnp.arange(chunks * blocks, dtype=jnp.int32)

    def flip(held_chunk):
        return jnp.where(held_chunk == 0, 0, quarter_block)

    held = place // blocks
    block_at = (held ^ chunk) * blocks + ((place % blocks) ^ flip(held))
    pick = block_at[:, None] == place[None, :]
    cols = jnp.sum(jnp.where(pick[:, :, None], block_cols[None], 0), axis=1)
    count = jnp.sum(jnp.where(pick, block_count[None], 0), axis=1)
    cols_held = (cols // blocks) ^ chunk
    cols = cols_held * blocks + ((cols % blocks) ^ flip(cols_held))

    grads, att = attention(cols, count, qkv, g_all)

    dx = jnp.einsum("cte,cde->td", grads[:, :tok], w_qkv, preferred_element_type=F32)
    dx = dx.reshape(tok, ny, nc, width // pieces)
    y, c = lax.axis_index("y"), lax.axis_index("c")

    def at_c(k):
        return lax.dynamic_index_in_dim(dx, c ^ k, 2, keepdims=False)

    half = at_c(0)
    for k in range(1, nc):
        half = half + swap(at_c(k).astype(BF16), "c", k).astype(F32)

    def at_y(k):
        return lax.dynamic_index_in_dim(half, y ^ k, 1, keepdims=False)

    grad_x = at_y(0)
    for k in range(1, ny):
        grad_x = grad_x + swap(at_y(k).astype(BF16), "y", k).astype(F32)

    t_cols = jnp.concatenate([columns(t, 0) for t in all_tokens], axis=0)
    grad_qkv = jnp.einsum("td,cte->cde", t_cols, grads, preferred_element_type=F32)
    grad_out = dot(att, y_all, ((0,), (0,)))
    return (grad_x.astype(BF16), grad_qkv.astype(BF16), grad_out.astype(BF16))


def solution(mesh):
    chunks, pieces = mesh.shape["blk"], mesh.shape["mp"]
    sizes = (chunks // 2, 2, pieces // 2, 2)
    fine = Mesh(mesh.devices.reshape(sizes), ("z", "x", "y", "c"))
    blk, mp = ("z", "x"), ("y", "c")
    in_specs = (P(blk, None), P(None, None, mp), P(mp, None), P(blk, None), P(), P())
    out_specs = (P(blk, mp), P(None, blk, mp), P(mp, blk))
    return jax.shard_map(
        functools.partial(local, sizes), mesh=fine, in_specs=in_specs, out_specs=out_specs, check_vma=False
    )
```

time: 676 us -> 222 us (0.33)
  waiting for transfers between devices: 553 us -> 84 us
  starting transfers between devices: 0.24 us -> 40.3 us
  Pallas kernels: 0 us -> 33.3 us
  local copies, waits for them, and re-layouts: 52.7 us -> 21 us
  between operations: 14.4 us -> 1.56 us
  matrix products: 40.6 us -> 33.8 us
    reduce_scatter x4 -> x0, waiting for transfers between devices: 462 us -> none  [the longest x1 210 us: local(): lax.psum_scatter(qkv_term, 'blk', scatter_dimension=1, tiled=True)]
    all_gather x2 -> x0, waiting for transfers between devices: 90.2 us -> none  [the longest x1 49 us: local(): lax.all_gather(keys_loc, 'blk', axis=0, tiled=True)]
    ppermute x0 -> x39, waiting for transfers between devices: none -> 84 us  [swap(): return lax.ppermute(a, axis, [(i, i ^ k) for i in range(n)])]
    ppermute x0 -> x39, starting transfers between devices: none -> 40.3 us  [swap(): return lax.ppermute(a, axis, [(i, i ^ k) for i in range(n)])]
    pallas_call x0 -> x1, Pallas kernels: none -> 33.3 us  [attention(): pl.pallas_call(attention_kernel, out_shape=(jax.ShapeDtypeStruct((3, toke...]
    gather x12 -> x0, local copies, waits for them, and re-layouts: 25.1 us -> none  [the longest x6 14.3 us: slot_operands(): k_part = jnp.take(key_blocks, col_ids, axis=0)]
    while x20 -> x0, local copies, waits for them, and re-layouts: 12.8 us -> none  [the longest x2 7.2 us: local(): back_out = lax.fori_loop(0, slot_total, backward_slot, back_start)]
    unnamed x26 -> x93, local copies, waits for them, and re-layouts: 3.59 us -> 12.5 us
  transfers between devices with their start and end apart: 6 -> 39, of which waited for: 6 -> 17; matrix products, arithmetic and copies ran while one was open for 5% -> 15% of each run, Pallas kernels for 0% -> 0%
where the time goes in v1:
time: 222 us; the launch traced here: 221 us
  waiting for transfers between devices  84 us (38%)
  starting transfers between devices  40.3 us (18%)
  matrix products  33.8 us (15%)
  Pallas kernels  33.3 us (15%)
  local copies, waits for them, and re-layouts  21 us (9%)
  other arithmetic  7.33 us (3%)
    ppermute x39, waiting for transfers between devices, swap(): return lax.ppermute(a, axis, [(i, i ^ k) for i in range(n)])  84 us
    ppermute x39, starting transfers between devices, swap(): return lax.ppermute(a, axis, [(i, i ^ k) for i in range(n)])  40.3 us
    pallas_call x1, Pallas kernels, attention(): pl.pallas_call(attention_kernel, out_shape=(jax.ShapeDtypeStruct((3, toke...  33.3 us
    dot_general x8, matrix products, local(): jnp.einsum('td,cde->cte', t, w_qkv, preferred_element_type=F32).astype(BF16)  18.9 us
    unnamed x93, local copies, waits for them, and re-layouts  12.5 us
    dot_general x1, matrix products, local(): jnp.einsum('cte,cde->td', grads[:, :tok], w_qkv, preferred_element_type=F32)  6.16 us
    dot_general x1, matrix products, local(): jnp.einsum('td,cte->cde', t_cols, grads, preferred_element_type=F32)  4.62 us
  transfers between devices with their start and end apart: 39, of which 17 were waited for; matrix products, arithmetic and copies ran while one was open for 15% of the time, Pallas kernels for 0%

profile of v1, /device:TPU:0, one launch (start us, length us, event | category | flops | bytes accessed | tf_op | source)
XLA Modules:
  0.0 221.4 jit_solution(14517586043934640090)
XLA Ops:
  1.8 3.1 %collective-permute-start.3 = (bf16[64,2048]{1,0:T(8,128)(2,1)S(1)}, bf16[64,2048]{1,0:T(8,128)(2,1)S(1)}, u32[]{:S(2)}, u32[]{:S(2)}) collective-permute-start(bf16[64,2048]{1,0:T(8,128)(2,1)S(1)} %constant_dynamic-slice_fusion.7), channel_id=1, source_target_pairs={{0,8},{8,0},{16,24},{24,16},{1,9},{9,1},{17,25},{25,17},{2,10},{10... | collective-permute-start | bytes 786440 | tf_op jit(solution)/shard_map/ppermute | solution.py:95
  6.4 2.7 %constant_dynamic-update-slice_fusion.7 = (bf16[2048,512]{1,0:T(8,128)(2,1)}, bf16[256,512]{1,0:T(8,128)(2,1)S(1)}) fusion(bf16[256,2048]{1,0:T(8,128)(2,1)} %param.9, bf16[512,2048]{1,0:T(8,128)(2,1)S(1)} %copy-done), kind=kOutput, calls=%fused_computation.81 | convolution fusion | flops 537001984 | bytes 3670016 | tf_op jit(solution)/shard_map/dot_general | solution.py:20
  14.7 5.9 %fusion.16 = bf16[3,2048,512]{2,1,0:T(8,128)(2,1)} fusion(bf16[3,2048,512]{2,1,0:T(8,128)(2,1)} %param.7, bf16[256,2048]{1,0:T(8,128)(2,1)} %param.6), kind=kOutput, calls=%fused_computation.26 | convolution fusion | flops 1611005952 | bytes 8126464 | tf_op jit(solution)/shard_map/td,cde->cte/dot_general | solution.py:139
  27.7 3.7 %collective-permute-done.32 = bf16[64,256]{1,0:T(8,128)(2,1)S(1)} collective-permute-done((bf16[64,256]{1,0:T(8,128)(2,1)S(1)}, bf16[64,256]{1,0:T(8,128)(2,1)S(1)}, u32[]{:S(2)}, u32[]{:S(2)}) %collective-permute-start.32) | collective-permute-done | bytes 32800 | tf_op jit(solution)/shard_map/ppermute | solution.py:95
  33.6 2.8 %collective-permute-done.33 = bf16[64,256]{1,0:T(8,128)(2,1)S(1)} collective-permute-done((bf16[64,256]{1,0:T(8,128)(2,1)S(1)}, bf16[64,256]{1,0:T(8,128)(2,1)S(1)}, u32[]{:S(2)}, u32[]{:S(2)}) %collective-permute-start.33) | collective-permute-done | bytes 32800 | tf_op jit(solution)/shard_map/ppermute | solution.py:95
  38.8 3.4 %collective-permute-done.34 = bf16[64,256]{1,0:T(8,128)(2,1)S(1)} collective-permute-done((bf16[64,256]{1,0:T(8,128)(2,1)S(1)}, bf16[64,256]{1,0:T(8,128)(2,1)S(1)}, u32[]{:S(2)}, u32[]{:S(2)}) %collective-permute-start.34) | collective-permute-done | bytes 32800 | tf_op jit(solution)/shard_map/ppermute | solution.py:95
  42.1 3.4 %collective-permute-start.35 = (bf16[64,256]{1,0:T(8,128)(2,1)S(1)}, bf16[64,256]{1,0:T(8,128)(2,1)S(1)}, u32[]{:S(2)}, u32[]{:S(2)}) collective-permute-start(bf16[64,256]{1,0:T(8,128)(2,1)S(1)} %get-tuple-element.22), channel_id=1, source_target_pairs={{0,24},{4,28},{8,16},{12,20},{16,8},{20,12},{24,0},{28,4},{1,25},{... | collective-permute-start | bytes 98312 | tf_op jit(solution)/shard_map/ppermute | solution.py:95
  47.9 4.3 %collective-permute-start.36 = (bf16[64,256]{1,0:T(8,128)(2,1)S(1)}, bf16[64,256]{1,0:T(8,128)(2,1)S(1)}, u32[]{:S(2)}, u32[]{:S(2)}) collective-permute-start(bf16[64,256]{1,0:T(8,128)(2,1)S(1)} %get-tuple-element.16), channel_id=1, source_target_pairs={{0,28},{4,24},{8,20},{12,16},{16,12},{20,8},{24,4},{28,0},{1,29},{... | collective-permute-start | bytes 98312 | tf_op jit(solution)/shard_map/ppermute | solution.py:95
  52.2 2.7 %collective-permute-done.36 = bf16[64,256]{1,0:T(8,128)(2,1)S(1)} collective-permute-done((bf16[64,256]{1,0:T(8,128)(2,1)S(1)}, bf16[64,256]{1,0:T(8,128)(2,1)S(1)}, u32[]{:S(2)}, u32[]{:S(2)}) %collective-permute-start.36) | collective-permute-done | bytes 32800 | tf_op jit(solution)/shard_map/ppermute | solution.py:95
  58.6 4.6 %collective-permute-done.37 = bf16[7,64,256]{2,1,0:T(8,128)(2,1)} collective-permute-done((bf16[7,64,256]{2,1,0:T(8,128)(2,1)S(1)}, bf16[7,64,256]{2,1,0:T(8,128)(2,1)}, u32[]{:S(2)}, u32[]{:S(2)}) %collective-permute-start.37) | collective-permute-done | bytes 229408 | tf_op jit(solution)/shard_map/ppermute | solution.py:95
  70.0 10.4 %collective-permute-done.9 = bf16[64,2048]{1,0:T(8,128)(2,1)S(1)} collective-permute-done((bf16[64,2048]{1,0:T(8,128)(2,1)S(1)}, bf16[64,2048]{1,0:T(8,128)(2,1)S(1)}, u32[]{:S(2)}, u32[]{:S(2)}) %collective-permute-start.9) | collective-permute-done | bytes 262176 | tf_op jit(solution)/shard_map/ppermute | solution.py:95
  82.7 6.2 %collective-permute-done.10 = bf16[64,2048]{1,0:T(8,128)(2,1)S(1)} collective-permute-done((bf16[64,2048]{1,0:T(8,128)(2,1)S(1)}, bf16[64,2048]{1,0:T(8,128)(2,1)S(1)}, u32[]{:S(2)}, u32[]{:S(2)}) %collective-permute-start.10) | collective-permute-done | bytes 262176 | tf_op jit(solution)/shard_map/ppermute | solution.py:95
  89.0 8.0 %collective-permute-done.24 = bf16[256,512]{1,0:T(8,128)(2,1)S(1)} collective-permute-done((bf16[256,512]{1,0:T(8,128)(2,1)}, bf16[256,512]{1,0:T(8,128)(2,1)S(1)}, u32[]{:S(2)}, u32[]{:S(2)}) %collective-permute-start.24) | collective-permute-done | bytes 262176 | tf_op jit(solution)/shard_map/ppermute | solution.py:95
  101.2 5.0 %collective-permute-done.6 = bf16[64,2048]{1,0:T(8,128)(2,1)S(1)} collective-permute-done((bf16[64,2048]{1,0:T(8,128)(2,1)S(1)}, bf16[64,2048]{1,0:T(8,128)(2,1)S(1)}, u32[]{:S(2)}, u32[]{:S(2)}) %collective-permute-start.6) | collective-permute-done | bytes 262176 | tf_op jit(solution)/shard_map/ppermute | solution.py:95
  106.7 5.1 %collective-permute-done.25 = bf16[256,512]{1,0:T(8,128)(2,1)S(1)} collective-permute-done((bf16[256,512]{1,0:T(8,128)(2,1)S(1)}, bf16[256,512]{1,0:T(8,128)(2,1)S(1)}, u32[]{:S(2)}, u32[]{:S(2)}) %collective-permute-start.25) | collective-permute-done | bytes 262176 | tf_op jit(solution)/shard_map/ppermute | solution.py:95
  112.6 9.0 %collective-permute-done.27 = bf16[256,512]{1,0:T(8,128)(2,1)S(1)} collective-permute-done((bf16[256,512]{1,0:T(8,128)(2,1)S(1)}, bf16[256,512]{1,0:T(8,128)(2,1)S(1)}, u32[]{:S(2)}, u32[]{:S(2)}) %collective-permute-start.27) | collective-permute-done | bytes 262176 | tf_op jit(solution)/shard_map/ppermute | solution.py:95
  125.4 6.0 %collective-permute-done.19 = bf16[64,2048]{1,0:T(8,128)(2,1)S(1)} collective-permute-done((bf16[64,2048]{1,0:T(8,128)(2,1)S(1)}, bf16[64,2048]{1,0:T(8,128)(2,1)S(1)}, u32[]{:S(2)}, u32[]{:S(2)}) %collective-permute-start.19) | collective-permute-done | bytes 262176 | tf_op jit(solution)/shard_map/ppermute | solution.py:95
  131.4 4.7 %collective-permute-done.13 = bf16[64,2048]{1,0:T(8,128)(2,1)S(1)} collective-permute-done((bf16[64,2048]{1,0:T(8,128)(2,1)S(1)}, bf16[64,2048]{1,0:T(8,128)(2,1)S(1)}, u32[]{:S(2)}, u32[]{:S(2)}) %collective-permute-start.13) | collective-permute-done | bytes 262176 | tf_op jit(solution)/shard_map/ppermute | solution.py:95
  153.2 2.7 %copy-done.5 = bf16[3,2048,512]{2,1,0:T(8,128)(2,1)} copy-done((bf16[3,2048,512]{2,1,0:T(8,128)(2,1)}, bf16[3,2048,512]{2,1,0:T(8,128)(2,1)S(1)}, u32[]{:S(2)}) %copy-start.5) | copy-done | bytes 6291480
  155.9 33.3 %attention.1 = (bf16[3,2048,512]{2,1,0:T(8,128)(2,1)}, bf16[2048,512]{1,0:T(8,128)(2,1)S(1)}) custom-call(s32[16,2]{1,0:T(8,128)S(1)} %fusion.35.cols_ref, s32[16]{0:T(128)S(1)} %select_reduce_fusion.1.count_ref, bf16[3,2048,512]{2,1,0:T(8,128)(2,1)} %copy-done.5, bf16[2048,512]{1,0:T(8,128)(2,1)S(1)} %constant_dynamic-update-slice_fusion.g_ref), custom_call_target="tpu_custom_call" | custom-call | tf_op jit(solution)/shard_map/attention/pallas_call | solution.py:68
  190.6 6.2 %convolution_bitcast_fusion = f32[256,2048]{1,0:T(8,128)} fusion(bf16[3,2048,512]{2,1,0:T(8,128)(2,1)} %param.7, bf16[3,2048,512]{2,1,0:T(8,128)(2,1)} %get-tuple-element.5), kind=kOutput, calls=%fused_computation | convolution fusion | flops 1610612736 | bytes 9175040 | tf_op jit(solution)/shard_map/cte,cde->td/dot_general | solution.py:160
  196.8 3.0 %reshape.62 = f32[256,2,2,512]{3,2,1,0:T(2,128)S(1)} reshape(f32[256,2048]{1,0:T(8,128)} %convolution_bitcast_fusion) | data formatting | bytes 4194304 | tf_op jit(solution)/shard_map/reshape | solution.py:161
  203.8 4.6 %fusion.14 = bf16[3,256,512]{1,2,0:T(8,128)(2,1)S(1)} fusion(bf16[3,2048,512]{2,1,0:T(8,128)(2,1)} %get-tuple-element.5, bf16[2048,256]{1,0:T(8,128)(2,1)S(1)} %dynamic-slice_dynamic-update-slice_fusion), kind=kOutput, calls=%fused_computation.24 | convolution fusion | flops 1611005952 | bytes 8126464 | tf_op jit(solution)/shard_map/td,cte->cde/dot_general | solution.py:179
  213.9 6.7 %collective-permute-done.29 = bf16[256,512]{1,0:T(8,128)(2,1)S(1)} collective-permute-done((bf16[256,512]{1,0:T(8,128)(2,1)S(1)}, bf16[256,512]{1,0:T(8,128)(2,1)S(1)}, u32[]{:S(2)}, u32[]{:S(2)}) %collective-permute-start.29) | collective-permute-done | bytes 262176 | tf_op jit(solution)/shard_map/ppermute | solution.py:95
  (205 shorter events, 72.1 us)
Async XLA Ops:
  1.8 65.3 %collective-permute-start.3 = (bf16[64,2048]{1,0:T(8,128)(2,1)S(1)}, bf16[64,2048]{1,0:T(8,128)(2,1)S(1)}, u32[]{:S(2)}, u32[]{:S(2)}) collective-permute-start(bf16[64,2048]{1,0:T(8,128)(2,1)S(1)} %constant_dynamic-slice_fusion.7), channel_id=1, source_target_pairs={{0,8},{8,0},{16,24},{24,16},{1,9},{9,1},{17,25},{25,17},{2,10},{10... | collective-permute-start | bytes 786440 | tf_op jit(solution)/shard_map/ppermute | solution.py:95
  4.9 51.3 %collective-permute-start = (bf16[64,2048]{1,0:T(8,128)(2,1)S(1)}, bf16[64,2048]{1,0:T(8,128)(2,1)S(1)}, u32[]{:S(2)}, u32[]{:S(2)}) collective-permute-start(bf16[64,2048]{1,0:T(8,128)(2,1)S(1)} %constant_dynamic-slice_fusion.7), channel_id=1, source_target_pairs={{0,4},{4,0},{1,5},{5,1},{2,6},{6,2},{3,7},{7,3},{8,12},{12,8},{9,1... | collective-permute-start | bytes 786440 | tf_op jit(solution)/shard_map/ppermute | solution.py:95
  9.8 58.5 %collective-permute-start.22 = (bf16[256,512]{1,0:T(8,128)(2,1)}, bf16[256,512]{1,0:T(8,128)(2,1)}, u32[]{:S(2)}, u32[]{:S(2)}) collective-permute-start(bf16[256,512]{1,0:T(8,128)(2,1)} %pad_maximum_fusion.16), channel_id=1, source_target_pairs={{0,8},{8,0},{16,24},{24,16},{1,9},{9,1},{17,25},{25,17},{2,10},{10... | collective-permute-start | bytes 786440 | tf_op jit(solution)/shard_map/ppermute | solution.py:95
  10.2 46.3 %collective-permute-start.21 = (bf16[256,512]{1,0:T(8,128)(2,1)}, bf16[256,512]{1,0:T(8,128)(2,1)}, u32[]{:S(2)}, u32[]{:S(2)}) collective-permute-start(bf16[256,512]{1,0:T(8,128)(2,1)} %pad_maximum_fusion.16), channel_id=1, source_target_pairs={{0,4},{4,0},{1,5},{5,1},{2,6},{6,2},{3,7},{7,3},{8,12},{12,8},{9,1... | collective-permute-start | bytes 786440 | tf_op jit(solution)/shard_map/ppermute | solution.py:95
  11.5 10.7 %collective-permute-start.30 = (bf16[64,256]{1,0:T(8,128)(2,1)S(1)}, bf16[64,256]{1,0:T(8,128)(2,1)S(1)}, u32[]{:S(2)}, u32[]{:S(2)}) collective-permute-start(bf16[64,256]{1,0:T(8,128)(2,1)S(1)} %get-tuple-element.21), channel_id=1, source_target_pairs={{0,4},{4,0},{8,12},{12,8},{16,20},{20,16},{24,28},{28,24},{1,5},{5... | collective-permute-start | bytes 98312 | tf_op jit(solution)/shard_map/ppermute | solution.py:95
  56.2 24.3 %collective-permute-start.9 = (bf16[64,2048]{1,0:T(8,128)(2,1)S(1)}, bf16[64,2048]{1,0:T(8,128)(2,1)S(1)}, u32[]{:S(2)}, u32[]{:S(2)}) collective-permute-start(bf16[64,2048]{1,0:T(8,128)(2,1)S(1)} %constant_dynamic-slice_fusion.7), channel_id=1, source_target_pairs={{0,16},{8,24},{16,0},{24,8},{1,17},{9,25},{17,1},{25,9},{2,18},{10... | collective-permute-start | bytes 786440 | tf_op jit(solution)/shard_map/ppermute | solution.py:95
  56.6 23.9 %collective-permute-start.1 = (bf16[64,2048]{1,0:T(8,128)(2,1)S(1)}, bf16[64,2048]{1,0:T(8,128)(2,1)S(1)}, u32[]{:S(2)}, u32[]{:S(2)}) collective-permute-start(bf16[64,2048]{1,0:T(8,128)(2,1)S(1)} %collective-permute-done), channel_id=1, source_target_pairs={{0,2},{2,0},{1,3},{3,1},{4,6},{6,4},{5,7},{7,5},{8,10},{10,8},{9,1... | collective-permute-start | bytes 786440 | tf_op jit(solution)/shard_map/ppermute | solution.py:95
  63.2 18.3 %collective-permute-start.15 = (bf16[64,2048]{1,0:T(8,128)(2,1)S(1)}, bf16[64,2048]{1,0:T(8,128)(2,1)S(1)}, u32[]{:S(2)}, u32[]{:S(2)}) collective-permute-start(bf16[64,2048]{1,0:T(8,128)(2,1)S(1)} %constant_dynamic-slice_fusion.7), channel_id=1, source_target_pairs={{0,24},{8,16},{16,8},{24,0},{1,25},{9,17},{17,9},{25,1},{2,26},{10... | collective-permute-start | bytes 786440 | tf_op jit(solution)/shard_map/ppermute | solution.py:95
  67.1 32.0 %collective-permute-start.26 = (bf16[256,512]{1,0:T(8,128)(2,1)}, bf16[256,512]{1,0:T(8,128)(2,1)S(1)}, u32[]{:S(2)}, u32[]{:S(2)}) collective-permute-start(bf16[256,512]{1,0:T(8,128)(2,1)} %pad_maximum_fusion.16), channel_id=1, source_target_pairs={{0,24},{8,16},{16,8},{24,0},{1,25},{9,17},{17,9},{25,1},{2,26},{10... | collective-permute-start | bytes 786440 | tf_op jit(solution)/shard_map/ppermute | solution.py:95
  68.3 13.3 %collective-permute-start.4 = (bf16[64,2048]{1,0:T(8,128)(2,1)S(1)}, bf16[64,2048]{1,0:T(8,128)(2,1)S(1)}, u32[]{:S(2)}, u32[]{:S(2)}) collective-permute-start(bf16[64,2048]{1,0:T(8,128)(2,1)S(1)} %collective-permute-done.3), channel_id=1, source_target_pairs={{0,2},{2,0},{1,3},{3,1},{4,6},{6,4},{5,7},{7,5},{8,10},{10,8},{9,1... | collective-permute-start | bytes 786440 | tf_op jit(solution)/shard_map/ppermute | solution.py:95
  80.4 16.6 %collective-permute-start.24 = (bf16[256,512]{1,0:T(8,128)(2,1)}, bf16[256,512]{1,0:T(8,128)(2,1)S(1)}, u32[]{:S(2)}, u32[]{:S(2)}) collective-permute-start(bf16[256,512]{1,0:T(8,128)(2,1)} %pad_maximum_fusion.16), channel_id=1, source_target_pairs={{0,16},{8,24},{16,0},{24,8},{1,17},{9,25},{17,1},{25,9},{2,18},{10... | collective-permute-start | bytes 786440 | tf_op jit(solution)/shard_map/ppermute | solution.py:95
  81.5 40.7 %collective-permute-start.38 = (bf16[7,2,64,256]{3,2,1,0:T(8,128)(2,1)S(1)}, bf16[7,2,64,256]{3,2,1,0:T(8,128)(2,1)S(1)}, u32[]{:S(2)}, u32[]{:S(2)}) collective-permute-start(bf16[7,2,64,256]{3,2,1,0:T(8,128)(2,1)S(1)} %get-tuple-element.38), channel_id=1, source_target_pairs={{0,1},{1,0},{2,3},{3,2},{4,5},{5,4},{6,7},{7,6},{8,9},{9,8},{10,11... | collective-permute-start | bytes 1376264 | tf_op jit(solution)/shard_map/ppermute | solution.py:95
  81.6 15.9 %collective-permute-start.16 = (bf16[64,2048]{1,0:T(8,128)(2,1)S(1)}, bf16[64,2048]{1,0:T(8,128)(2,1)S(1)}, u32[]{:S(2)}, u32[]{:S(2)}) collective-permute-start(bf16[64,2048]{1,0:T(8,128)(2,1)S(1)} %collective-permute-done.15), channel_id=1, source_target_pairs={{0,2},{2,0},{1,3},{3,1},{4,6},{6,4},{5,7},{7,5},{8,10},{10,8},{9,1... | collective-permute-start | bytes 786440 | tf_op jit(solution)/shard_map/ppermute | solution.py:95
  89.0 10.7 %collective-permute-start.23 = (bf16[256,512]{1,0:T(8,128)(2,1)}, bf16[256,512]{1,0:T(8,128)(2,1)S(1)}, u32[]{:S(2)}, u32[]{:S(2)}) collective-permute-start(bf16[256,512]{1,0:T(8,128)(2,1)} %collective-permute-done.22), channel_id=1, source_target_pairs={{0,4},{4,0},{1,5},{5,1},{2,6},{6,2},{3,7},{7,3},{8,12},{12,8},{9,1... | collective-permute-start | bytes 786440 | tf_op jit(solution)/shard_map/ppermute | solution.py:95
  97.0 9.2 %collective-permute-start.6 = (bf16[64,2048]{1,0:T(8,128)(2,1)S(1)}, bf16[64,2048]{1,0:T(8,128)(2,1)S(1)}, u32[]{:S(2)}, u32[]{:S(2)}) collective-permute-start(bf16[64,2048]{1,0:T(8,128)(2,1)S(1)} %collective-permute-done.3), channel_id=1, source_target_pairs={{0,4},{4,0},{1,5},{5,1},{2,6},{6,2},{3,7},{7,3},{8,12},{12,8},{9,1... | collective-permute-start | bytes 786440 | tf_op jit(solution)/shard_map/ppermute | solution.py:95
  97.5 14.4 %collective-permute-start.25 = (bf16[256,512]{1,0:T(8,128)(2,1)S(1)}, bf16[256,512]{1,0:T(8,128)(2,1)S(1)}, u32[]{:S(2)}, u32[]{:S(2)}) collective-permute-start(bf16[256,512]{1,0:T(8,128)(2,1)S(1)} %collective-permute-done.24), channel_id=1, source_target_pairs={{0,4},{4,0},{1,5},{5,1},{2,6},{6,2},{3,7},{7,3},{8,12},{12,8},{9,1... | collective-permute-start | bytes 786440 | tf_op jit(solution)/shard_map/ppermute | solution.py:95
  99.1 22.5 %collective-permute-start.18 = (bf16[64,2048]{1,0:T(8,128)(2,1)S(1)}, bf16[64,2048]{1,0:T(8,128)(2,1)S(1)}, u32[]{:S(2)}, u32[]{:S(2)}) collective-permute-start(bf16[64,2048]{1,0:T(8,128)(2,1)S(1)} %collective-permute-done.15), channel_id=1, source_target_pairs={{0,4},{4,0},{1,5},{5,1},{2,6},{6,2},{3,7},{7,3},{8,12},{12,8},{9,1... | collective-permute-start | bytes 786440 | tf_op jit(solution)/shard_map/ppermute | solution.py:95
  99.7 21.9 %collective-permute-start.27 = (bf16[256,512]{1,0:T(8,128)(2,1)S(1)}, bf16[256,512]{1,0:T(8,128)(2,1)S(1)}, u32[]{:S(2)}, u32[]{:S(2)}) collective-permute-start(bf16[256,512]{1,0:T(8,128)(2,1)S(1)} %collective-permute-done.26), channel_id=1, source_target_pairs={{0,4},{4,0},{1,5},{5,1},{2,6},{6,2},{3,7},{7,3},{8,12},{12,8},{9,1... | collective-permute-start | bytes 786440 | tf_op jit(solution)/shard_map/ppermute | solution.py:95
  106.2 18.2 %collective-permute-start.12 = (bf16[64,2048]{1,0:T(8,128)(2,1)S(1)}, bf16[64,2048]{1,0:T(8,128)(2,1)S(1)}, u32[]{:S(2)}, u32[]{:S(2)}) collective-permute-start(bf16[64,2048]{1,0:T(8,128)(2,1)S(1)} %collective-permute-done.9), channel_id=1, source_target_pairs={{0,4},{4,0},{1,5},{5,1},{2,6},{6,2},{3,7},{7,3},{8,12},{12,8},{9,1... | collective-permute-start | bytes 786440 | tf_op jit(solution)/shard_map/ppermute | solution.py:95
  111.9 12.6 %collective-permute-start.7 = (bf16[64,2048]{1,0:T(8,128)(2,1)S(1)}, bf16[64,2048]{1,0:T(8,128)(2,1)S(1)}, u32[]{:S(2)}, u32[]{:S(2)}) collective-permute-start(bf16[64,2048]{1,0:T(8,128)(2,1)S(1)} %collective-permute-done.6), channel_id=1, source_target_pairs={{0,2},{2,0},{1,3},{3,1},{4,6},{6,4},{5,7},{7,5},{8,10},{10,8},{9,1... | collective-permute-start | bytes 786440 | tf_op jit(solution)/shard_map/ppermute | solution.py:95
  121.6 14.6 %collective-permute-start.17 = (bf16[128,2048]{1,0:T(8,128)(2,1)S(1)}, bf16[128,2048]{1,0:T(8,128)(2,1)S(1)}, u32[]{:S(2)}, u32[]{:S(2)}) collective-permute-start(bf16[128,2048]{1,0:T(8,128)(2,1)S(1)} %pad_maximum_fusion.13), channel_id=1, source_target_pairs={{0,1},{1,0},{2,3},{3,2},{4,5},{5,4},{6,7},{7,6},{8,9},{9,8},{10,11... | collective-permute-start | bytes 1572872 | tf_op jit(solution)/shard_map/ppermute | solution.py:95
  121.6 15.2 %collective-permute-start.11 = (bf16[128,2048]{1,0:T(8,128)(2,1)S(1)}, bf16[128,2048]{1,0:T(8,128)(2,1)S(1)}, u32[]{:S(2)}, u32[]{:S(2)}) collective-permute-start(bf16[128,2048]{1,0:T(8,128)(2,1)S(1)} %pad_maximum_fusion.11), channel_id=1, source_target_pairs={{0,1},{1,0},{2,3},{3,2},{4,5},{5,4},{6,7},{7,6},{8,9},{9,8},{10,11... | collective-permute-start | bytes 1572872 | tf_op jit(solution)/shard_map/ppermute | solution.py:95
  124.4 12.5 %collective-permute-start.5 = (bf16[128,2048]{1,0:T(8,128)(2,1)S(1)}, bf16[128,2048]{1,0:T(8,128)(2,1)S(1)}, u32[]{:S(2)}, u32[]{:S(2)}) collective-permute-start(bf16[128,2048]{1,0:T(8,128)(2,1)S(1)} %pad_maximum_fusion.9), channel_id=1, source_target_pairs={{0,1},{1,0},{2,3},{3,2},{4,5},{5,4},{6,7},{7,6},{8,9},{9,8},{10,11... | collective-permute-start | bytes 1572872 | tf_op jit(solution)/shard_map/ppermute | solution.py:95
  124.4 11.7 %collective-permute-start.13 = (bf16[64,2048]{1,0:T(8,128)(2,1)S(1)}, bf16[64,2048]{1,0:T(8,128)(2,1)S(1)}, u32[]{:S(2)}, u32[]{:S(2)}) collective-permute-start(bf16[64,2048]{1,0:T(8,128)(2,1)S(1)} %collective-permute-done.12), channel_id=1, source_target_pairs={{0,2},{2,0},{1,3},{3,1},{4,6},{6,4},{5,7},{7,5},{8,10},{10,8},{9,1... | collective-permute-start | bytes 786440 | tf_op jit(solution)/shard_map/ppermute | solution.py:95
  (51 other events, 516.7 us)

commit v2 on v1

v2 whole, which is shorter than its diff:
```python
import functools
import math

import jax
import jax.numpy as jnp
from jax import lax
from jax.experimental import pallas as pl
from jax.experimental.pallas import tpu as pltpu
from jax.sharding import Mesh
from jax.sharding import PartitionSpec as P

HEAD = 128
BLOCK = 128
NEG_FILL = -1e30
BF16 = jnp.bfloat16
F32 = jnp.float32
MIB = 2**20

VMEM = pl.BlockSpec(memory_space=pltpu.VMEM)
SMEM = pl.BlockSpec(memory_space=pltpu.SMEM)
ANY = pl.BlockSpec(memory_space=pl.ANY)


def dot(a, b, dims):
    return lax.dot_general(a, b, (dims, ((), ())), preferred_element_type=F32)


def load_rows(parts, held, sems):
    copies, at = [], 0
    for i, part in enumerate(parts):
        rows = part.shape[-2]
        to = held.at[:, pl.ds(at, rows)] if len(part.shape) == 3 else held.at[pl.ds(at, rows)]
        copies.append(pltpu.make_async_copy(part, to, sems.at[i]))
        at += rows
    return copies


SPLIT = 4


def load_pieces(parts, piece, held, sems):
    copies, n = [], len(parts)
    for i, part in enumerate(parts):
        for j in range(part.shape[0] // piece):
            at = j * n + i
            copies.append(
                pltpu.make_async_copy(
                    part.at[pl.ds(j * piece, piece)], held.at[pl.ds(at * piece, piece)], sems.at[at]
                )
            )
    return copies


def load_weights(w_ref, w_held, sems):
    copies = []
    rows = w_ref.shape[1] // SPLIT
    for c in range(3):
        for i in range(SPLIT):
            at = pl.ds(i * rows, rows)
            copies.append(pltpu.make_async_copy(w_ref.at[c, at], w_held.at[c, at], sems.at[c * SPLIT + i]))
    return copies


def load_groups(groups, piece, held, sems):
    copies, at = [], 0
    for group in groups:
        size = piece if len(group) > 1 else group[0].shape[0]
        rows = sum(p.shape[0] for p in group)
        to = held.at[pl.ds(at, rows)]
        copies += load_pieces(group, size, to, sems.at[pl.ds(at // piece, rows // size)])
        at += rows
    return copies


def cut(parts, counts):
    groups, at = [], 0
    for n in counts:
        groups.append(parts[at : at + n])
        at += n
    return groups


def project_kernel(counts, piece, tok, *refs):
    n = sum(counts)
    parts, (w_ref, qkv_ref, held, sems) = refs[:n], refs[n:]

    @pl.when(pl.program_id(0) == 0)
    def _():
        copies = load_groups(cut(parts, counts), piece, held, sems)
        for copy in copies:
            copy.start()
        for copy in copies:
            copy.wait()

    for i in range(0, held.shape[0], tok):
        qkv_ref[0, i : i + tok] = dot(held[i : i + tok], w_ref[0], ((1,), (0,))).astype(BF16)


def project(groups, piece, w_qkv):
    counts = [len(g) for g in groups]
    parts = [p for g in groups for p in g]
    rows = sum(p.shape[0] for p in parts)
    tok = groups[0][0].shape[0]
    _, width, heads = w_qkv.shape
    n = len(parts)
    return pl.pallas_call(
        functools.partial(project_kernel, counts, piece, tok),
        grid=(3,),
        out_shape=jax.ShapeDtypeStruct((3, rows, heads), BF16),
        in_specs=[ANY] * n + [pl.BlockSpec((1, width, heads), lambda c: (c, 0, 0))],
        out_specs=pl.BlockSpec((1, rows, heads), lambda c: (c, 0, 0)),
        scratch_shapes=[pltpu.VMEM((rows, width), BF16), pltpu.SemaphoreType.DMA((rows // piece,))],
        compiler_params=pltpu.CompilerParams(vmem_limit_bytes=32 * MIB),
        cost_estimate=pl.CostEstimate(
            flops=6 * rows * width * heads, bytes_accessed=2 * (3 * heads * (width + rows) + rows * width), transcendentals=0
        ),
        name="project",
    )(*parts, w_qkv)


def cotangent_kernel(pieces, at_ref, grad_y_ref, w_ref, own_ref, sent_ref, cols_ref):
    quarter, chunk = at_ref[0], at_ref[1]
    chunks, tok, cols = cols_ref.shape
    piece = tok // pieces
    own_ref[...] = dot(grad_y_ref[...], w_ref[...], ((1,), (1,))).astype(BF16)
    for i in range(pieces):
        source = pl.ds(pl.multiple_of((quarter ^ i) * piece, piece), piece)
        to = slice(i * piece, (i + 1) * piece)
        sent_ref[to] = own_ref[source]
        for d in range(chunks):
            cols_ref[d, to] = grad_y_ref[source, d * cols : (d + 1) * cols]
    here = pl.ds(pl.multiple_of(chunk * cols, cols), cols)
    cols_ref[chunk] = grad_y_ref[:, here]


def cotangent(quarter, chunk, grad_y, w_out, pieces, chunks):
    tok, width = grad_y.shape
    heads = w_out.shape[0]
    return pl.pallas_call(
        functools.partial(cotangent_kernel, pieces),
        out_shape=(
            jax.ShapeDtypeStruct((tok, heads), BF16),
            jax.ShapeDtypeStruct((tok, heads), BF16),
            jax.ShapeDtypeStruct((chunks, tok, width // chunks), BF16),
        ),
        in_specs=[SMEM, VMEM, VMEM],
        out_specs=(VMEM, VMEM, VMEM),
        compiler_params=pltpu.CompilerParams(vmem_limit_bytes=60 * MIB),
        cost_estimate=pl.CostEstimate(
            flops=2 * tok * width * heads, bytes_accessed=2 * width * (2 * tok + heads), transcendentals=0
        ),
        name="cotangent",
    )(jnp.stack([quarter, chunk]), grad_y, w_out)


def attention_kernel(n_qkv, g_places, n_late, piece, tok, cols_ref, count_ref, home_ref, place_ref, *refs):
    refs, late = refs[n_late:], refs[:n_late]
    n_g = len(g_places)
    qkv_parts, g_parts = refs[:n_qkv], refs[n_qkv : n_qkv + n_g]
    (w_ref, grads_out, att_ref, sent_ref, kept_ref, qkv_ref, g_ref, dk_ref, dv_ref, grads_ref, w_held, held) = refs[n_qkv + n_g : -5]
    qkv_sems, g_sems, w_sems, out_sems, late_sems = refs[-5:]
    row_blocks, slots = cols_ref.shape
    heads = g_ref.shape[1] // HEAD
    scale = 1.0 / math.sqrt(HEAD)
    copies = load_rows(qkv_parts, qkv_ref, qkv_sems)
    for part, places in zip(g_parts, g_places):
        for i, at in enumerate(places):
            to = g_ref.at[pl.ds(at * tok, tok)]
            copies.append(pltpu.make_async_copy(part.at[pl.ds(i * tok, tok)], to, g_sems.at[at]))
    weights = load_weights(w_ref, w_held, w_sems)
    late_copies = load_pieces(late, piece, held, late_sems)
    for copy in late_copies + weights + copies:
        copy.start()
    dk_ref[...] = jnp.zeros_like(dk_ref)
    dv_ref[...] = jnp.zeros_like(dv_ref)
    for copy in late_copies:
        copy.wait()
    first = qkv_ref.shape[1] - held.shape[0]
    for c in range(3):
        for copy in weights[c * SPLIT : (c + 1) * SPLIT]:
            copy.wait()
        for i in range(0, held.shape[0], tok):
            qkv_ref[c, first + i : first + i + tok] = dot(held[i : i + tok], w_held[c], ((1,), (0,))).astype(BF16)
    for copy in copies:
        copy.wait()

    def row(r, carry):
        rows = pl.ds(pl.multiple_of(r * BLOCK, BLOCK), BLOCK)
        at = [pl.ds(pl.multiple_of(cols_ref[r, s] * BLOCK, BLOCK), BLOCK) for s in range(slots)]
        live = count_ref[r]
        home = pl.ds(pl.multiple_of(home_ref[r] * BLOCK, BLOCK), BLOCK)
        for h in range(heads):
            lanes = slice(h * HEAD, (h + 1) * HEAD)
            q = qkv_ref[0, rows, lanes]
            g = g_ref[rows, lanes]
            k = jnp.concatenate([qkv_ref[1, a, lanes] for a in at], axis=0)
            v = jnp.concatenate([qkv_ref[2, a, lanes] for a in at], axis=0)
            s = dot(k, q, ((1,), (1,))) * scale
            slot_of = lax.broadcasted_iota(jnp.int32, s.shape, 0) // BLOCK
            s = jnp.where(slot_of < live, s, NEG_FILL)
            e = jnp.exp(s - jnp.max(s, axis=0, keepdims=True))
            p = e * (1.0 / jnp.sum(e, axis=0, keepdims=True))
            p16 = p.astype(BF16)
            att_ref[home, lanes] = dot(p16, v, ((0,), (0,))).astype(BF16)
            dp = dot(v, g, ((1,), (1,)))
            delta = jnp.sum(p * dp, axis=0, keepdims=True)
            ds16 = (p * (dp - delta)).astype(BF16)
            grads_ref[0, rows, lanes] = (dot(ds16, k, ((0,), (0,))) * scale).astype(BF16)
            dk = dot(ds16, q, ((1,), (0,)))
            dv = dot(p16, g, ((1,), (0,)))
            for i, a in enumerate(at):
                part = slice(i * BLOCK, (i + 1) * BLOCK)
                dk_ref[a, lanes] += dk[part]
                dv_ref[a, lanes] += dv[part]
        return carry

    lax.fori_loop(0, row_blocks, row, 0)
    stores = [pltpu.make_async_copy(grads_ref.at[c], grads_out.at[c], out_sems.at[c]) for c in range(3)]
    stores[0].start()
    grads_ref[1] = (dk_ref[...] * scale).astype(BF16)
    stores[1].start()
    grads_ref[2] = dv_ref[...].astype(BF16)
    stores[2].start()

    def part(i):
        cols = kept_ref.shape[2]
        at = pl.ds(pl.multiple_of(place_ref[i] * cols, cols), cols)
        return sum(dot(grads_ref[c, :tok], w_held[c, at], ((1,), (1,))) for c in range(3))

    n_sent, n_kept = sent_ref.shape[0], kept_ref.shape[0]
    for i in range(n_sent):
        sent_ref[i] = part(i).astype(BF16)
    for i in range(n_kept):
        kept_ref[i] = part(n_sent + i)
    for copy in stores:
        copy.wait()


def attention(cols, count, home, places, n_kept, late, piece, qkv_parts, g_parts, g_places, w_qkv, tok, mp_cols):
    tokens = sum(p.shape[0] for p in g_parts)
    width = g_parts[0].shape[1]
    n_qkv, n_g = len(qkv_parts), len(g_parts)
    n_late, late_rows = len(late), sum(p.shape[0] for p in late)
    n_sent = places.shape[0] - n_kept
    return pl.pallas_call(
        functools.partial(attention_kernel, n_qkv, g_places, n_late, piece, tok),
        out_shape=(
            jax.ShapeDtypeStruct((3, tokens, width), BF16),
            jax.ShapeDtypeStruct((tokens, width), BF16),
            jax.ShapeDtypeStruct((n_sent, tok, mp_cols), BF16),
            jax.ShapeDtypeStruct((n_kept, tok, mp_cols), F32),
        ),
        in_specs=[SMEM] * 4 + [ANY] * (n_late + n_qkv + n_g + 1),
        out_specs=(ANY, VMEM, VMEM, VMEM),
        scratch_shapes=[
            pltpu.VMEM((3, tokens, width), BF16),
            pltpu.VMEM((tokens, width), BF16),
            pltpu.VMEM((tokens, width), F32),
            pltpu.VMEM((tokens, width), F32),
            pltpu.VMEM((3, tokens, width), BF16),
            pltpu.VMEM(w_qkv.shape, BF16),
            pltpu.VMEM((late_rows, late[0].shape[1]), BF16),
            pltpu.SemaphoreType.DMA((n_qkv,)),
            pltpu.SemaphoreType.DMA((tokens // tok,)),
            pltpu.SemaphoreType.DMA((3 * SPLIT,)),
            pltpu.SemaphoreType.DMA((3,)),
            pltpu.SemaphoreType.DMA((late_rows // piece,)),
        ],
        compiler_params=pltpu.CompilerParams(vmem_limit_bytes=60 * MIB),
        cost_estimate=pl.CostEstimate(flops=10**10, bytes_accessed=30 * MIB, transcendentals=0),
        name="attention",
    )(cols, count, home, places, *late, *qkv_parts, *g_parts, w_qkv)


def weight_grad_kernel(counts, piece, chunk_ref, *refs):
    n = sum(counts)
    parts, (grads_ref, out_ref, held, cols_held, sems, cols_sems) = refs[:n], refs[n:]
    rows = held.shape[1] // SPLIT
    cols = cols_held.shape[1]
    here = pl.ds(pl.multiple_of(chunk_ref[0] * cols, cols), cols)
    groups = cut([p.at[:, here] for p in parts], counts)
    loads = load_groups(groups, piece, cols_held, cols_sems)
    grad_loads = []
    for c in range(3):
        for i in range(SPLIT):
            at = pl.ds(i * rows, rows)
            grad_loads.append(pltpu.make_async_copy(grads_ref.at[c, at], held.at[c, at], sems.at[c * SPLIT + i]))
    for load in loads + grad_loads:
        load.start()
    for load in loads:
        load.wait()
    turned = cols_held[...].T
    for c in range(3):
        for load in grad_loads[c * SPLIT : (c + 1) * SPLIT]:
            load.wait()
        out_ref[c] = dot(turned, held[c], ((1,), (0,))).astype(BF16)


def weight_grad(chunk, groups, piece, grads, cols):
    counts = [len(g) for g in groups]
    token_parts = [p for g in groups for p in g]
    n = len(token_parts)
    _, tokens, heads = grads.shape
    return pl.pallas_call(
        functools.partial(weight_grad_kernel, counts, piece),
        in_specs=[SMEM] + [ANY] * (n + 1),
        out_specs=VMEM,
        out_shape=jax.ShapeDtypeStruct((3, cols, heads), BF16),
        scratch_shapes=[
            pltpu.VMEM(grads.shape, BF16),
            pltpu.VMEM((tokens, cols), BF16),
            pltpu.SemaphoreType.DMA((3 * SPLIT,)),
            pltpu.SemaphoreType.DMA((tokens // piece,)),
        ],
        compiler_params=pltpu.CompilerParams(vmem_limit_bytes=60 * MIB),
        cost_estimate=pl.CostEstimate(
            flops=6 * tokens * cols * heads, bytes_accessed=6 * tokens * heads, transcendentals=0
        ),
        name="weight_grad",
    )(chunk, *token_parts, grads)


def local(sizes, tokens_in, w_qkv, w_out, grad_y, block_cols, block_count):
    nz, nx, ny, nc = sizes
    mesh_size = dict(z=nz, x=nx, y=ny, c=nc)
    chunks, pieces = nz * nx, ny * nc
    tok, width = tokens_in.shape
    piece = tok // pieces
    out_cols = width // chunks
    blocks = tok // BLOCK
    y, c = lax.axis_index("y"), lax.axis_index("c")
    chunk = lax.axis_index("z") * nx + lax.axis_index("x")
    quarter = y * nc + c
    quarter_block = quarter * blocks // pieces

    def swap(a, axis, k):
        n = mesh_size[axis]
        return lax.ppermute(a, axis, [(i, i ^ k) for i in range(n)])

    def my_piece(a, k):
        return lax.dynamic_slice_in_dim(a, (quarter ^ k) * piece, piece, 0)

    def after(a, *done):
        return lax.optimization_barrier((a, done))[0]

    batches = [[1, 2], [4, 3], [i for k in range(3, nz) for i in (2 * k, 2 * k - 1)] + [2 * nz - 1]]
    order = [0] + [k for batch in batches for k in batch]
    g_own, g_sent, y_sent = cotangent(quarter, chunk, grad_y, w_out, pieces, chunks)

    def along_z(held, start, k):
        low = k & -k
        held[2 * k] = swap(start if k == low else held[2 * (k ^ low)], "z", low)

    own = my_piece(tokens_in, 0)
    got = {}
    for k in range(1, nz):
        along_z(got, own, k)
    got[1] = swap(own, "x", 1)
    got[3] = swap(after(got[2], got[1], g_own), "x", 1)
    last_x = got[3]
    for k in range(2, nz - 1):
        got[2 * k + 1] = last_x = swap(after(got[2 * k], last_x), "x", 1)
    got[2 * nz - 1] = swap(got[2 * nz - 3], "z", 1)

    groups = [[tokens_in]]
    behind, qkv_parts = [], []
    for at, batch in enumerate(batches):
        mine = jnp.concatenate([got[k] for k in batch], axis=0)
        ys = [mine] + [swap(after(mine, *behind), "y", i) for i in range(1, ny)]
        behind = ys[1:]
        parts = []
        for i, a in enumerate(ys):
            core = after(a, *qkv_parts) if i == 0 else a
            parts += [a] + [swap(core, "c", j) for j in range(1, nc)]
        groups.append(parts)
        if at == 1:
            qkv_parts = [project(groups, piece, w_qkv)]
    late = groups[-1]

    g = {0: g_own, 1: swap(after(g_sent, last_x), "x", 1)}
    g_late = after(g_sent, got[2 * nz - 1])
    for k in range(1, nz):
        along_z(g, g_late, k)
    g_far = [g[2 * k] for k in range(1, nz)]
    g_x = swap(after(jnp.concatenate(g_far, axis=0), g[1]), "x", 1)
    g_parts = [g_own, g[1]] + g_far + [g_x]
    g_places, at = [], 0
    g_order = [0, 1] + [2 * k for k in range(1, nz)] + [2 * k + 1 for k in range(1, nz)]
    for part in g_parts:
        n = part.shape[0] // tok
        g_places.append([order.index(k) for k in g_order[at : at + n]])
        at += n

    y_sent = after(y_sent, *g_far)
    y_all = lax.all_to_all(y_sent, ("z", "x"), 0, 0, tiled=True).reshape(chunks * tok, out_cols)

    held = jnp.repeat(jnp.array(order, jnp.int32), blocks)
    inner = jnp.tile(jnp.arange(blocks, dtype=jnp.int32), chunks)
    number = jnp.arange(chunks * blocks, dtype=jnp.int32)

    def flip(k):
        return jnp.where(k == 0, 0, quarter_block)

    block_at = (held ^ chunk) * blocks + (inner ^ flip(held))
    pick = block_at[:, None] == number[None, :]
    cols = jnp.sum(jnp.where(pick[:, :, None], block_cols[None], 0), axis=1)
    count = jnp.sum(jnp.where(pick, block_count[None], 0), axis=1)
    cols = jnp.sum(jnp.where(cols[:, :, None] == block_at[None, None, :], number[None, None, :], 0), axis=2)
    home = (held ^ chunk) * blocks + inner

    by_y = y ^ jnp.arange(ny, dtype=jnp.int32)
    places = jnp.concatenate([by_y * nc + (c ^ j) for j in range(1, nc)] + [by_y * nc + c])
    grads, att, sent, half = attention(
        cols, count, home, places, ny, late, piece, qkv_parts, g_parts, g_places, w_qkv, tok, width // pieces
    )
    for j in range(1, nc):
        half = half + swap(sent[(j - 1) * ny : j * ny], "c", j).astype(F32)
    grad_x = half[0]
    for k in range(1, ny):
        grad_x = grad_x + swap(half[k].astype(BF16), "y", k).astype(F32)

    grad_qkv = weight_grad(chunk.reshape(1), groups, piece, grads, out_cols)
    grad_out = dot(att, y_all, ((0,), (0,))).astype(BF16)
    return (grad_x.astype(BF16), grad_qkv, grad_out)


def solution(mesh):
    chunks, pieces = mesh.shape["blk"], mesh.shape["mp"]
    sizes = (chunks // 2, 2, pieces // 2, 2)
    fine = Mesh(mesh.devices.reshape(sizes), ("z", "x", "y", "c"))
    blk, mp = ("z", "x"), ("y", "c")
    in_specs = (P(blk, None), P(None, None, mp), P(mp, None), P(blk, None), P(), P())
    out_specs = (P(blk, mp), P(None, blk, mp), P(mp, blk))
    return jax.shard_map(
        functools.partial(local, sizes), mesh=fine, in_specs=in_specs, out_specs=out_specs, check_vma=False
    )
```

time: 222 us -> 146 us (0.66)
  waiting for transfers between devices: 84 us -> 33.1 us
  matrix products: 33.8 us -> 3.05 us
  Pallas kernels: 33.3 us -> 61.9 us
  starting transfers between devices: 40.3 us -> 26.9 us
  local copies, waits for them, and re-layouts: 21 us -> 13.4 us
    ppermute x39 -> x23, waiting for transfers between devices: 84 us -> 33.1 us  [swap(): return lax.ppermute(a, axis, [(i, i ^ k) for i in range(n)])]
    dot_general x10 -> x0, matrix products: 29.7 us -> none  [the longest x8 18.9 us: local(): jnp.einsum('td,cde->cte', t, w_qkv, preferred_element_type=F32).astype(BF16)]
    pallas_call x1 -> x4, Pallas kernels: 33.3 us -> 61.9 us  [the longest x1 42.1 us: attention(): pl.pallas_call(functools.partial(attention_kernel, n_qkv, g_places, n_lat...]
    ppermute x39 -> x23, starting transfers between devices: 40.3 us -> 23.1 us  [swap(): return lax.ppermute(a, axis, [(i, i ^ k) for i in range(n)])]
    dynamic_slice x4 -> x0, local copies, waits for them, and re-layouts: 3.92 us -> none  [the longest x2 2.06 us: columns(): return lax.dynamic_slice_in_dim(a, (chunk ^ k) * out_cols, out_cols, 1)]
    all_to_all x0 -> x1, starting transfers between devices: none -> 3.83 us  [local(): lax.all_to_all(y_sent, ('z', 'x'), 0, 0, tiled=True)]
    reshape x1 -> x0, local copies, waits for them, and re-layouts: 3.03 us -> none  [local(): dx = dx.reshape(tok, ny, nc, width // pieces)]
    unnamed x93 -> x42, local copies, waits for them, and re-layouts: 12.5 us -> 9.62 us
  transfers between devices with their start and end apart: 39 -> 24, of which waited for: 17 -> 9; matrix products, arithmetic and copies ran while one was open for 15% -> 10% of each run, Pallas kernels for 0% -> 43%
where the time goes in v2:
time: 146 us; the launch traced here: 145 us
  Pallas kernels  61.9 us (42%)
  waiting for transfers between devices  33.1 us (23%)
  starting transfers between devices  26.9 us (18%)
  local copies, waits for them, and re-layouts  13.4 us (9%)
  other arithmetic  5.84 us (4%)
  matrix products  3.05 us (2%)
    pallas_call x1, Pallas kernels, attention(): pl.pallas_call(functools.partial(attention_kernel, n_qkv, g_places, n_lat...  42.1 us
    ppermute x23, waiting for transfers between devices, swap(): return lax.ppermute(a, axis, [(i, i ^ k) for i in range(n)])  33.1 us
    ppermute x23, starting transfers between devices, swap(): return lax.ppermute(a, axis, [(i, i ^ k) for i in range(n)])  23.1 us
    unnamed x42, local copies, waits for them, and re-layouts  9.62 us
    pallas_call x1, Pallas kernels, project(): pl.pallas_call(functools.partial(project_kernel, counts, piece, tok), gri...  9.19 us
    pallas_call x1, Pallas kernels, weight_grad(): pl.pallas_call(functools.partial(weight_grad_kernel, counts, piece), in_s...  6.69 us
    pallas_call x1, Pallas kernels, cotangent(): pl.pallas_call(functools.partial(cotangent_kernel, pieces), out_shape=(ja...  3.92 us
    all_to_all x1, starting transfers between devices, local(): lax.all_to_all(y_sent, ('z', 'x'), 0, 0, tiled=True)  3.83 us
  transfers between devices with their start and end apart: 24, of which 9 were waited for; matrix products, arithmetic and copies ran while one was open for 10% of the time, Pallas kernels for 43%

profile of v2, /device:TPU:0, one launch (start us, length us, event | category | flops | bytes accessed | tf_op | source)
XLA Modules:
  0.0 145.2 jit_solution(7307356886634922930)
XLA Ops:
  1.6 3.0 %collective-permute-start.3 = (bf16[64,2048]{1,0:T(8,128)(2,1)S(1)}, bf16[64,2048]{1,0:T(8,128)(2,1)S(1)}, u32[]{:S(2)}, u32[]{:S(2)}) collective-permute-start(bf16[64,2048]{1,0:T(8,128)(2,1)S(1)} %constant_dynamic-slice_fusion), channel_id=1, source_target_pairs={{0,4},{4,0},{1,5},{5,1},{2,6},{6,2},{3,7},{7,3},{8,12},{12,8},{9,1... | collective-permute-start | bytes 786440 | tf_op jit(solution)/shard_map/ppermute | solution.py:338
  6.2 2.6 %collective-permute-start = (bf16[64,2048]{1,0:T(8,128)(2,1)S(1)}, bf16[64,2048]{1,0:T(8,128)(2,1)S(1)}, u32[]{:S(2)}, u32[]{:S(2)}) collective-permute-start(bf16[64,2048]{1,0:T(8,128)(2,1)S(1)} %constant_dynamic-slice_fusion), channel_id=1, source_target_pairs={{0,16},{8,24},{16,0},{24,8},{1,17},{9,25},{17,1},{25,9},{2,18},{10... | collective-permute-start | bytes 786440 | tf_op jit(solution)/shard_map/ppermute | solution.py:338
  9.4 3.9 %cotangent.1 = (bf16[256,512]{1,0:T(8,128)(2,1)}, bf16[256,512]{1,0:T(8,128)(2,1)}, bf16[8,256,256]{2,1,0:T(8,128)(2,1)}) custom-call(s32[2]{0:T(128)} %pad_add_fusion.1.at_ref, bf16[256,2048]{1,0:T(8,128)(2,1)} %grad_y_ref.1, bf16[512,2048]{1,0:T(8,128)(2,1)} %w_ref.1), custom_call_target="tpu_custom_call" | custom-call | flops 536870912 | bytes 4194304 | tf_op jit(solution)/shard_map/cotangent/pallas_call | solution.py:139
  13.4 4.5 %collective-permute-done.2 = bf16[64,2048]{1,0:T(8,128)(2,1)S(1)} collective-permute-done((bf16[64,2048]{1,0:T(8,128)(2,1)S(1)}, bf16[64,2048]{1,0:T(8,128)(2,1)S(1)}, u32[]{:S(2)}, u32[]{:S(2)}) %collective-permute-start.2) | collective-permute-done | bytes 262176 | tf_op jit(solution)/shard_map/ppermute | solution.py:338
  18.3 1.8 %collective-permute-start.8 = (bf16[128,2048]{1,0:T(8,128)(2,1)S(1)}, bf16[128,2048]{1,0:T(8,128)(2,1)S(1)}, u32[]{:S(2)}, u32[]{:S(2)}) collective-permute-start(bf16[128,2048]{1,0:T(8,128)(2,1)S(1)} %constant_dynamic-update-slice_fusion.3.refs_1_), channel_id=1, source_target_pairs={{0,2},{2,0},{1,3},{3,1},{4,6},{6,4},{5,7},{7,5},{8,10},{10,8},{9,1... | collective-permute-start | bytes 1572872 | tf_op jit(solution)/shard_map/ppermute | solution.py:338
  20.2 4.5 %collective-permute-done.4 = bf16[64,2048]{1,0:T(8,128)(2,1)S(1)} collective-permute-done((bf16[64,2048]{1,0:T(8,128)(2,1)S(1)}, bf16[64,2048]{1,0:T(8,128)(2,1)S(1)}, u32[]{:S(2)}, u32[]{:S(2)}) %collective-permute-start.4) | collective-permute-done | bytes 262176 | tf_op jit(solution)/shard_map/ppermute | solution.py:338
  25.5 5.7 %collective-permute-done.5 = bf16[64,2048]{1,0:T(8,128)(2,1)} collective-permute-done((bf16[64,2048]{1,0:T(8,128)(2,1)S(1)}, bf16[64,2048]{1,0:T(8,128)(2,1)}, u32[]{:S(2)}, u32[]{:S(2)}) %collective-permute-start.5) | collective-permute-done | bytes 262176 | tf_op jit(solution)/shard_map/ppermute | solution.py:338
  34.2 3.8 %collective-permute-done.6 = bf16[64,2048]{1,0:T(8,128)(2,1)} collective-permute-done((bf16[64,2048]{1,0:T(8,128)(2,1)}, bf16[64,2048]{1,0:T(8,128)(2,1)}, u32[]{:S(2)}, u32[]{:S(2)}) %collective-permute-start.6) | collective-permute-done | bytes 262176 | tf_op jit(solution)/shard_map/ppermute | solution.py:338
  39.4 2.3 %collective-permute-start.17 = (bf16[256,512]{1,0:T(8,128)(2,1)}, bf16[256,512]{1,0:T(8,128)(2,1)}, u32[]{:S(2)}, u32[]{:S(2)}) collective-permute-start(bf16[256,512]{1,0:T(8,128)(2,1)} %get-tuple-element.27), channel_id=1, source_target_pairs={{0,8},{8,0},{16,24},{24,16},{1,9},{9,1},{17,25},{25,17},{2,10},{10... | collective-permute-start | bytes 786440 | tf_op jit(solution)/shard_map/ppermute | solution.py:338
  42.3 1.7 %constant_dynamic-update-slice_fusion.2 = bf16[192,2048]{1,0:T(8,128)(2,1)} fusion(bf16[64,2048]{1,0:T(8,128)(2,1)} %collective-permute-done.1), kind=kLoop, calls=%fused_computation.10 | loop fusion | bytes 524288
  44.4 5.4 %collective-permute-done.18.refs_8_ = bf16[256,512]{1,0:T(8,128)(2,1)} collective-permute-done((bf16[256,512]{1,0:T(8,128)(2,1)}, bf16[256,512]{1,0:T(8,128)(2,1)}, u32[]{:S(2)}, u32[]{:S(2)}) %collective-permute-start.18) | collective-permute-done | bytes 262176 | tf_op jit(solution)/shard_map/ppermute | solution.py:338
  50.4 1.7 %constant_dynamic-update-slice_fusion.1 = bf16[192,2048]{1,0:T(8,128)(2,1)} fusion(bf16[192,2048]{1,0:T(8,128)(2,1)} %constant_dynamic-update-slice_fusion.2, bf16[64,2048]{1,0:T(8,128)(2,1)} %collective-permute-done.5), kind=kLoop, calls=%fused_computation.9 | loop fusion | bytes 524288
  52.0 1.7 %constant_dynamic-update-slice_fusion.refs_0_.refs_9_ = bf16[192,2048]{1,0:T(8,128)(2,1)} fusion(bf16[192,2048]{1,0:T(8,128)(2,1)} %constant_dynamic-update-slice_fusion.1, bf16[64,2048]{1,0:T(8,128)(2,1)} %collective-permute-done.6), kind=kLoop, calls=%fused_computation.8 | loop fusion | bytes 524288 | tf_op jit(solution)/shard_map/concatenate | solution.py:368
  53.7 5.0 %collective-permute-done.19.refs_9_ = bf16[256,512]{1,0:T(8,128)(2,1)S(1)} collective-permute-done((bf16[256,512]{1,0:T(8,128)(2,1)}, bf16[256,512]{1,0:T(8,128)(2,1)S(1)}, u32[]{:S(2)}, u32[]{:S(2)}) %collective-permute-start.19) | collective-permute-done | bytes 262176 | tf_op jit(solution)/shard_map/ppermute | solution.py:338
  60.1 2.0 %pad_maximum_fusion = bf16[768,512]{1,0:T(8,128)(2,1)} fusion(bf16[256,512]{1,0:T(8,128)(2,1)S(1)} %collective-permute-done.19.refs_9_, bf16[256,512]{1,0:T(8,128)(2,1)} %collective-permute-done.18.refs_8_, bf16[256,512]{1,0:T(8,128)(2,1)} %collective-permute-done.17.refs_7_), kind=kLoop, calls=%fused_computation.2 | loop fusion | flops 2359296 | bytes 1572864 | tf_op jit(solution)/shard_map/concatenate | solution.py:385
  62.1 2.1 %collective-permute-start.20 = (bf16[768,512]{1,0:T(8,128)(2,1)}, bf16[768,512]{1,0:T(8,128)(2,1)}, u32[]{:S(2)}, u32[]{:S(2)}) collective-permute-start(bf16[768,512]{1,0:T(8,128)(2,1)} %pad_maximum_fusion), channel_id=1, source_target_pairs={{0,4},{4,0},{1,5},{5,1},{2,6},{6,2},{3,7},{7,3},{8,12},{12,8},{9,1... | collective-permute-start | bytes 2359304 | tf_op jit(solution)/shard_map/ppermute | solution.py:338
  64.3 3.1 %copy-done.9 = bf16[3,2048,512]{2,1,0:T(8,128)(2,1)S(1)} copy-done((bf16[3,2048,512]{2,1,0:T(8,128)(2,1)S(1)}, bf16[3,2048,512]{2,1,0:T(8,128)(2,1)}, u32[]{:S(2)}) %copy-start.9) | copy-done | bytes 6291480
  67.4 9.2 %project.1.refs_4_ = bf16[3,1280,512]{2,1,0:T(8,128)(2,1)S(1)} custom-call(bf16[256,2048]{1,0:T(8,128)(2,1)S(1)} %copy-done, bf16[128,2048]{1,0:T(8,128)(2,1)S(1)} %constant_dynamic-update-slice_fusion.3.refs_1_, bf16[128,2048]{1,0:T(8,128)(2,1)S(1)} %collective-permute-done.7.refs_2_, bf16[128,2048]{1,0:T(8,128)(2,1)S(1)} %collective-permute-done.8.refs_3_, ...), custom_call_target="tpu_custom_call" | custom-call | flops 8053063680 | bytes 15466496 | tf_op jit(solution)/shard_map/project/pallas_call | solution.py:106
  76.7 2.0 %copy-done.10 = bf16[3,1280,512]{2,1,0:T(8,128)(2,1)} copy-done((bf16[3,1280,512]{2,1,0:T(8,128)(2,1)}, bf16[3,1280,512]{2,1,0:T(8,128)(2,1)S(1)}, u32[]{:S(2)}) %copy-start.10) | copy-done | bytes 3932184
  81.6 3.8 %all-to-all-start = ((bf16[8,256,256]{2,1,0:T(8,128)(2,1)}), bf16[8,256,256]{2,1,0:T(8,128)(2,1)S(1)}, u32[]{:S(2)}, u32[]{:S(2)}) async-start(bf16[8,256,256]{2,1,0:T(8,128)(2,1)} %get-tuple-element.34), calls=%async_computation | async-start | bytes 2097152 | tf_op jit(solution)/shard_map/all_to_all | solution.py:395
  86.5 42.1 %attention.1 = (bf16[3,2048,512]{2,1,0:T(8,128)(2,1)}, bf16[2048,512]{1,0:T(8,128)(2,1)}, bf16[2,256,512]{2,1,0:T(8,128)(2,1)}, f32[2,256,512]{2,1,0:T(8,128)}) custom-call(s32[16,2]{1,0:T(8,128)} %copy.12.cols_ref, s32[16]{0:T(128)} %select_reduce_fusion.2.count_ref, s32[16]{0:T(128)} %get-tuple-element.35.home_ref, s32[4]{0:T(128)} %pad_add_fusion.place_ref, ...), custom_call_target="tpu_custom_call" | custom-call | flops 10000000000 | bytes 31457280 | tf_op jit(solution)/shard_map/attention/pallas_call | solution.py:245
  128.9 6.7 %weight_grad.1 = bf16[3,256,512]{2,1,0:T(8,128)(2,1)} custom-call(s32[1]{0:T(128)} %bitcast.1.chunk_ref, bf16[256,2048]{1,0:T(8,128)(2,1)} %refs_0_.3, bf16[128,2048]{1,0:T(8,128)(2,1)} %copy-done.2, bf16[128,2048]{1,0:T(8,128)(2,1)} %copy-done.5, bf16[128,2048]{1,0:T(8,128)(2,1)} %copy-done.3, bf16[128,2048]{1,0:T(8,128)(2,1)} %copy-done.7, ...), custom_call_target="tpu_custom_call" | custom-call | flops 1610612736 | bytes 6291456 | tf_op jit(solution)/shard_map/weight_grad/pallas_call | solution.py:304
  137.5 3.0 %convolution_convert_fusion = bf16[512,256]{1,0:T(8,128)(2,1)} fusion(bf16[2048,512]{1,0:T(8,128)(2,1)} %get-tuple-element.32, bf16[2048,256]{1,0:T(8,128)(2,1)S(1)} %bitcast.13), kind=kOutput, calls=%fused_computation | convolution fusion | flops 537001984 | bytes 3407872 | tf_op jit(solution)/shard_map/dot_general | solution.py:25
  140.5 3.9 %collective-permute-done.22 = bf16[256,512]{1,0:T(8,128)(2,1)S(1)} collective-permute-done((bf16[256,512]{1,0:T(8,128)(2,1)S(1)}, bf16[256,512]{1,0:T(8,128)(2,1)S(1)}, u32[]{:S(2)}, u32[]{:S(2)}) %collective-permute-start.22) | collective-permute-done | bytes 262176 | tf_op jit(solution)/shard_map/ppermute | solution.py:338
  (96 shorter events, 18.9 us)
Async XLA Ops:
  1.6 11.7 %collective-permute-start.3 = (bf16[64,2048]{1,0:T(8,128)(2,1)S(1)}, bf16[64,2048]{1,0:T(8,128)(2,1)S(1)}, u32[]{:S(2)}, u32[]{:S(2)}) collective-permute-start(bf16[64,2048]{1,0:T(8,128)(2,1)S(1)} %constant_dynamic-slice_fusion), channel_id=1, source_target_pairs={{0,4},{4,0},{1,5},{5,1},{2,6},{6,2},{3,7},{7,3},{8,12},{12,8},{9,1... | collective-permute-start | bytes 786440 | tf_op jit(solution)/shard_map/ppermute | solution.py:338
  4.6 13.3 %collective-permute-start.2 = (bf16[64,2048]{1,0:T(8,128)(2,1)S(1)}, bf16[64,2048]{1,0:T(8,128)(2,1)S(1)}, u32[]{:S(2)}, u32[]{:S(2)}) collective-permute-start(bf16[64,2048]{1,0:T(8,128)(2,1)S(1)} %constant_dynamic-slice_fusion), channel_id=1, source_target_pairs={{0,8},{8,0},{16,24},{24,16},{1,9},{9,1},{17,25},{25,17},{2,10},{10... | collective-permute-start | bytes 786440 | tf_op jit(solution)/shard_map/ppermute | solution.py:338
  6.2 14.0 %collective-permute-start = (bf16[64,2048]{1,0:T(8,128)(2,1)S(1)}, bf16[64,2048]{1,0:T(8,128)(2,1)S(1)}, u32[]{:S(2)}, u32[]{:S(2)}) collective-permute-start(bf16[64,2048]{1,0:T(8,128)(2,1)S(1)} %constant_dynamic-slice_fusion), channel_id=1, source_target_pairs={{0,16},{8,24},{16,0},{24,8},{1,17},{9,25},{17,1},{25,9},{2,18},{10... | collective-permute-start | bytes 786440 | tf_op jit(solution)/shard_map/ppermute | solution.py:338
  17.9 6.9 %collective-permute-start.4 = (bf16[64,2048]{1,0:T(8,128)(2,1)S(1)}, bf16[64,2048]{1,0:T(8,128)(2,1)S(1)}, u32[]{:S(2)}, u32[]{:S(2)}) collective-permute-start(bf16[64,2048]{1,0:T(8,128)(2,1)S(1)} %collective-permute-done.2), channel_id=1, source_target_pairs={{0,4},{4,0},{1,5},{5,1},{2,6},{6,2},{3,7},{7,3},{8,12},{12,8},{9,1... | collective-permute-start | bytes 786440 | tf_op jit(solution)/shard_map/ppermute | solution.py:338
  18.3 12.9 %collective-permute-start.8 = (bf16[128,2048]{1,0:T(8,128)(2,1)S(1)}, bf16[128,2048]{1,0:T(8,128)(2,1)S(1)}, u32[]{:S(2)}, u32[]{:S(2)}) collective-permute-start(bf16[128,2048]{1,0:T(8,128)(2,1)S(1)} %constant_dynamic-update-slice_fusion.3.refs_1_), channel_id=1, source_target_pairs={{0,2},{2,0},{1,3},{3,1},{4,6},{6,4},{5,7},{7,5},{8,10},{10,8},{9,1... | collective-permute-start | bytes 1572872 | tf_op jit(solution)/shard_map/ppermute | solution.py:338
  24.7 6.5 %collective-permute-start.5 = (bf16[64,2048]{1,0:T(8,128)(2,1)S(1)}, bf16[64,2048]{1,0:T(8,128)(2,1)}, u32[]{:S(2)}, u32[]{:S(2)}) collective-permute-start(bf16[64,2048]{1,0:T(8,128)(2,1)S(1)} %collective-permute-done), channel_id=1, source_target_pairs={{0,4},{4,0},{1,5},{5,1},{2,6},{6,2},{3,7},{7,3},{8,12},{12,8},{9,1... | collective-permute-start | bytes 786440 | tf_op jit(solution)/shard_map/ppermute | solution.py:338
  25.4 16.8 %collective-permute-start.1 = (bf16[64,2048]{1,0:T(8,128)(2,1)S(1)}, bf16[64,2048]{1,0:T(8,128)(2,1)}, u32[]{:S(2)}, u32[]{:S(2)}) collective-permute-start(bf16[64,2048]{1,0:T(8,128)(2,1)S(1)} %collective-permute-done), channel_id=1, source_target_pairs={{0,8},{8,0},{16,24},{24,16},{1,9},{9,1},{17,25},{25,17},{2,10},{10... | collective-permute-start | bytes 786440 | tf_op jit(solution)/shard_map/ppermute | solution.py:338
  31.2 6.7 %collective-permute-start.6 = (bf16[64,2048]{1,0:T(8,128)(2,1)}, bf16[64,2048]{1,0:T(8,128)(2,1)}, u32[]{:S(2)}, u32[]{:S(2)}) collective-permute-start(bf16[64,2048]{1,0:T(8,128)(2,1)} %collective-permute-done.5), channel_id=1, source_target_pairs={{0,8},{8,0},{16,24},{24,16},{1,9},{9,1},{17,25},{25,17},{2,10},{10... | collective-permute-start | bytes 786440 | tf_op jit(solution)/shard_map/ppermute | solution.py:338
  31.3 18.7 %collective-permute-start.11 = (bf16[128,2048]{1,0:T(8,128)(2,1)S(1)}, bf16[128,2048]{1,0:T(8,128)(2,1)S(1)}, u32[]{:S(2)}, u32[]{:S(2)}) collective-permute-start(bf16[128,2048]{1,0:T(8,128)(2,1)S(1)} %constant_dynamic-update-slice_fusion.5.refs_5_), channel_id=1, source_target_pairs={{0,2},{2,0},{1,3},{3,1},{4,6},{6,4},{5,7},{7,5},{8,10},{10,8},{9,1... | collective-permute-start | bytes 1572872 | tf_op jit(solution)/shard_map/ppermute | solution.py:338
  33.3 10.7 %collective-permute-start.16 = (bf16[256,512]{1,0:T(8,128)(2,1)}, bf16[256,512]{1,0:T(8,128)(2,1)}, u32[]{:S(2)}, u32[]{:S(2)}) collective-permute-start(bf16[256,512]{1,0:T(8,128)(2,1)} %get-tuple-element.27), channel_id=1, source_target_pairs={{0,4},{4,0},{1,5},{5,1},{2,6},{6,2},{3,7},{7,3},{8,12},{12,8},{9,1... | collective-permute-start | bytes 786440 | tf_op jit(solution)/shard_map/ppermute | solution.py:338
  37.9 11.9 %collective-permute-start.18 = (bf16[256,512]{1,0:T(8,128)(2,1)}, bf16[256,512]{1,0:T(8,128)(2,1)}, u32[]{:S(2)}, u32[]{:S(2)}) collective-permute-start(bf16[256,512]{1,0:T(8,128)(2,1)} %get-tuple-element.27), channel_id=1, source_target_pairs={{0,16},{8,24},{16,0},{24,8},{1,17},{9,25},{17,1},{25,9},{2,18},{10... | collective-permute-start | bytes 786440 | tf_op jit(solution)/shard_map/ppermute | solution.py:338
  39.4 10.6 %collective-permute-start.17 = (bf16[256,512]{1,0:T(8,128)(2,1)}, bf16[256,512]{1,0:T(8,128)(2,1)}, u32[]{:S(2)}, u32[]{:S(2)}) collective-permute-start(bf16[256,512]{1,0:T(8,128)(2,1)} %get-tuple-element.27), channel_id=1, source_target_pairs={{0,8},{8,0},{16,24},{24,16},{1,9},{9,1},{17,25},{25,17},{2,10},{10... | collective-permute-start | bytes 786440 | tf_op jit(solution)/shard_map/ppermute | solution.py:338
  42.3 19.8 %collective-permute-start.7 = (bf16[128,2048]{1,0:T(8,128)(2,1)S(1)}, bf16[128,2048]{1,0:T(8,128)(2,1)S(1)}, u32[]{:S(2)}, u32[]{:S(2)}) collective-permute-start(bf16[128,2048]{1,0:T(8,128)(2,1)S(1)} %constant_dynamic-update-slice_fusion.3.refs_1_), channel_id=1, source_target_pairs={{0,1},{1,0},{2,3},{3,2},{4,5},{5,4},{6,7},{7,6},{8,9},{9,8},{10,11... | collective-permute-start | bytes 1572872 | tf_op jit(solution)/shard_map/ppermute | solution.py:338
  43.9 20.3 %collective-permute-start.10 = (bf16[128,2048]{1,0:T(8,128)(2,1)S(1)}, bf16[128,2048]{1,0:T(8,128)(2,1)S(1)}, u32[]{:S(2)}, u32[]{:S(2)}) collective-permute-start(bf16[128,2048]{1,0:T(8,128)(2,1)S(1)} %constant_dynamic-update-slice_fusion.5.refs_5_), channel_id=1, source_target_pairs={{0,1},{1,0},{2,3},{3,2},{4,5},{5,4},{6,7},{7,6},{8,9},{9,8},{10,11... | collective-permute-start | bytes 1572872 | tf_op jit(solution)/shard_map/ppermute | solution.py:338
  49.8 14.4 %collective-permute-start.9 = (bf16[128,2048]{1,0:T(8,128)(2,1)S(1)}, bf16[128,2048]{1,0:T(8,128)(2,1)S(1)}, u32[]{:S(2)}, u32[]{:S(2)}) collective-permute-start(bf16[128,2048]{1,0:T(8,128)(2,1)S(1)} %collective-permute-done.8.refs_3_), channel_id=1, source_target_pairs={{0,1},{1,0},{2,3},{3,2},{4,5},{5,4},{6,7},{7,6},{8,9},{9,8},{10,11... | collective-permute-start | bytes 1572872 | tf_op jit(solution)/shard_map/ppermute | solution.py:338
  50.0 8.8 %collective-permute-start.19 = (bf16[256,512]{1,0:T(8,128)(2,1)}, bf16[256,512]{1,0:T(8,128)(2,1)S(1)}, u32[]{:S(2)}, u32[]{:S(2)}) collective-permute-start(bf16[256,512]{1,0:T(8,128)(2,1)} %collective-permute-done.18.refs_8_), channel_id=1, source_target_pairs={{0,8},{8,0},{16,24},{24,16},{1,9},{9,1},{17,25},{25,17},{2,10},{10... | collective-permute-start | bytes 786440 | tf_op jit(solution)/shard_map/ppermute | solution.py:338
  50.0 14.3 %collective-permute-start.12 = (bf16[128,2048]{1,0:T(8,128)(2,1)S(1)}, bf16[128,2048]{1,0:T(8,128)(2,1)S(1)}, u32[]{:S(2)}, u32[]{:S(2)}) collective-permute-start(bf16[128,2048]{1,0:T(8,128)(2,1)S(1)} %collective-permute-done.11.refs_7_), channel_id=1, source_target_pairs={{0,1},{1,0},{2,3},{3,2},{4,5},{5,4},{6,7},{7,6},{8,9},{9,8},{10,11... | collective-permute-start | bytes 1572872 | tf_op jit(solution)/shard_map/ppermute | solution.py:338
  58.7 19.9 %collective-permute-start.14 = (bf16[192,2048]{1,0:T(8,128)(2,1)}, bf16[192,2048]{1,0:T(8,128)(2,1)}, u32[]{:S(2)}, u32[]{:S(2)}) collective-permute-start(bf16[192,2048]{1,0:T(8,128)(2,1)} %constant_dynamic-update-slice_fusion.refs_0_.refs_9_), channel_id=1, source_target_pairs={{0,2},{2,0},{1,3},{3,1},{4,6},{6,4},{5,7},{7,5},{8,10},{10,8},{9,1... | collective-permute-start | bytes 2359304 | tf_op jit(solution)/shard_map/ppermute | solution.py:338
  62.1 23.3 %collective-permute-start.20 = (bf16[768,512]{1,0:T(8,128)(2,1)}, bf16[768,512]{1,0:T(8,128)(2,1)}, u32[]{:S(2)}, u32[]{:S(2)}) collective-permute-start(bf16[768,512]{1,0:T(8,128)(2,1)} %pad_maximum_fusion), channel_id=1, source_target_pairs={{0,4},{4,0},{1,5},{5,1},{2,6},{6,2},{3,7},{7,3},{8,12},{12,8},{9,1... | collective-permute-start | bytes 2359304 | tf_op jit(solution)/shard_map/ppermute | solution.py:338
  78.7 6.7 %collective-permute-start.13 = (bf16[192,2048]{1,0:T(8,128)(2,1)}, bf16[192,2048]{1,0:T(8,128)(2,1)S(1)}, u32[]{:S(2)}, u32[]{:S(2)}) collective-permute-start(bf16[192,2048]{1,0:T(8,128)(2,1)} %constant_dynamic-update-slice_fusion.refs_0_.refs_9_), channel_id=1, source_target_pairs={{0,1},{1,0},{2,3},{3,2},{4,5},{5,4},{6,7},{7,6},{8,9},{9,8},{10,11... | collective-permute-start | bytes 2359304 | tf_op jit(solution)/shard_map/ppermute | solution.py:338
  78.7 6.7 %collective-permute-start.15 = (bf16[192,2048]{1,0:T(8,128)(2,1)}, bf16[192,2048]{1,0:T(8,128)(2,1)S(1)}, u32[]{:S(2)}, u32[]{:S(2)}) collective-permute-start(bf16[192,2048]{1,0:T(8,128)(2,1)} %collective-permute-done.14.refs_2_.refs_11_), channel_id=1, source_target_pairs={{0,1},{1,0},{2,3},{3,2},{4,5},{5,4},{6,7},{7,6},{8,9},{9,8},{10,11... | collective-permute-start | bytes 2359304 | tf_op jit(solution)/shard_map/ppermute | solution.py:338
  81.6 55.9 %all-to-all-start = ((bf16[8,256,256]{2,1,0:T(8,128)(2,1)}), bf16[8,256,256]{2,1,0:T(8,128)(2,1)S(1)}, u32[]{:S(2)}, u32[]{:S(2)}) async-start(bf16[8,256,256]{2,1,0:T(8,128)(2,1)} %get-tuple-element.34), calls=%async_computation | async-start | bytes 2097152 | tf_op jit(solution)/shard_map/all_to_all | solution.py:395
  128.6 7.0 %collective-permute-start.21 = (bf16[2,256,512]{2,1,0:T(8,128)(2,1)}, bf16[2,256,512]{2,1,0:T(8,128)(2,1)S(1)}, u32[]{:S(2)}, u32[]{:S(2)}) collective-permute-start(bf16[2,256,512]{2,1,0:T(8,128)(2,1)} %get-tuple-element.30), channel_id=1, source_target_pairs={{0,1},{1,0},{2,3},{3,2},{4,5},{5,4},{6,7},{7,6},{8,9},{9,8},{10,11... | collective-permute-start | bytes 1572872 | tf_op jit(solution)/shard_map/ppermute | solution.py:338
  135.9 8.6 %collective-permute-start.22 = (bf16[256,512]{1,0:T(8,128)(2,1)S(1)}, bf16[256,512]{1,0:T(8,128)(2,1)S(1)}, u32[]{:S(2)}, u32[]{:S(2)}) collective-permute-start(bf16[256,512]{1,0:T(8,128)(2,1)S(1)} %fusion.2), channel_id=1, source_target_pairs={{0,2},{2,0},{1,3},{3,1},{4,6},{6,4},{5,7},{7,5},{8,10},{10,8},{9,1... | collective-permute-start | bytes 786440 | tf_op jit(solution)/shard_map/ppermute | solution.py:338
  (19 other events, 361.9 us)

commit v3 on v2

--- a/solution.py
+++ b/solution.py
@@ -36,6 +36,7 @@
 
 
 SPLIT = 4
+ROWS = 2
 
 
 def load_pieces(parts, piece, held, sems):
@@ -70,6 +71,26 @@
         copies += load_pieces(group, size, to, sems.at[pl.ds(at // piece, rows // size)])
         at += rows
     return copies
+
+
+def join_kernel(*refs):
+    at = 0
+    for part in refs[:-1]:
+        refs[-1][at : at + part.shape[0]] = part[...]
+        at += part.shape[0]
+
+
+def join(parts):
+    rows = sum(p.shape[0] for p in parts)
+    cols = parts[0].shape[1]
+    return pl.pallas_call(
+        join_kernel,
+        out_shape=jax.ShapeDtypeStruct((rows, cols), parts[0].dtype),
+        in_specs=[VMEM] * len(parts),
+        out_specs=VMEM,
+        cost_estimate=pl.CostEstimate(flops=0, bytes_accessed=4 * rows * cols, transcendentals=0),
+        name="join",
+    )(*parts)
 
 
 def cut(parts, counts):
@@ -153,7 +174,8 @@
     )(jnp.stack([quarter, chunk]), grad_y, w_out)
 
 
-def attention_kernel(n_qkv, g_places, n_late, piece, tok, cols_ref, count_ref, home_ref, place_ref, *refs):
+def attention_kernel(n_qkv, g_places, late_counts, piece, tok, cols_ref, count_ref, home_ref, place_ref, *refs):
+    n_late = sum(late_counts)
     refs, late = refs[n_late:], refs[:n_late]
     n_g = len(g_places)
     qkv_parts, g_parts = refs[:n_qkv], refs[n_qkv : n_qkv + n_g]
@@ -168,7 +190,7 @@
             to = g_ref.at[pl.ds(at * tok, tok)]
             copies.append(pltpu.make_async_copy(part.at[pl.ds(i * tok, tok)], to, g_sems.at[at]))
     weights = load_weights(w_ref, w_held, w_sems)
-    late_copies = load_pieces(late, piece, held, late_sems)
+    late_copies = load_groups(cut(late, late_counts), piece, held, late_sems)
     for copy in late_copies + weights + copies:
         copy.start()
     dk_ref[...] = jnp.zeros_like(dk_ref)
@@ -184,37 +206,44 @@
     for copy in copies:
         copy.wait()
 
-    def row(r, carry):
-        rows = pl.ds(pl.multiple_of(r * BLOCK, BLOCK), BLOCK)
-        at = [pl.ds(pl.multiple_of(cols_ref[r, s] * BLOCK, BLOCK), BLOCK) for s in range(slots)]
-        live = count_ref[r]
-        home = pl.ds(pl.multiple_of(home_ref[r] * BLOCK, BLOCK), BLOCK)
-        for h in range(heads):
-            lanes = slice(h * HEAD, (h + 1) * HEAD)
-            q = qkv_ref[0, rows, lanes]
-            g = g_ref[rows, lanes]
-            k = jnp.concatenate([qkv_ref[1, a, lanes] for a in at], axis=0)
-            v = jnp.concatenate([qkv_ref[2, a, lanes] for a in at], axis=0)
-            s = dot(k, q, ((1,), (1,))) * scale
-            slot_of = lax.broadcasted_iota(jnp.int32, s.shape, 0) // BLOCK
-            s = jnp.where(slot_of < live, s, NEG_FILL)
-            e = jnp.exp(s - jnp.max(s, axis=0, keepdims=True))
-            p = e * (1.0 / jnp.sum(e, axis=0, keepdims=True))
-            p16 = p.astype(BF16)
-            att_ref[home, lanes] = dot(p16, v, ((0,), (0,))).astype(BF16)
-            dp = dot(v, g, ((1,), (1,)))
-            delta = jnp.sum(p * dp, axis=0, keepdims=True)
-            ds16 = (p * (dp - delta)).astype(BF16)
-            grads_ref[0, rows, lanes] = (dot(ds16, k, ((0,), (0,))) * scale).astype(BF16)
-            dk = dot(ds16, q, ((1,), (0,)))
-            dv = dot(p16, g, ((1,), (0,)))
+    def some_rows(step, carry):
+        units = []
+        for i in range(ROWS):
+            r = step * ROWS + i
+            rows = pl.ds(pl.multiple_of(r * BLOCK, BLOCK), BLOCK)
+            at = [pl.ds(pl.multiple_of(cols_ref[r, s] * BLOCK, BLOCK), BLOCK) for s in range(slots)]
+            home = pl.ds(pl.multiple_of(home_ref[r] * BLOCK, BLOCK), BLOCK)
+            for h in range(heads):
+                units.append((rows, at, home, count_ref[r], slice(h * HEAD, (h + 1) * HEAD)))
+        q = [qkv_ref[0, rows, lane] for rows, _, _, _, lane in units]
+        g = [g_ref[rows, lane] for rows, _, _, _, lane in units]
+        k = [jnp.concatenate([qkv_ref[1, a, lane] for a in at], axis=0) for _, at, _, _, lane in units]
+        v = [jnp.concatenate([qkv_ref[2, a, lane] for a in at], axis=0) for _, at, _, _, lane in units]
+        s = [dot(a, b, ((1,), (1,))) * scale for a, b in zip(k, q)]
+        dp = [dot(a, b, ((1,), (1,))) for a, b in zip(v, g)]
+        slot_of = lax.broadcasted_iota(jnp.int32, s[0].shape, 0) // BLOCK
+        p, p16, ds16 = [], [], []
+        for u, unit in enumerate(units):
+            kept = jnp.where(slot_of < unit[3], s[u], NEG_FILL)
+            e = jnp.exp(kept - jnp.max(kept, axis=0, keepdims=True))
+            p.append(e * (1.0 / jnp.sum(e, axis=0, keepdims=True)))
+            p16.append(p[u].astype(BF16))
+        for u in range(len(units)):
+            delta = jnp.sum(p[u] * dp[u], axis=0, keepdims=True)
+            ds16.append((p[u] * (dp[u] - delta)).astype(BF16))
+        for u, (rows, _, home, _, lane) in enumerate(units):
+            att_ref[home, lane] = dot(p16[u], v[u], ((0,), (0,))).astype(BF16)
+            grads_ref[0, rows, lane] = (dot(ds16[u], k[u], ((0,), (0,))) * scale).astype(BF16)
+        for u, (_, at, _, _, lane) in enumerate(units):
+            dk = dot(ds16[u], q[u], ((1,), (0,)))
+            dv = dot(p16[u], g[u], ((1,), (0,)))
             for i, a in enumerate(at):
                 part = slice(i * BLOCK, (i + 1) * BLOCK)
-                dk_ref[a, lanes] += dk[part]
-                dv_ref[a, lanes] += dv[part]
+                dk_ref[a, lane] += dk[part]
+                dv_ref[a, lane] += dv[part]
         return carry
 
-    lax.fori_loop(0, row_blocks, row, 0)
+    lax.fori_loop(0, row_blocks // ROWS, some_rows, 0)
     stores = [pltpu.make_async_copy(grads_ref.at[c], grads_out.at[c], out_sems.at[c]) for c in range(3)]
     stores[0].start()
     grads_ref[1] = (dk_ref[...] * scale).astype(BF16)
@@ -240,10 +269,12 @@
     tokens = sum(p.shape[0] for p in g_parts)
     width = g_parts[0].shape[1]
     n_qkv, n_g = len(qkv_parts), len(g_parts)
+    late_counts = [len(group) for group in late]
+    late = [p for group in late for p in group]
     n_late, late_rows = len(late), sum(p.shape[0] for p in late)
     n_sent = places.shape[0] - n_kept
     return pl.pallas_call(
-        functools.partial(attention_kernel, n_qkv, g_places, n_late, piece, tok),
+        functools.partial(attention_kernel, n_qkv, g_places, late_counts, piece, tok),
         out_shape=(
             jax.ShapeDtypeStruct((3, tokens, width), BF16),
             jax.ShapeDtypeStruct((tokens, width), BF16),
@@ -358,38 +389,34 @@
     got[1] = swap(own, "x", 1)
     got[3] = swap(after(got[2], got[1], g_own), "x", 1)
     last_x = got[3]
-    for k in range(2, nz - 1):
+    for k in range(2, nz):
         got[2 * k + 1] = last_x = swap(after(got[2 * k], last_x), "x", 1)
-    got[2 * nz - 1] = swap(got[2 * nz - 3], "z", 1)
-
-    groups = [[tokens_in]]
-    behind, qkv_parts = [], []
+
+    g_x = swap(after(g_sent, last_x), "x", 1)
+    g_z = {}
+    for k in range(1, nz):
+        low = k & -k
+        g_z[k] = swap(after(g_sent, got[4]) if k == low else g_z[k ^ low], "z", low)
+    g_far = [g_z[k] for k in range(1, nz)]
+    g_far.append(swap(after(join(g_far), g_x), "x", 1))
+    g_parts = [g_own, g_x] + g_far
+    places = [[0], [1]] + [[2 * k] for k in range(1, nz)] + [[2 * k + 1 for k in range(1, nz)]]
+    g_places = [[order.index(k) for k in part] for part in places]
+
+    groups, behind, qkv_parts = [[tokens_in]], [], []
     for at, batch in enumerate(batches):
-        mine = jnp.concatenate([got[k] for k in batch], axis=0)
+        first = after(got[batch[0]], *qkv_parts) if at == 2 else got[batch[0]]
+        mine = join([first] + [got[k] for k in batch[1:]])
         ys = [mine] + [swap(after(mine, *behind), "y", i) for i in range(1, ny)]
         behind = ys[1:]
         parts = []
         for i, a in enumerate(ys):
-            core = after(a, *qkv_parts) if i == 0 else a
+            core = after(a, *ys[1:]) if i == 0 else a
             parts += [a] + [swap(core, "c", j) for j in range(1, nc)]
         groups.append(parts)
-        if at == 1:
+        if at == 0:
             qkv_parts = [project(groups, piece, w_qkv)]
-    late = groups[-1]
-
-    g = {0: g_own, 1: swap(after(g_sent, last_x), "x", 1)}
-    g_late = after(g_sent, got[2 * nz - 1])
-    for k in range(1, nz):
-        along_z(g, g_late, k)
-    g_far = [g[2 * k] for k in range(1, nz)]
-    g_x = swap(after(jnp.concatenate(g_far, axis=0), g[1]), "x", 1)
-    g_parts = [g_own, g[1]] + g_far + [g_x]
-    g_places, at = [], 0
-    g_order = [0, 1] + [2 * k for k in range(1, nz)] + [2 * k + 1 for k in range(1, nz)]
-    for part in g_parts:
-        n = part.shape[0] // tok
-        g_places.append([order.index(k) for k in g_order[at : at + n]])
-        at += n
+    late = groups[2:]
 
     y_sent = after(y_sent, *g_far)
     y_all = lax.all_to_all(y_sent, ("z", "x"), 0, 0, tiled=True).reshape(chunks * tok, out_cols)
@@ -413,14 +440,15 @@
     grads, att, sent, half = attention(
         cols, count, home, places, ny, late, piece, qkv_parts, g_parts, g_places, w_qkv, tok, width // pieces
     )
+    grad_out = dot(att, y_all, ((0,), (0,))).astype(BF16)
+    half = after(half, grad_out)
     for j in range(1, nc):
         half = half + swap(sent[(j - 1) * ny : j * ny], "c", j).astype(F32)
     grad_x = half[0]
     for k in range(1, ny):
         grad_x = grad_x + swap(half[k].astype(BF16), "y", k).astype(F32)
 
-    grad_qkv = weight_grad(chunk.reshape(1), groups, piece, grads, out_cols)
-    grad_out = dot(att, y_all, ((0,), (0,))).astype(BF16)
+    grad_qkv = weight_grad(chunk.reshape(1), groups, piece, after(grads, half), out_cols)
     return (grad_x.astype(BF16), grad_qkv, grad_out)
 
 

time: 146 us -> 133 us (0.911)
  Pallas kernels: 61.9 us -> 54.6 us
  waiting for transfers between devices: 33.1 us -> 39.4 us
  local copies, waits for them, and re-layouts: 13.4 us -> 7.97 us
  starting transfers between devices: 26.9 us -> 23.3 us
  other arithmetic: 5.84 us -> 3.77 us
    ppermute x23, waiting for transfers between devices: 33.1 us -> 39.4 us  [swap(): return lax.ppermute(a, axis, [(i, i ^ k) for i in range(n)])]
    ppermute x23, starting transfers between devices: 23.1 us -> 19 us  [swap(): return lax.ppermute(a, axis, [(i, i ^ k) for i in range(n)])]
    unnamed x42 -> x46, local copies, waits for them, and re-layouts: 9.62 us -> 5.89 us
    pallas_call x1 -> x5, Pallas kernels: 42.1 us -> 38.5 us  [the longest x1 30.7 us: attention(): pl.pallas_call(functools.partial(attention_kernel, n_qkv, g_places, late_...]
    pallas_call x1, Pallas kernels: 9.19 us -> 5.72 us  [project(): pl.pallas_call(functools.partial(project_kernel, counts, piece, tok), gri...]
    concatenate x1 -> x0, other arithmetic: 1.98 us -> none  [local(): g_x = swap(after(jnp.concatenate(g_far, axis=0), g[1]), 'x', 1)]
    concatenate x3 -> x0, local copies, waits for them, and re-layouts: 1.69 us -> none  [local(): mine = jnp.concatenate([got[k] for k in batch], axis=0)]
  transfers between devices with their start and end apart: 24 -> 24, of which waited for: 9 -> 12; matrix products, arithmetic and copies ran while one was open for 10% -> 5% of each run, Pallas kernels for 43% -> 41%
where the time goes in v3:
time: 133 us
  Pallas kernels  54.6 us (41%)
  waiting for transfers between devices  39.4 us (30%)
  starting transfers between devices  23.3 us (18%)
  local copies, waits for them, and re-layouts  7.97 us (6%)
  other arithmetic  3.77 us (3%)
  matrix products  3.15 us (2%)
    ppermute x23, waiting for transfers between devices, swap(): return lax.ppermute(a, axis, [(i, i ^ k) for i in range(n)])  39.4 us
    pallas_call x1, Pallas kernels, attention(): pl.pallas_call(functools.partial(attention_kernel, n_qkv, g_places, late_...  30.7 us
    ppermute x23, starting transfers between devices, swap(): return lax.ppermute(a, axis, [(i, i ^ k) for i in range(n)])  19 us
    pallas_call x4, Pallas kernels, join(): pl.pallas_call(join_kernel, out_shape=jax.ShapeDtypeStruct((rows, cols),...  7.82 us
    pallas_call x1, Pallas kernels, weight_grad(): pl.pallas_call(functools.partial(weight_grad_kernel, counts, piece), in_s...  6.6 us
    unnamed x46, local copies, waits for them, and re-layouts  5.89 us
    pallas_call x1, Pallas kernels, project(): pl.pallas_call(functools.partial(project_kernel, counts, piece, tok), gri...  5.72 us
    all_to_all x1, starting transfers between devices, local(): lax.all_to_all(y_sent, ('z', 'x'), 0, 0, tiled=True)  4.21 us
  transfers between devices with their start and end apart: 24, of which 12 were waited for; matrix products, arithmetic and copies ran while one was open for 5% of the time, Pallas kernels for 41%

profile of v3, /device:TPU:0, one launch (start us, length us, event | category | flops | bytes accessed | tf_op | source)
XLA Modules:
  0.0 133.0 jit_solution(6946793678026403834)
XLA Ops:
  1.6 3.0 %collective-permute-start.2 = (bf16[64,2048]{1,0:T(8,128)(2,1)S(1)}, bf16[64,2048]{1,0:T(8,128)(2,1)S(1)}, u32[]{:S(2)}, u32[]{:S(2)}) collective-permute-start(bf16[64,2048]{1,0:T(8,128)(2,1)S(1)} %constant_dynamic-slice_fusion), channel_id=1, source_target_pairs={{0,4},{4,0},{1,5},{5,1},{2,6},{6,2},{3,7},{7,3},{8,12},{12,8},{9,1... | collective-permute-start | bytes 786440 | tf_op jit(solution)/shard_map/ppermute | solution.py:369
  4.6 1.6 %collective-permute-start.1 = (bf16[64,2048]{1,0:T(8,128)(2,1)S(1)}, bf16[64,2048]{1,0:T(8,128)(2,1)S(1)}, u32[]{:S(2)}, u32[]{:S(2)}) collective-permute-start(bf16[64,2048]{1,0:T(8,128)(2,1)S(1)} %constant_dynamic-slice_fusion), channel_id=1, source_target_pairs={{0,8},{8,0},{16,24},{24,16},{1,9},{9,1},{17,25},{25,17},{2,10},{10... | collective-permute-start | bytes 786440 | tf_op jit(solution)/shard_map/ppermute | solution.py:369
  6.2 2.6 %collective-permute-start = (bf16[64,2048]{1,0:T(8,128)(2,1)S(1)}, bf16[64,2048]{1,0:T(8,128)(2,1)S(1)}, u32[]{:S(2)}, u32[]{:S(2)}) collective-permute-start(bf16[64,2048]{1,0:T(8,128)(2,1)S(1)} %constant_dynamic-slice_fusion), channel_id=1, source_target_pairs={{0,16},{8,24},{16,0},{24,8},{1,17},{9,25},{17,1},{25,9},{2,18},{10... | collective-permute-start | bytes 786440 | tf_op jit(solution)/shard_map/ppermute | solution.py:369
  9.4 3.8 %cotangent.1 = (bf16[256,512]{1,0:T(8,128)(2,1)}, bf16[256,512]{1,0:T(8,128)(2,1)}, bf16[8,256,256]{2,1,0:T(8,128)(2,1)}) custom-call(s32[2]{0:T(128)} %pad_add_fusion.1.at_ref, bf16[256,2048]{1,0:T(8,128)(2,1)} %grad_y_ref.1, bf16[512,2048]{1,0:T(8,128)(2,1)} %w_ref.1), custom_call_target="tpu_custom_call" | custom-call | flops 536870912 | bytes 4194304 | tf_op jit(solution)/shard_map/cotangent/pallas_call | solution.py:160
  13.2 4.7 %collective-permute-done.1.refs_1_ = bf16[64,2048]{1,0:T(8,128)(2,1)S(1)} collective-permute-done((bf16[64,2048]{1,0:T(8,128)(2,1)S(1)}, bf16[64,2048]{1,0:T(8,128)(2,1)S(1)}, u32[]{:S(2)}, u32[]{:S(2)}) %collective-permute-start.1) | collective-permute-done | bytes 262176 | tf_op jit(solution)/shard_map/ppermute | solution.py:369
  18.6 1.8 %join.5.refs_1_ = bf16[128,2048]{1,0:T(8,128)(2,1)} custom-call(bf16[64,2048]{1,0:T(8,128)(2,1)} %copy-done.18, bf16[64,2048]{1,0:T(8,128)(2,1)} %copy-done.17), custom_call_target="tpu_custom_call" | custom-call | bytes 1048576 | tf_op jit(solution)/shard_map/join/pallas_call | solution.py:86
  22.0 2.8 %collective-permute-done.3.refs_1_ = bf16[64,2048]{1,0:T(8,128)(2,1)S(1)} collective-permute-done((bf16[64,2048]{1,0:T(8,128)(2,1)S(1)}, bf16[64,2048]{1,0:T(8,128)(2,1)S(1)}, u32[]{:S(2)}, u32[]{:S(2)}) %collective-permute-start.3) | collective-permute-done | bytes 262176 | tf_op jit(solution)/shard_map/ppermute | solution.py:369
  26.3 4.3 %collective-permute-done.8.refs_0_ = bf16[64,2048]{1,0:T(8,128)(2,1)S(1)} collective-permute-done((bf16[64,2048]{1,0:T(8,128)(2,1)S(1)}, bf16[64,2048]{1,0:T(8,128)(2,1)S(1)}, u32[]{:S(2)}, u32[]{:S(2)}) %collective-permute-start.8) | collective-permute-done | bytes 262176 | tf_op jit(solution)/shard_map/ppermute | solution.py:369
  33.6 4.6 %collective-permute-done.18.refs_1_.refs_12_ = bf16[256,512]{1,0:T(8,128)(2,1)S(1)} collective-permute-done((bf16[256,512]{1,0:T(8,128)(2,1)}, bf16[256,512]{1,0:T(8,128)(2,1)S(1)}, u32[]{:S(2)}, u32[]{:S(2)}) %collective-permute-start.18) | collective-permute-done | bytes 262176 | tf_op jit(solution)/shard_map/ppermute | solution.py:369
  40.0 1.8 %join.4.refs_0_.refs_5_ = bf16[128,2048]{1,0:T(8,128)(2,1)} custom-call(bf16[64,2048]{1,0:T(8,128)(2,1)} %copy-done.12, bf16[64,2048]{1,0:T(8,128)(2,1)} %copy-done.15), custom_call_target="tpu_custom_call" | custom-call | bytes 1048576 | tf_op jit(solution)/shard_map/join/pallas_call | solution.py:86
  41.9 2.1 %collective-permute-done.17.refs_0_.refs_11_ = bf16[256,512]{1,0:T(8,128)(2,1)} collective-permute-done((bf16[256,512]{1,0:T(8,128)(2,1)}, bf16[256,512]{1,0:T(8,128)(2,1)}, u32[]{:S(2)}, u32[]{:S(2)}) %collective-permute-start.17) | collective-permute-done | bytes 262176 | tf_op jit(solution)/shard_map/ppermute | solution.py:369
  45.0 4.5 %collective-permute-done.19.refs_2_.refs_13_ = bf16[256,512]{1,0:T(8,128)(2,1)} collective-permute-done((bf16[256,512]{1,0:T(8,128)(2,1)S(1)}, bf16[256,512]{1,0:T(8,128)(2,1)}, u32[]{:S(2)}, u32[]{:S(2)}) %collective-permute-start.19) | collective-permute-done | bytes 262176 | tf_op jit(solution)/shard_map/ppermute | solution.py:369
  49.5 2.1 %join.7 = bf16[768,512]{1,0:T(8,128)(2,1)} custom-call(bf16[256,512]{1,0:T(8,128)(2,1)} %collective-permute-done.17.refs_0_.refs_11_, bf16[256,512]{1,0:T(8,128)(2,1)} %copy-done.11, bf16[256,512]{1,0:T(8,128)(2,1)} %collective-permute-done.19.refs_2_.refs_13_), custom_call_target="tpu_custom_call" | custom-call | bytes 1572864 | tf_op jit(solution)/shard_map/join/pallas_call | solution.py:86
  52.6 3.0 %copy-done.5 = bf16[3,2048,512]{2,1,0:T(8,128)(2,1)S(1)} copy-done((bf16[3,2048,512]{2,1,0:T(8,128)(2,1)S(1)}, bf16[3,2048,512]{2,1,0:T(8,128)(2,1)}, u32[]{:S(2)}) %copy-start.5) | copy-done | bytes 6291480
  55.6 5.7 %project.1.refs_8_ = bf16[3,768,512]{2,1,0:T(8,128)(2,1)S(1)} custom-call(bf16[256,2048]{1,0:T(8,128)(2,1)S(1)} %copy-done.1, bf16[128,2048]{1,0:T(8,128)(2,1)S(1)} %copy-done, bf16[128,2048]{1,0:T(8,128)(2,1)S(1)} %collective-permute-done.9.refs_2_, bf16[128,2048]{1,0:T(8,128)(2,1)S(1)} %collective-permute-done.4.refs_3_, ...), custom_call_target="tpu_custom_call" | custom-call | flops 4831838208 | bytes 11796480 | tf_op jit(solution)/shard_map/project/pallas_call | solution.py:127
  62.8 2.1 %join.6.refs_4_.refs_9_ = bf16[192,2048]{1,0:T(8,128)(2,1)} custom-call(bf16[64,2048]{1,0:T(8,128)(2,1)} %copy-done.13, bf16[64,2048]{1,0:T(8,128)(2,1)} %copy-done.14, bf16[64,2048]{1,0:T(8,128)(2,1)} %copy-done.16), custom_call_target="tpu_custom_call" | custom-call | bytes 1572864 | tf_op jit(solution)/shard_map/join/pallas_call | solution.py:86
  64.9 1.6 %collective-permute-start.13 = (bf16[192,2048]{1,0:T(8,128)(2,1)}, bf16[192,2048]{1,0:T(8,128)(2,1)S(1)}, u32[]{:S(2)}, u32[]{:S(2)}) collective-permute-start(bf16[192,2048]{1,0:T(8,128)(2,1)} %join.6.refs_4_.refs_9_), channel_id=1, source_target_pairs={{0,2},{2,0},{1,3},{3,1},{4,6},{6,4},{5,7},{7,5},{8,10},{10,8},{9,1... | collective-permute-start | bytes 2359304 | tf_op jit(solution)/shard_map/ppermute | solution.py:369
  67.4 4.0 %collective-permute-done.20.refs_14_ = bf16[768,512]{1,0:T(8,128)(2,1)} collective-permute-done((bf16[768,512]{1,0:T(8,128)(2,1)}, bf16[768,512]{1,0:T(8,128)(2,1)}, u32[]{:S(2)}, u32[]{:S(2)}) %collective-permute-start.20) | collective-permute-done | bytes 786464 | tf_op jit(solution)/shard_map/ppermute | solution.py:369
  71.3 4.2 %all-to-all-start = ((bf16[8,256,256]{2,1,0:T(8,128)(2,1)}), bf16[8,256,256]{2,1,0:T(8,128)(2,1)S(1)}, u32[]{:S(2)}, u32[]{:S(2)}) async-start(bf16[8,256,256]{2,1,0:T(8,128)(2,1)} %get-tuple-element.42), calls=%async_computation | async-start | bytes 2097152 | tf_op jit(solution)/shard_map/all_to_all | solution.py:422
  75.6 8.8 %collective-permute-done.13.refs_6_.refs_11_ = bf16[192,2048]{1,0:T(8,128)(2,1)S(1)} collective-permute-done((bf16[192,2048]{1,0:T(8,128)(2,1)}, bf16[192,2048]{1,0:T(8,128)(2,1)S(1)}, u32[]{:S(2)}, u32[]{:S(2)}) %collective-permute-start.13) | collective-permute-done | bytes 786464 | tf_op jit(solution)/shard_map/ppermute | solution.py:369
  89.4 30.7 %attention.1 = (bf16[3,2048,512]{2,1,0:T(8,128)(2,1)}, bf16[2048,512]{1,0:T(8,128)(2,1)}, bf16[2,256,512]{2,1,0:T(8,128)(2,1)}, f32[2,256,512]{2,1,0:T(8,128)}) custom-call(s32[16,2]{1,0:T(8,128)} %copy.12.cols_ref, s32[16]{0:T(128)} %select_reduce_fusion.2.count_ref, s32[16]{0:T(128)} %get-tuple-element.47.home_ref, s32[4]{0:T(128)} %pad_add_fusion.place_ref, ...), custom_call_target="tpu_custom_call" | custom-call | flops 10000000000 | bytes 31457280 | tf_op jit(solution)/shard_map/attention/pallas_call | solution.py:276
  120.3 3.1 %convolution_convert_fusion = bf16[512,256]{1,0:T(8,128)(2,1)} fusion(bf16[2048,512]{1,0:T(8,128)(2,1)} %get-tuple-element.40, bf16[2048,256]{1,0:T(8,128)(2,1)S(1)} %bitcast.13), kind=kOutput, calls=%fused_computation | convolution fusion | flops 537001984 | bytes 3407872 | tf_op jit(solution)/shard_map/dot_general | solution.py:25
  123.7 1.6 %collective-permute-start.22 = (bf16[256,512]{1,0:T(8,128)(2,1)S(1)}, bf16[256,512]{1,0:T(8,128)(2,1)S(1)}, u32[]{:S(2)}, u32[]{:S(2)}) collective-permute-start(bf16[256,512]{1,0:T(8,128)(2,1)S(1)} %fusion.2), channel_id=1, source_target_pairs={{0,2},{2,0},{1,3},{3,1},{4,6},{6,4},{5,7},{7,5},{8,10},{10,8},{9,1... | collective-permute-start | bytes 786440 | tf_op jit(solution)/shard_map/ppermute | solution.py:369
  125.3 6.6 %weight_grad.1 = bf16[3,256,512]{2,1,0:T(8,128)(2,1)} custom-call(s32[1]{0:T(128)} %bitcast.1.chunk_ref, bf16[256,2048]{1,0:T(8,128)(2,1)} %refs_0_.3, bf16[128,2048]{1,0:T(8,128)(2,1)} %join.5.refs_1_, bf16[128,2048]{1,0:T(8,128)(2,1)} %copy-done.3, bf16[128,2048]{1,0:T(8,128)(2,1)} %copy-done.2, bf16[128,2048]{1,0:T(8,128)(2,1)} %copy-done.4, ...), custom_call_target="tpu_custom_call" | custom-call | flops 1610612736 | bytes 6291456 | tf_op jit(solution)/shard_map/weight_grad/pallas_call | solution.py:335
  (100 shorter events, 21.2 us)
Async XLA Ops:
  1.6 11.6 %collective-permute-start.2 = (bf16[64,2048]{1,0:T(8,128)(2,1)S(1)}, bf16[64,2048]{1,0:T(8,128)(2,1)S(1)}, u32[]{:S(2)}, u32[]{:S(2)}) collective-permute-start(bf16[64,2048]{1,0:T(8,128)(2,1)S(1)} %constant_dynamic-slice_fusion), channel_id=1, source_target_pairs={{0,4},{4,0},{1,5},{5,1},{2,6},{6,2},{3,7},{7,3},{8,12},{12,8},{9,1... | collective-permute-start | bytes 786440 | tf_op jit(solution)/shard_map/ppermute | solution.py:369
  4.6 13.3 %collective-permute-start.1 = (bf16[64,2048]{1,0:T(8,128)(2,1)S(1)}, bf16[64,2048]{1,0:T(8,128)(2,1)S(1)}, u32[]{:S(2)}, u32[]{:S(2)}) collective-permute-start(bf16[64,2048]{1,0:T(8,128)(2,1)S(1)} %constant_dynamic-slice_fusion), channel_id=1, source_target_pairs={{0,8},{8,0},{16,24},{24,16},{1,9},{9,1},{17,25},{25,17},{2,10},{10... | collective-permute-start | bytes 786440 | tf_op jit(solution)/shard_map/ppermute | solution.py:369
  6.2 15.8 %collective-permute-start = (bf16[64,2048]{1,0:T(8,128)(2,1)S(1)}, bf16[64,2048]{1,0:T(8,128)(2,1)S(1)}, u32[]{:S(2)}, u32[]{:S(2)}) collective-permute-start(bf16[64,2048]{1,0:T(8,128)(2,1)S(1)} %constant_dynamic-slice_fusion), channel_id=1, source_target_pairs={{0,16},{8,24},{16,0},{24,8},{1,17},{9,25},{17,1},{25,9},{2,18},{10... | collective-permute-start | bytes 786440 | tf_op jit(solution)/shard_map/ppermute | solution.py:369
  17.9 6.9 %collective-permute-start.3 = (bf16[64,2048]{1,0:T(8,128)(2,1)S(1)}, bf16[64,2048]{1,0:T(8,128)(2,1)S(1)}, u32[]{:S(2)}, u32[]{:S(2)}) collective-permute-start(bf16[64,2048]{1,0:T(8,128)(2,1)S(1)} %collective-permute-done.1.refs_1_), channel_id=1, source_target_pairs={{0,4},{4,0},{1,5},{5,1},{2,6},{6,2},{3,7},{7,3},{8,12},{12,8},{9,1... | collective-permute-start | bytes 786440 | tf_op jit(solution)/shard_map/ppermute | solution.py:369
  20.4 12.7 %collective-permute-start.4 = (bf16[128,2048]{1,0:T(8,128)(2,1)}, bf16[128,2048]{1,0:T(8,128)(2,1)S(1)}, u32[]{:S(2)}, u32[]{:S(2)}) collective-permute-start(bf16[128,2048]{1,0:T(8,128)(2,1)} %join.5.refs_1_), channel_id=1, source_target_pairs={{0,2},{2,0},{1,3},{3,1},{4,6},{6,4},{5,7},{7,5},{8,10},{10,8},{9,1... | collective-permute-start | bytes 1572872 | tf_op jit(solution)/shard_map/ppermute | solution.py:369
  22.0 8.7 %collective-permute-start.8 = (bf16[64,2048]{1,0:T(8,128)(2,1)S(1)}, bf16[64,2048]{1,0:T(8,128)(2,1)S(1)}, u32[]{:S(2)}, u32[]{:S(2)}) collective-permute-start(bf16[64,2048]{1,0:T(8,128)(2,1)S(1)} %collective-permute-done.refs_0_), channel_id=1, source_target_pairs={{0,8},{8,0},{16,24},{24,16},{1,9},{9,1},{17,25},{25,17},{2,10},{10... | collective-permute-start | bytes 786440 | tf_op jit(solution)/shard_map/ppermute | solution.py:369
  24.7 6.8 %collective-permute-start.11 = (bf16[64,2048]{1,0:T(8,128)(2,1)S(1)}, bf16[64,2048]{1,0:T(8,128)(2,1)S(1)}, u32[]{:S(2)}, u32[]{:S(2)}) collective-permute-start(bf16[64,2048]{1,0:T(8,128)(2,1)S(1)} %collective-permute-done.refs_0_), channel_id=1, source_target_pairs={{0,4},{4,0},{1,5},{5,1},{2,6},{6,2},{3,7},{7,3},{8,12},{12,8},{9,1... | collective-permute-start | bytes 786440 | tf_op jit(solution)/shard_map/ppermute | solution.py:369
  25.4 12.8 %collective-permute-start.18 = (bf16[256,512]{1,0:T(8,128)(2,1)}, bf16[256,512]{1,0:T(8,128)(2,1)S(1)}, u32[]{:S(2)}, u32[]{:S(2)}) collective-permute-start(bf16[256,512]{1,0:T(8,128)(2,1)} %get-tuple-element.37), channel_id=1, source_target_pairs={{0,16},{8,24},{16,0},{24,8},{1,17},{9,25},{17,1},{25,9},{2,18},{10... | collective-permute-start | bytes 786440 | tf_op jit(solution)/shard_map/ppermute | solution.py:369
  31.6 6.7 %collective-permute-start.12 = (bf16[64,2048]{1,0:T(8,128)(2,1)S(1)}, bf16[64,2048]{1,0:T(8,128)(2,1)S(1)}, u32[]{:S(2)}, u32[]{:S(2)}) collective-permute-start(bf16[64,2048]{1,0:T(8,128)(2,1)S(1)} %collective-permute-done.8.refs_0_), channel_id=1, source_target_pairs={{0,4},{4,0},{1,5},{5,1},{2,6},{6,2},{3,7},{7,3},{8,12},{12,8},{9,1... | collective-permute-start | bytes 786440 | tf_op jit(solution)/shard_map/ppermute | solution.py:369
  33.1 19.4 %collective-permute-start.9 = (bf16[128,2048]{1,0:T(8,128)(2,1)}, bf16[128,2048]{1,0:T(8,128)(2,1)S(1)}, u32[]{:S(2)}, u32[]{:S(2)}) collective-permute-start(bf16[128,2048]{1,0:T(8,128)(2,1)} %join.5.refs_1_), channel_id=1, source_target_pairs={{0,1},{1,0},{2,3},{3,2},{4,5},{5,4},{6,7},{7,6},{8,9},{9,8},{10,11... | collective-permute-start | bytes 1572872 | tf_op jit(solution)/shard_map/ppermute | solution.py:369
  33.1 19.4 %collective-permute-start.10 = (bf16[128,2048]{1,0:T(8,128)(2,1)S(1)}, bf16[128,2048]{1,0:T(8,128)(2,1)S(1)}, u32[]{:S(2)}, u32[]{:S(2)}) collective-permute-start(bf16[128,2048]{1,0:T(8,128)(2,1)S(1)} %collective-permute-done.4.refs_3_), channel_id=1, source_target_pairs={{0,1},{1,0},{2,3},{3,2},{4,5},{5,4},{6,7},{7,6},{8,9},{9,8},{10,11... | collective-permute-start | bytes 1572872 | tf_op jit(solution)/shard_map/ppermute | solution.py:369
  33.6 10.3 %collective-permute-start.17 = (bf16[256,512]{1,0:T(8,128)(2,1)}, bf16[256,512]{1,0:T(8,128)(2,1)}, u32[]{:S(2)}, u32[]{:S(2)}) collective-permute-start(bf16[256,512]{1,0:T(8,128)(2,1)} %get-tuple-element.37), channel_id=1, source_target_pairs={{0,8},{8,0},{16,24},{24,16},{1,9},{9,1},{17,25},{25,17},{2,10},{10... | collective-permute-start | bytes 786440 | tf_op jit(solution)/shard_map/ppermute | solution.py:369
  38.2 11.2 %collective-permute-start.19 = (bf16[256,512]{1,0:T(8,128)(2,1)S(1)}, bf16[256,512]{1,0:T(8,128)(2,1)}, u32[]{:S(2)}, u32[]{:S(2)}) collective-permute-start(bf16[256,512]{1,0:T(8,128)(2,1)S(1)} %collective-permute-done.18.refs_1_.refs_12_), channel_id=1, source_target_pairs={{0,8},{8,0},{16,24},{24,16},{1,9},{9,1},{17,25},{25,17},{2,10},{10... | collective-permute-start | bytes 786440 | tf_op jit(solution)/shard_map/ppermute | solution.py:369
  39.0 12.5 %collective-permute-start.16 = (bf16[256,512]{1,0:T(8,128)(2,1)}, bf16[256,512]{1,0:T(8,128)(2,1)}, u32[]{:S(2)}, u32[]{:S(2)}) collective-permute-start(bf16[256,512]{1,0:T(8,128)(2,1)} %get-tuple-element.37), channel_id=1, source_target_pairs={{0,4},{4,0},{1,5},{5,1},{2,6},{6,2},{3,7},{7,3},{8,12},{12,8},{9,1... | collective-permute-start | bytes 786440 | tf_op jit(solution)/shard_map/ppermute | solution.py:369
  43.9 20.9 %collective-permute-start.5 = (bf16[128,2048]{1,0:T(8,128)(2,1)}, bf16[128,2048]{1,0:T(8,128)(2,1)}, u32[]{:S(2)}, u32[]{:S(2)}) collective-permute-start(bf16[128,2048]{1,0:T(8,128)(2,1)} %join.4.refs_0_.refs_5_), channel_id=1, source_target_pairs={{0,2},{2,0},{1,3},{3,1},{4,6},{6,4},{5,7},{7,5},{8,10},{10,8},{9,1... | collective-permute-start | bytes 1572872 | tf_op jit(solution)/shard_map/ppermute | solution.py:369
  51.6 19.8 %collective-permute-start.20 = (bf16[768,512]{1,0:T(8,128)(2,1)}, bf16[768,512]{1,0:T(8,128)(2,1)}, u32[]{:S(2)}, u32[]{:S(2)}) collective-permute-start(bf16[768,512]{1,0:T(8,128)(2,1)} %join.7), channel_id=1, source_target_pairs={{0,4},{4,0},{1,5},{5,1},{2,6},{6,2},{3,7},{7,3},{8,12},{12,8},{9,1... | collective-permute-start | bytes 2359304 | tf_op jit(solution)/shard_map/ppermute | solution.py:369
  64.9 19.5 %collective-permute-start.13 = (bf16[192,2048]{1,0:T(8,128)(2,1)}, bf16[192,2048]{1,0:T(8,128)(2,1)S(1)}, u32[]{:S(2)}, u32[]{:S(2)}) collective-permute-start(bf16[192,2048]{1,0:T(8,128)(2,1)} %join.6.refs_4_.refs_9_), channel_id=1, source_target_pairs={{0,2},{2,0},{1,3},{3,1},{4,6},{6,4},{5,7},{7,5},{8,10},{10,8},{9,1... | collective-permute-start | bytes 2359304 | tf_op jit(solution)/shard_map/ppermute | solution.py:369
  71.3 49.0 %all-to-all-start = ((bf16[8,256,256]{2,1,0:T(8,128)(2,1)}), bf16[8,256,256]{2,1,0:T(8,128)(2,1)S(1)}, u32[]{:S(2)}, u32[]{:S(2)}) async-start(bf16[8,256,256]{2,1,0:T(8,128)(2,1)} %get-tuple-element.42), calls=%async_computation | async-start | bytes 2097152 | tf_op jit(solution)/shard_map/all_to_all | solution.py:422
  84.3 5.0 %collective-permute-start.14 = (bf16[192,2048]{1,0:T(8,128)(2,1)S(1)}, bf16[192,2048]{1,0:T(8,128)(2,1)}, u32[]{:S(2)}, u32[]{:S(2)}) collective-permute-start(bf16[192,2048]{1,0:T(8,128)(2,1)S(1)} %copy-done.7), channel_id=1, source_target_pairs={{0,1},{1,0},{2,3},{3,2},{4,5},{5,4},{6,7},{7,6},{8,9},{9,8},{10,11... | collective-permute-start | bytes 2359304 | tf_op jit(solution)/shard_map/ppermute | solution.py:369
  84.3 5.0 %collective-permute-start.15 = (bf16[192,2048]{1,0:T(8,128)(2,1)S(1)}, bf16[192,2048]{1,0:T(8,128)(2,1)}, u32[]{:S(2)}, u32[]{:S(2)}) collective-permute-start(bf16[192,2048]{1,0:T(8,128)(2,1)S(1)} %collective-permute-done.13.refs_6_.refs_11_), channel_id=1, source_target_pairs={{0,1},{1,0},{2,3},{3,2},{4,5},{5,4},{6,7},{7,6},{8,9},{9,8},{10,11... | collective-permute-start | bytes 2359304 | tf_op jit(solution)/shard_map/ppermute | solution.py:369
  84.9 4.5 %collective-permute-start.6 = (bf16[128,2048]{1,0:T(8,128)(2,1)S(1)}, bf16[128,2048]{1,0:T(8,128)(2,1)}, u32[]{:S(2)}, u32[]{:S(2)}) collective-permute-start(bf16[128,2048]{1,0:T(8,128)(2,1)S(1)} %copy-done.8), channel_id=1, source_target_pairs={{0,1},{1,0},{2,3},{3,2},{4,5},{5,4},{6,7},{7,6},{8,9},{9,8},{10,11... | collective-permute-start | bytes 1572872 | tf_op jit(solution)/shard_map/ppermute | solution.py:369
  85.0 4.4 %collective-permute-start.7 = (bf16[128,2048]{1,0:T(8,128)(2,1)}, bf16[128,2048]{1,0:T(8,128)(2,1)}, u32[]{:S(2)}, u32[]{:S(2)}) collective-permute-start(bf16[128,2048]{1,0:T(8,128)(2,1)} %collective-permute-done.5.refs_2_.refs_7_), channel_id=1, source_target_pairs={{0,1},{1,0},{2,3},{3,2},{4,5},{5,4},{6,7},{7,6},{8,9},{9,8},{10,11... | collective-permute-start | bytes 1572872 | tf_op jit(solution)/shard_map/ppermute | solution.py:369
  120.1 3.4 %collective-permute-start.21 = (bf16[2,256,512]{2,1,0:T(8,128)(2,1)}, bf16[2,256,512]{2,1,0:T(8,128)(2,1)S(1)}, u32[]{:S(2)}, u32[]{:S(2)}) collective-permute-start(bf16[2,256,512]{2,1,0:T(8,128)(2,1)} %get-tuple-element.44), channel_id=1, source_target_pairs={{0,1},{1,0},{2,3},{3,2},{4,5},{5,4},{6,7},{7,6},{8,9},{9,8},{10,11... | collective-permute-start | bytes 1572872 | tf_op jit(solution)/shard_map/ppermute | solution.py:369
  123.7 8.6 %collective-permute-start.22 = (bf16[256,512]{1,0:T(8,128)(2,1)S(1)}, bf16[256,512]{1,0:T(8,128)(2,1)S(1)}, u32[]{:S(2)}, u32[]{:S(2)}) collective-permute-start(bf16[256,512]{1,0:T(8,128)(2,1)S(1)} %fusion.2), channel_id=1, source_target_pairs={{0,2},{2,0},{1,3},{3,1},{4,6},{6,4},{5,7},{7,5},{8,10},{10,8},{9,1... | collective-permute-start | bytes 786440 | tf_op jit(solution)/shard_map/ppermute | solution.py:369
  (23 other events, 292.2 us)

commit v4 on v3

--- a/solution.py
+++ b/solution.py
@@ -405,13 +405,12 @@
 
     groups, behind, qkv_parts = [[tokens_in]], [], []
     for at, batch in enumerate(batches):
-        first = after(got[batch[0]], *qkv_parts) if at == 2 else got[batch[0]]
-        mine = join([first] + [got[k] for k in batch[1:]])
+        mine = join([got[k] for k in batch])
         ys = [mine] + [swap(after(mine, *behind), "y", i) for i in range(1, ny)]
         behind = ys[1:]
         parts = []
         for i, a in enumerate(ys):
-            core = after(a, *ys[1:]) if i == 0 else a
+            core = after(a, *ys[1:], *(qkv_parts if at == 2 else [])) if i == 0 else a
             parts += [a] + [swap(core, "c", j) for j in range(1, nc)]
         groups.append(parts)
         if at == 0:

time: 133 us -> 128 us (0.962)
  waiting for transfers between devices: 39.4 us -> 33.1 us
    ppermute x23, waiting for transfers between devices: 39.4 us -> 33.1 us  [swap(): return lax.ppermute(a, axis, [(i, i ^ k) for i in range(n)])]
  transfers between devices with their start and end apart: 24 -> 24, of which waited for: 12 -> 12; matrix products, arithmetic and copies ran while one was open for 5% -> 6% of each run, Pallas kernels for 41% -> 43%
where the time goes in v4:
time: 128 us; the launch traced here: 127 us
  Pallas kernels  54.6 us (43%)
  waiting for transfers between devices  33.1 us (26%)
  starting transfers between devices  24.1 us (19%)
  local copies, waits for them, and re-layouts  7.8 us (6%)
  other arithmetic  3.78 us (3%)
  matrix products  3.15 us (2%)
    ppermute x23, waiting for transfers between devices, swap(): return lax.ppermute(a, axis, [(i, i ^ k) for i in range(n)])  33.1 us
    pallas_call x1, Pallas kernels, attention(): pl.pallas_call(functools.partial(attention_kernel, n_qkv, g_places, late_...  30.7 us
    ppermute x23, starting transfers between devices, swap(): return lax.ppermute(a, axis, [(i, i ^ k) for i in range(n)])  19.3 us
    pallas_call x4, Pallas kernels, join(): pl.pallas_call(join_kernel, out_shape=jax.ShapeDtypeStruct((rows, cols),...  7.77 us
    pallas_call x1, Pallas kernels, weight_grad(): pl.pallas_call(functools.partial(weight_grad_kernel, counts, piece), in_s...  6.6 us
    unnamed x46, local copies, waits for them, and re-layouts  5.72 us
    pallas_call x1, Pallas kernels, project(): pl.pallas_call(functools.partial(project_kernel, counts, piece, tok), gri...  5.72 us
    all_to_all x1, starting transfers between devices, local(): lax.all_to_all(y_sent, ('z', 'x'), 0, 0, tiled=True)  4.76 us
  transfers between devices with their start and end apart: 24, of which 12 were waited for; matrix products, arithmetic and copies ran while one was open for 6% of the time, Pallas kernels for 43%

profile of v4, /device:TPU:0, one launch (start us, length us, event | category | flops | bytes accessed | tf_op | source)
XLA Modules:
  0.0 127.3 jit_solution(18099735323211181017)
XLA Ops:
  1.6 3.0 %collective-permute-start.2 = (bf16[64,2048]{1,0:T(8,128)(2,1)S(1)}, bf16[64,2048]{1,0:T(8,128)(2,1)S(1)}, u32[]{:S(2)}, u32[]{:S(2)}) collective-permute-start(bf16[64,2048]{1,0:T(8,128)(2,1)S(1)} %constant_dynamic-slice_fusion), channel_id=1, source_target_pairs={{0,4},{4,0},{1,5},{5,1},{2,6},{6,2},{3,7},{7,3},{8,12},{12,8},{9,1... | collective-permute-start | bytes 786440 | tf_op jit(solution)/shard_map/ppermute | solution.py:369
  4.6 1.6 %collective-permute-start.1 = (bf16[64,2048]{1,0:T(8,128)(2,1)S(1)}, bf16[64,2048]{1,0:T(8,128)(2,1)S(1)}, u32[]{:S(2)}, u32[]{:S(2)}) collective-permute-start(bf16[64,2048]{1,0:T(8,128)(2,1)S(1)} %constant_dynamic-slice_fusion), channel_id=1, source_target_pairs={{0,8},{8,0},{16,24},{24,16},{1,9},{9,1},{17,25},{25,17},{2,10},{10... | collective-permute-start | bytes 786440 | tf_op jit(solution)/shard_map/ppermute | solution.py:369
  6.2 2.6 %collective-permute-start = (bf16[64,2048]{1,0:T(8,128)(2,1)S(1)}, bf16[64,2048]{1,0:T(8,128)(2,1)S(1)}, u32[]{:S(2)}, u32[]{:S(2)}) collective-permute-start(bf16[64,2048]{1,0:T(8,128)(2,1)S(1)} %constant_dynamic-slice_fusion), channel_id=1, source_target_pairs={{0,16},{8,24},{16,0},{24,8},{1,17},{9,25},{17,1},{25,9},{2,18},{10... | collective-permute-start | bytes 786440 | tf_op jit(solution)/shard_map/ppermute | solution.py:369
  9.4 3.8 %cotangent.1 = (bf16[256,512]{1,0:T(8,128)(2,1)}, bf16[256,512]{1,0:T(8,128)(2,1)}, bf16[8,256,256]{2,1,0:T(8,128)(2,1)}) custom-call(s32[2]{0:T(128)} %pad_add_fusion.1.at_ref, bf16[256,2048]{1,0:T(8,128)(2,1)} %grad_y_ref.1, bf16[512,2048]{1,0:T(8,128)(2,1)} %w_ref.1), custom_call_target="tpu_custom_call" | custom-call | flops 536870912 | bytes 4194304 | tf_op jit(solution)/shard_map/cotangent/pallas_call | solution.py:160
  13.2 4.7 %collective-permute-done.1.refs_1_ = bf16[64,2048]{1,0:T(8,128)(2,1)S(1)} collective-permute-done((bf16[64,2048]{1,0:T(8,128)(2,1)S(1)}, bf16[64,2048]{1,0:T(8,128)(2,1)S(1)}, u32[]{:S(2)}, u32[]{:S(2)}) %collective-permute-start.1) | collective-permute-done | bytes 262176 | tf_op jit(solution)/shard_map/ppermute | solution.py:369
  18.6 1.8 %join.5.refs_1_ = bf16[128,2048]{1,0:T(8,128)(2,1)} custom-call(bf16[64,2048]{1,0:T(8,128)(2,1)} %copy-done.17, bf16[64,2048]{1,0:T(8,128)(2,1)} %copy-done.16), custom_call_target="tpu_custom_call" | custom-call | bytes 1048576 | tf_op jit(solution)/shard_map/join/pallas_call | solution.py:86
  20.4 1.5 %collective-permute-start.4 = (bf16[128,2048]{1,0:T(8,128)(2,1)}, bf16[128,2048]{1,0:T(8,128)(2,1)S(1)}, u32[]{:S(2)}, u32[]{:S(2)}) collective-permute-start(bf16[128,2048]{1,0:T(8,128)(2,1)} %join.5.refs_1_), channel_id=1, source_target_pairs={{0,2},{2,0},{1,3},{3,1},{4,6},{6,4},{5,7},{7,5},{8,10},{10,8},{9,1... | collective-permute-start | bytes 1572872 | tf_op jit(solution)/shard_map/ppermute | solution.py:369
  22.0 2.8 %collective-permute-done.3.refs_1_ = bf16[64,2048]{1,0:T(8,128)(2,1)S(1)} collective-permute-done((bf16[64,2048]{1,0:T(8,128)(2,1)S(1)}, bf16[64,2048]{1,0:T(8,128)(2,1)S(1)}, u32[]{:S(2)}, u32[]{:S(2)}) %collective-permute-start.3) | collective-permute-done | bytes 262176 | tf_op jit(solution)/shard_map/ppermute | solution.py:369
  26.4 1.8 %join.4.refs_0_.refs_5_ = bf16[128,2048]{1,0:T(8,128)(2,1)} custom-call(bf16[64,2048]{1,0:T(8,128)(2,1)} %copy-done.15, bf16[64,2048]{1,0:T(8,128)(2,1)} %copy-done.18), custom_call_target="tpu_custom_call" | custom-call | bytes 1048576 | tf_op jit(solution)/shard_map/join/pallas_call | solution.py:86
  28.2 2.4 %collective-permute-done.8.refs_0_ = bf16[64,2048]{1,0:T(8,128)(2,1)S(1)} collective-permute-done((bf16[64,2048]{1,0:T(8,128)(2,1)S(1)}, bf16[64,2048]{1,0:T(8,128)(2,1)S(1)}, u32[]{:S(2)}, u32[]{:S(2)}) %collective-permute-start.8) | collective-permute-done | bytes 262176 | tf_op jit(solution)/shard_map/ppermute | solution.py:369
  33.1 1.5 %collective-permute-start.5 = (bf16[128,2048]{1,0:T(8,128)(2,1)}, bf16[128,2048]{1,0:T(8,128)(2,1)}, u32[]{:S(2)}, u32[]{:S(2)}) collective-permute-start(bf16[128,2048]{1,0:T(8,128)(2,1)} %join.4.refs_0_.refs_5_), channel_id=1, source_target_pairs={{0,2},{2,0},{1,3},{3,1},{4,6},{6,4},{5,7},{7,5},{8,10},{10,8},{9,1... | collective-permute-start | bytes 1572872 | tf_op jit(solution)/shard_map/ppermute | solution.py:369
  34.6 3.6 %collective-permute-done.18.refs_1_.refs_12_ = bf16[256,512]{1,0:T(8,128)(2,1)S(1)} collective-permute-done((bf16[256,512]{1,0:T(8,128)(2,1)}, bf16[256,512]{1,0:T(8,128)(2,1)S(1)}, u32[]{:S(2)}, u32[]{:S(2)}) %collective-permute-start.18) | collective-permute-done | bytes 262176 | tf_op jit(solution)/shard_map/ppermute | solution.py:369
  39.4 4.8 %collective-permute-done.17.refs_0_.refs_11_ = bf16[256,512]{1,0:T(8,128)(2,1)} collective-permute-done((bf16[256,512]{1,0:T(8,128)(2,1)}, bf16[256,512]{1,0:T(8,128)(2,1)}, u32[]{:S(2)}, u32[]{:S(2)}) %collective-permute-start.17) | collective-permute-done | bytes 262176 | tf_op jit(solution)/shard_map/ppermute | solution.py:369
  44.2 4.9 %collective-permute-done.19.refs_2_.refs_13_ = bf16[256,512]{1,0:T(8,128)(2,1)} collective-permute-done((bf16[256,512]{1,0:T(8,128)(2,1)S(1)}, bf16[256,512]{1,0:T(8,128)(2,1)}, u32[]{:S(2)}, u32[]{:S(2)}) %collective-permute-start.19) | collective-permute-done | bytes 262176 | tf_op jit(solution)/shard_map/ppermute | solution.py:369
  49.1 2.0 %join.7 = bf16[768,512]{1,0:T(8,128)(2,1)} custom-call(bf16[256,512]{1,0:T(8,128)(2,1)} %collective-permute-done.17.refs_0_.refs_11_, bf16[256,512]{1,0:T(8,128)(2,1)} %copy-done.11, bf16[256,512]{1,0:T(8,128)(2,1)} %collective-permute-done.19.refs_2_.refs_13_), custom_call_target="tpu_custom_call" | custom-call | bytes 1572864 | tf_op jit(solution)/shard_map/join/pallas_call | solution.py:86
  51.2 2.0 %join.6.refs_4_.refs_9_ = bf16[192,2048]{1,0:T(8,128)(2,1)} custom-call(bf16[64,2048]{1,0:T(8,128)(2,1)} %copy-done.12, bf16[64,2048]{1,0:T(8,128)(2,1)} %copy-done.13, bf16[64,2048]{1,0:T(8,128)(2,1)} %copy-done.14), custom_call_target="tpu_custom_call" | custom-call | bytes 1572864 | tf_op jit(solution)/shard_map/join/pallas_call | solution.py:86
  56.5 3.0 %copy-done.5 = bf16[3,2048,512]{2,1,0:T(8,128)(2,1)S(1)} copy-done((bf16[3,2048,512]{2,1,0:T(8,128)(2,1)S(1)}, bf16[3,2048,512]{2,1,0:T(8,128)(2,1)}, u32[]{:S(2)}) %copy-start.5) | copy-done | bytes 6291480
  59.4 5.7 %project.1.refs_8_ = bf16[3,768,512]{2,1,0:T(8,128)(2,1)S(1)} custom-call(bf16[256,2048]{1,0:T(8,128)(2,1)S(1)} %copy-done.1, bf16[128,2048]{1,0:T(8,128)(2,1)S(1)} %copy-done, bf16[128,2048]{1,0:T(8,128)(2,1)S(1)} %collective-permute-done.12.refs_2_, bf16[128,2048]{1,0:T(8,128)(2,1)S(1)} %collective-permute-done.4.refs_3_, ...), custom_call_target="tpu_custom_call" | custom-call | flops 4831838208 | bytes 11796480 | tf_op jit(solution)/shard_map/project/pallas_call | solution.py:127
  66.6 5.8 %collective-permute-done.20.refs_14_ = bf16[768,512]{1,0:T(8,128)(2,1)} collective-permute-done((bf16[768,512]{1,0:T(8,128)(2,1)}, bf16[768,512]{1,0:T(8,128)(2,1)}, u32[]{:S(2)}, u32[]{:S(2)}) %collective-permute-start.20) | collective-permute-done | bytes 786464 | tf_op jit(solution)/shard_map/ppermute | solution.py:369
  72.4 4.8 %all-to-all-start = ((bf16[8,256,256]{2,1,0:T(8,128)(2,1)}), bf16[8,256,256]{2,1,0:T(8,128)(2,1)S(1)}, u32[]{:S(2)}, u32[]{:S(2)}) async-start(bf16[8,256,256]{2,1,0:T(8,128)(2,1)} %get-tuple-element.40), calls=%async_computation | async-start | bytes 2097152 | tf_op jit(solution)/shard_map/all_to_all | solution.py:421
  83.4 30.7 %attention.1 = (bf16[3,2048,512]{2,1,0:T(8,128)(2,1)}, bf16[2048,512]{1,0:T(8,128)(2,1)}, bf16[2,256,512]{2,1,0:T(8,128)(2,1)}, f32[2,256,512]{2,1,0:T(8,128)}) custom-call(s32[16,2]{1,0:T(8,128)} %copy.12.cols_ref, s32[16]{0:T(128)} %select_reduce_fusion.2.count_ref, s32[16]{0:T(128)} %get-tuple-element.45.home_ref, s32[4]{0:T(128)} %pad_add_fusion.place_ref, ...), custom_call_target="tpu_custom_call" | custom-call | flops 10000000000 | bytes 31457280 | tf_op jit(solution)/shard_map/attention/pallas_call | solution.py:276
  114.3 3.2 %convolution_convert_fusion = bf16[512,256]{1,0:T(8,128)(2,1)} fusion(bf16[2048,512]{1,0:T(8,128)(2,1)} %get-tuple-element.38, bf16[2048,256]{1,0:T(8,128)(2,1)S(1)} %bitcast.13), kind=kOutput, calls=%fused_computation | convolution fusion | flops 537001984 | bytes 3407872 | tf_op jit(solution)/shard_map/dot_general | solution.py:25
  117.7 2.1 %collective-permute-start.22 = (bf16[256,512]{1,0:T(8,128)(2,1)S(1)}, bf16[256,512]{1,0:T(8,128)(2,1)S(1)}, u32[]{:S(2)}, u32[]{:S(2)}) collective-permute-start(bf16[256,512]{1,0:T(8,128)(2,1)S(1)} %fusion.2), channel_id=1, source_target_pairs={{0,2},{2,0},{1,3},{3,1},{4,6},{6,4},{5,7},{7,5},{8,10},{10,8},{9,1... | collective-permute-start | bytes 786440 | tf_op jit(solution)/shard_map/ppermute | solution.py:369
  119.8 6.6 %weight_grad.1 = bf16[3,256,512]{2,1,0:T(8,128)(2,1)} custom-call(s32[1]{0:T(128)} %bitcast.1.chunk_ref, bf16[256,2048]{1,0:T(8,128)(2,1)} %refs_0_.3, bf16[128,2048]{1,0:T(8,128)(2,1)} %join.5.refs_1_, bf16[128,2048]{1,0:T(8,128)(2,1)} %copy-done.3, bf16[128,2048]{1,0:T(8,128)(2,1)} %copy-done.2, bf16[128,2048]{1,0:T(8,128)(2,1)} %copy-done.4, ...), custom_call_target="tpu_custom_call" | custom-call | flops 1610612736 | bytes 6291456 | tf_op jit(solution)/shard_map/weight_grad/pallas_call | solution.py:335
  (100 shorter events, 19.7 us)
Async XLA Ops:
  1.6 11.6 %collective-permute-start.2 = (bf16[64,2048]{1,0:T(8,128)(2,1)S(1)}, bf16[64,2048]{1,0:T(8,128)(2,1)S(1)}, u32[]{:S(2)}, u32[]{:S(2)}) collective-permute-start(bf16[64,2048]{1,0:T(8,128)(2,1)S(1)} %constant_dynamic-slice_fusion), channel_id=1, source_target_pairs={{0,4},{4,0},{1,5},{5,1},{2,6},{6,2},{3,7},{7,3},{8,12},{12,8},{9,1... | collective-permute-start | bytes 786440 | tf_op jit(solution)/shard_map/ppermute | solution.py:369
  4.6 13.3 %collective-permute-start.1 = (bf16[64,2048]{1,0:T(8,128)(2,1)S(1)}, bf16[64,2048]{1,0:T(8,128)(2,1)S(1)}, u32[]{:S(2)}, u32[]{:S(2)}) collective-permute-start(bf16[64,2048]{1,0:T(8,128)(2,1)S(1)} %constant_dynamic-slice_fusion), channel_id=1, source_target_pairs={{0,8},{8,0},{16,24},{24,16},{1,9},{9,1},{17,25},{25,17},{2,10},{10... | collective-permute-start | bytes 786440 | tf_op jit(solution)/shard_map/ppermute | solution.py:369
  6.2 15.8 %collective-permute-start = (bf16[64,2048]{1,0:T(8,128)(2,1)S(1)}, bf16[64,2048]{1,0:T(8,128)(2,1)S(1)}, u32[]{:S(2)}, u32[]{:S(2)}) collective-permute-start(bf16[64,2048]{1,0:T(8,128)(2,1)S(1)} %constant_dynamic-slice_fusion), channel_id=1, source_target_pairs={{0,16},{8,24},{16,0},{24,8},{1,17},{9,25},{17,1},{25,9},{2,18},{10... | collective-permute-start | bytes 786440 | tf_op jit(solution)/shard_map/ppermute | solution.py:369
  17.9 6.9 %collective-permute-start.3 = (bf16[64,2048]{1,0:T(8,128)(2,1)S(1)}, bf16[64,2048]{1,0:T(8,128)(2,1)S(1)}, u32[]{:S(2)}, u32[]{:S(2)}) collective-permute-start(bf16[64,2048]{1,0:T(8,128)(2,1)S(1)} %collective-permute-done.1.refs_1_), channel_id=1, source_target_pairs={{0,4},{4,0},{1,5},{5,1},{2,6},{6,2},{3,7},{7,3},{8,12},{12,8},{9,1... | collective-permute-start | bytes 786440 | tf_op jit(solution)/shard_map/ppermute | solution.py:369
  20.4 12.7 %collective-permute-start.4 = (bf16[128,2048]{1,0:T(8,128)(2,1)}, bf16[128,2048]{1,0:T(8,128)(2,1)S(1)}, u32[]{:S(2)}, u32[]{:S(2)}) collective-permute-start(bf16[128,2048]{1,0:T(8,128)(2,1)} %join.5.refs_1_), channel_id=1, source_target_pairs={{0,2},{2,0},{1,3},{3,1},{4,6},{6,4},{5,7},{7,5},{8,10},{10,8},{9,1... | collective-permute-start | bytes 1572872 | tf_op jit(solution)/shard_map/ppermute | solution.py:369
  22.0 8.7 %collective-permute-start.8 = (bf16[64,2048]{1,0:T(8,128)(2,1)S(1)}, bf16[64,2048]{1,0:T(8,128)(2,1)S(1)}, u32[]{:S(2)}, u32[]{:S(2)}) collective-permute-start(bf16[64,2048]{1,0:T(8,128)(2,1)S(1)} %collective-permute-done.refs_0_), channel_id=1, source_target_pairs={{0,8},{8,0},{16,24},{24,16},{1,9},{9,1},{17,25},{25,17},{2,10},{10... | collective-permute-start | bytes 786440 | tf_op jit(solution)/shard_map/ppermute | solution.py:369
  24.7 6.8 %collective-permute-start.9 = (bf16[64,2048]{1,0:T(8,128)(2,1)S(1)}, bf16[64,2048]{1,0:T(8,128)(2,1)S(1)}, u32[]{:S(2)}, u32[]{:S(2)}) collective-permute-start(bf16[64,2048]{1,0:T(8,128)(2,1)S(1)} %collective-permute-done.refs_0_), channel_id=1, source_target_pairs={{0,4},{4,0},{1,5},{5,1},{2,6},{6,2},{3,7},{7,3},{8,12},{12,8},{9,1... | collective-permute-start | bytes 786440 | tf_op jit(solution)/shard_map/ppermute | solution.py:369
  25.4 12.8 %collective-permute-start.18 = (bf16[256,512]{1,0:T(8,128)(2,1)}, bf16[256,512]{1,0:T(8,128)(2,1)S(1)}, u32[]{:S(2)}, u32[]{:S(2)}) collective-permute-start(bf16[256,512]{1,0:T(8,128)(2,1)} %get-tuple-element.35), channel_id=1, source_target_pairs={{0,16},{8,24},{16,0},{24,8},{1,17},{9,25},{17,1},{25,9},{2,18},{10... | collective-permute-start | bytes 786440 | tf_op jit(solution)/shard_map/ppermute | solution.py:369
  31.6 6.7 %collective-permute-start.10 = (bf16[64,2048]{1,0:T(8,128)(2,1)S(1)}, bf16[64,2048]{1,0:T(8,128)(2,1)S(1)}, u32[]{:S(2)}, u32[]{:S(2)}) collective-permute-start(bf16[64,2048]{1,0:T(8,128)(2,1)S(1)} %collective-permute-done.8.refs_0_), channel_id=1, source_target_pairs={{0,4},{4,0},{1,5},{5,1},{2,6},{6,2},{3,7},{7,3},{8,12},{12,8},{9,1... | collective-permute-start | bytes 786440 | tf_op jit(solution)/shard_map/ppermute | solution.py:369
  33.1 20.1 %collective-permute-start.5 = (bf16[128,2048]{1,0:T(8,128)(2,1)}, bf16[128,2048]{1,0:T(8,128)(2,1)}, u32[]{:S(2)}, u32[]{:S(2)}) collective-permute-start(bf16[128,2048]{1,0:T(8,128)(2,1)} %join.4.refs_0_.refs_5_), channel_id=1, source_target_pairs={{0,2},{2,0},{1,3},{3,1},{4,6},{6,4},{5,7},{7,5},{8,10},{10,8},{9,1... | collective-permute-start | bytes 1572872 | tf_op jit(solution)/shard_map/ppermute | solution.py:369
  34.6 9.6 %collective-permute-start.17 = (bf16[256,512]{1,0:T(8,128)(2,1)}, bf16[256,512]{1,0:T(8,128)(2,1)}, u32[]{:S(2)}, u32[]{:S(2)}) collective-permute-start(bf16[256,512]{1,0:T(8,128)(2,1)} %get-tuple-element.35), channel_id=1, source_target_pairs={{0,8},{8,0},{16,24},{24,16},{1,9},{9,1},{17,25},{25,17},{2,10},{10... | collective-permute-start | bytes 786440 | tf_op jit(solution)/shard_map/ppermute | solution.py:369
  38.3 10.9 %collective-permute-start.19 = (bf16[256,512]{1,0:T(8,128)(2,1)S(1)}, bf16[256,512]{1,0:T(8,128)(2,1)}, u32[]{:S(2)}, u32[]{:S(2)}) collective-permute-start(bf16[256,512]{1,0:T(8,128)(2,1)S(1)} %collective-permute-done.18.refs_1_.refs_12_), channel_id=1, source_target_pairs={{0,8},{8,0},{16,24},{24,16},{1,9},{9,1},{17,25},{25,17},{2,10},{10... | collective-permute-start | bytes 786440 | tf_op jit(solution)/shard_map/ppermute | solution.py:369
  38.3 14.9 %collective-permute-start.16 = (bf16[256,512]{1,0:T(8,128)(2,1)}, bf16[256,512]{1,0:T(8,128)(2,1)}, u32[]{:S(2)}, u32[]{:S(2)}) collective-permute-start(bf16[256,512]{1,0:T(8,128)(2,1)} %get-tuple-element.35), channel_id=1, source_target_pairs={{0,4},{4,0},{1,5},{5,1},{2,6},{6,2},{3,7},{7,3},{8,12},{12,8},{9,1... | collective-permute-start | bytes 786440 | tf_op jit(solution)/shard_map/ppermute | solution.py:369
  39.4 17.0 %collective-permute-start.12 = (bf16[128,2048]{1,0:T(8,128)(2,1)}, bf16[128,2048]{1,0:T(8,128)(2,1)S(1)}, u32[]{:S(2)}, u32[]{:S(2)}) collective-permute-start(bf16[128,2048]{1,0:T(8,128)(2,1)} %join.5.refs_1_), channel_id=1, source_target_pairs={{0,1},{1,0},{2,3},{3,2},{4,5},{5,4},{6,7},{7,6},{8,9},{9,8},{10,11... | collective-permute-start | bytes 1572872 | tf_op jit(solution)/shard_map/ppermute | solution.py:369
  44.2 12.2 %collective-permute-start.13 = (bf16[128,2048]{1,0:T(8,128)(2,1)S(1)}, bf16[128,2048]{1,0:T(8,128)(2,1)S(1)}, u32[]{:S(2)}, u32[]{:S(2)}) collective-permute-start(bf16[128,2048]{1,0:T(8,128)(2,1)S(1)} %collective-permute-done.4.refs_3_), channel_id=1, source_target_pairs={{0,1},{1,0},{2,3},{3,2},{4,5},{5,4},{6,7},{7,6},{8,9},{9,8},{10,11... | collective-permute-start | bytes 1572872 | tf_op jit(solution)/shard_map/ppermute | solution.py:369
  53.2 19.2 %collective-permute-start.20 = (bf16[768,512]{1,0:T(8,128)(2,1)}, bf16[768,512]{1,0:T(8,128)(2,1)}, u32[]{:S(2)}, u32[]{:S(2)}) collective-permute-start(bf16[768,512]{1,0:T(8,128)(2,1)} %join.7), channel_id=1, source_target_pairs={{0,4},{4,0},{1,5},{5,1},{2,6},{6,2},{3,7},{7,3},{8,12},{12,8},{9,1... | collective-permute-start | bytes 2359304 | tf_op jit(solution)/shard_map/ppermute | solution.py:369
  54.1 23.1 %collective-permute-start.11 = (bf16[192,2048]{1,0:T(8,128)(2,1)}, bf16[192,2048]{1,0:T(8,128)(2,1)}, u32[]{:S(2)}, u32[]{:S(2)}) collective-permute-start(bf16[192,2048]{1,0:T(8,128)(2,1)} %join.6.refs_4_.refs_9_), channel_id=1, source_target_pairs={{0,2},{2,0},{1,3},{3,1},{4,6},{6,4},{5,7},{7,5},{8,10},{10,8},{9,1... | collective-permute-start | bytes 2359304 | tf_op jit(solution)/shard_map/ppermute | solution.py:369
  72.4 41.9 %all-to-all-start = ((bf16[8,256,256]{2,1,0:T(8,128)(2,1)}), bf16[8,256,256]{2,1,0:T(8,128)(2,1)S(1)}, u32[]{:S(2)}, u32[]{:S(2)}) async-start(bf16[8,256,256]{2,1,0:T(8,128)(2,1)} %get-tuple-element.40), calls=%async_computation | async-start | bytes 2097152 | tf_op jit(solution)/shard_map/all_to_all | solution.py:421
  77.2 5.3 %collective-permute-start.14 = (bf16[192,2048]{1,0:T(8,128)(2,1)S(1)}, bf16[192,2048]{1,0:T(8,128)(2,1)S(1)}, u32[]{:S(2)}, u32[]{:S(2)}) collective-permute-start(bf16[192,2048]{1,0:T(8,128)(2,1)S(1)} %copy-done.7), channel_id=1, source_target_pairs={{0,1},{1,0},{2,3},{3,2},{4,5},{5,4},{6,7},{7,6},{8,9},{9,8},{10,11... | collective-permute-start | bytes 2359304 | tf_op jit(solution)/shard_map/ppermute | solution.py:369
  77.3 5.2 %collective-permute-start.15 = (bf16[192,2048]{1,0:T(8,128)(2,1)}, bf16[192,2048]{1,0:T(8,128)(2,1)}, u32[]{:S(2)}, u32[]{:S(2)}) collective-permute-start(bf16[192,2048]{1,0:T(8,128)(2,1)} %collective-permute-done.11.refs_6_.refs_11_), channel_id=1, source_target_pairs={{0,1},{1,0},{2,3},{3,2},{4,5},{5,4},{6,7},{7,6},{8,9},{9,8},{10,11... | collective-permute-start | bytes 2359304 | tf_op jit(solution)/shard_map/ppermute | solution.py:369
  77.8 3.7 %collective-permute-start.6 = (bf16[128,2048]{1,0:T(8,128)(2,1)S(1)}, bf16[128,2048]{1,0:T(8,128)(2,1)}, u32[]{:S(2)}, u32[]{:S(2)}) collective-permute-start(bf16[128,2048]{1,0:T(8,128)(2,1)S(1)} %copy-done.8), channel_id=1, source_target_pairs={{0,1},{1,0},{2,3},{3,2},{4,5},{5,4},{6,7},{7,6},{8,9},{9,8},{10,11... | collective-permute-start | bytes 1572872 | tf_op jit(solution)/shard_map/ppermute | solution.py:369
  77.9 4.6 %collective-permute-start.7 = (bf16[128,2048]{1,0:T(8,128)(2,1)}, bf16[128,2048]{1,0:T(8,128)(2,1)}, u32[]{:S(2)}, u32[]{:S(2)}) collective-permute-start(bf16[128,2048]{1,0:T(8,128)(2,1)} %collective-permute-done.5.refs_2_.refs_7_), channel_id=1, source_target_pairs={{0,1},{1,0},{2,3},{3,2},{4,5},{5,4},{6,7},{7,6},{8,9},{9,8},{10,11... | collective-permute-start | bytes 1572872 | tf_op jit(solution)/shard_map/ppermute | solution.py:369
  114.1 3.4 %collective-permute-start.21 = (bf16[2,256,512]{2,1,0:T(8,128)(2,1)}, bf16[2,256,512]{2,1,0:T(8,128)(2,1)S(1)}, u32[]{:S(2)}, u32[]{:S(2)}) collective-permute-start(bf16[2,256,512]{2,1,0:T(8,128)(2,1)} %get-tuple-element.42), channel_id=1, source_target_pairs={{0,1},{1,0},{2,3},{3,2},{4,5},{5,4},{6,7},{7,6},{8,9},{9,8},{10,11... | collective-permute-start | bytes 1572872 | tf_op jit(solution)/shard_map/ppermute | solution.py:369
  117.7 8.9 %collective-permute-start.22 = (bf16[256,512]{1,0:T(8,128)(2,1)S(1)}, bf16[256,512]{1,0:T(8,128)(2,1)S(1)}, u32[]{:S(2)}, u32[]{:S(2)}) collective-permute-start(bf16[256,512]{1,0:T(8,128)(2,1)S(1)} %fusion.2), channel_id=1, source_target_pairs={{0,2},{2,0},{1,3},{3,1},{4,6},{6,4},{5,7},{7,5},{8,10},{10,8},{9,1... | collective-permute-start | bytes 786440 | tf_op jit(solution)/shard_map/ppermute | solution.py:369
  (23 other events, 261.3 us)

commit v5 on v4

--- a/solution.py
+++ b/solution.py
@@ -191,12 +191,14 @@
             copies.append(pltpu.make_async_copy(part.at[pl.ds(i * tok, tok)], to, g_sems.at[at]))
     weights = load_weights(w_ref, w_held, w_sems)
     late_copies = load_groups(cut(late, late_counts), piece, held, late_sems)
-    for copy in late_copies + weights + copies:
+    for copy in late_copies + weights[:SPLIT]:
         copy.start()
     dk_ref[...] = jnp.zeros_like(dk_ref)
     dv_ref[...] = jnp.zeros_like(dv_ref)
     for copy in late_copies:
         copy.wait()
+    for copy in weights[SPLIT:] + copies:
+        copy.start()
     first = qkv_ref.shape[1] - held.shape[0]
     for c in range(3):
         for copy in weights[c * SPLIT : (c + 1) * SPLIT]:

time: 128 us -> 126 us (0.984)
  Pallas kernels: 54.6 us -> 53 us
    pallas_call x1, Pallas kernels: 30.7 us -> 29.1 us  [attention(): pl.pallas_call(functools.partial(attention_kernel, n_qkv, g_places, late_...]
  transfers between devices with their start and end apart: 24 -> 24, of which waited for: 12 -> 12; matrix products, arithmetic and copies ran while one was open for 6% -> 6% of each run, Pallas kernels for 43% -> 42%
where the time goes in v5:
time: 126 us
  Pallas kernels  53 us (42%)
  waiting for transfers between devices  33.1 us (26%)
  starting transfers between devices  24.2 us (19%)
  local copies, waits for them, and re-layouts  7.8 us (6%)
  other arithmetic  3.78 us (3%)
  matrix products  3.1 us (2%)
    ppermute x23, waiting for transfers between devices, swap(): return lax.ppermute(a, axis, [(i, i ^ k) for i in range(n)])  33.1 us
    pallas_call x1, Pallas kernels, attention(): pl.pallas_call(functools.partial(attention_kernel, n_qkv, g_places, late_...  29.1 us
    ppermute x23, starting transfers between devices, swap(): return lax.ppermute(a, axis, [(i, i ^ k) for i in range(n)])  19.4 us
    pallas_call x4, Pallas kernels, join(): pl.pallas_call(join_kernel, out_shape=jax.ShapeDtypeStruct((rows, cols),...  7.77 us
    pallas_call x1, Pallas kernels, weight_grad(): pl.pallas_call(functools.partial(weight_grad_kernel, counts, piece), in_s...  6.6 us
    unnamed x46, local copies, waits for them, and re-layouts  5.72 us
    pallas_call x1, Pallas kernels, project(): pl.pallas_call(functools.partial(project_kernel, counts, piece, tok), gri...  5.72 us
    all_to_all x1, starting transfers between devices, local(): lax.all_to_all(y_sent, ('z', 'x'), 0, 0, tiled=True)  4.76 us
  transfers between devices with their start and end apart: 24, of which 12 were waited for; matrix products, arithmetic and copies ran while one was open for 6% of the time, Pallas kernels for 42%

profile of v5, /device:TPU:0, one launch (start us, length us, event | category | flops | bytes accessed | tf_op | source)
XLA Modules:
  0.0 125.8 jit_solution(600189349964835230)
XLA Ops:
  1.6 3.0 %collective-permute-start.2 = (bf16[64,2048]{1,0:T(8,128)(2,1)S(1)}, bf16[64,2048]{1,0:T(8,128)(2,1)S(1)}, u32[]{:S(2)}, u32[]{:S(2)}) collective-permute-start(bf16[64,2048]{1,0:T(8,128)(2,1)S(1)} %constant_dynamic-slice_fusion), channel_id=1, source_target_pairs={{0,4},{4,0},{1,5},{5,1},{2,6},{6,2},{3,7},{7,3},{8,12},{12,8},{9,1... | collective-permute-start | bytes 786440 | tf_op jit(solution)/shard_map/ppermute | solution.py:371
  4.6 1.6 %collective-permute-start.1 = (bf16[64,2048]{1,0:T(8,128)(2,1)S(1)}, bf16[64,2048]{1,0:T(8,128)(2,1)S(1)}, u32[]{:S(2)}, u32[]{:S(2)}) collective-permute-start(bf16[64,2048]{1,0:T(8,128)(2,1)S(1)} %constant_dynamic-slice_fusion), channel_id=1, source_target_pairs={{0,8},{8,0},{16,24},{24,16},{1,9},{9,1},{17,25},{25,17},{2,10},{10... | collective-permute-start | bytes 786440 | tf_op jit(solution)/shard_map/ppermute | solution.py:371
  6.2 2.6 %collective-permute-start = (bf16[64,2048]{1,0:T(8,128)(2,1)S(1)}, bf16[64,2048]{1,0:T(8,128)(2,1)S(1)}, u32[]{:S(2)}, u32[]{:S(2)}) collective-permute-start(bf16[64,2048]{1,0:T(8,128)(2,1)S(1)} %constant_dynamic-slice_fusion), channel_id=1, source_target_pairs={{0,16},{8,24},{16,0},{24,8},{1,17},{9,25},{17,1},{25,9},{2,18},{10... | collective-permute-start | bytes 786440 | tf_op jit(solution)/shard_map/ppermute | solution.py:371
  9.4 3.8 %cotangent.1 = (bf16[256,512]{1,0:T(8,128)(2,1)}, bf16[256,512]{1,0:T(8,128)(2,1)}, bf16[8,256,256]{2,1,0:T(8,128)(2,1)}) custom-call(s32[2]{0:T(128)} %pad_add_fusion.1.at_ref, bf16[256,2048]{1,0:T(8,128)(2,1)} %grad_y_ref.1, bf16[512,2048]{1,0:T(8,128)(2,1)} %w_ref.1), custom_call_target="tpu_custom_call" | custom-call | flops 536870912 | bytes 4194304 | tf_op jit(solution)/shard_map/cotangent/pallas_call | solution.py:160
  13.2 4.7 %collective-permute-done.1.refs_1_ = bf16[64,2048]{1,0:T(8,128)(2,1)S(1)} collective-permute-done((bf16[64,2048]{1,0:T(8,128)(2,1)S(1)}, bf16[64,2048]{1,0:T(8,128)(2,1)S(1)}, u32[]{:S(2)}, u32[]{:S(2)}) %collective-permute-start.1) | collective-permute-done | bytes 262176 | tf_op jit(solution)/shard_map/ppermute | solution.py:371
  18.6 1.8 %join.5.refs_1_ = bf16[128,2048]{1,0:T(8,128)(2,1)} custom-call(bf16[64,2048]{1,0:T(8,128)(2,1)} %copy-done.17, bf16[64,2048]{1,0:T(8,128)(2,1)} %copy-done.16), custom_call_target="tpu_custom_call" | custom-call | bytes 1048576 | tf_op jit(solution)/shard_map/join/pallas_call | solution.py:86
  20.4 1.5 %collective-permute-start.4 = (bf16[128,2048]{1,0:T(8,128)(2,1)}, bf16[128,2048]{1,0:T(8,128)(2,1)S(1)}, u32[]{:S(2)}, u32[]{:S(2)}) collective-permute-start(bf16[128,2048]{1,0:T(8,128)(2,1)} %join.5.refs_1_), channel_id=1, source_target_pairs={{0,2},{2,0},{1,3},{3,1},{4,6},{6,4},{5,7},{7,5},{8,10},{10,8},{9,1... | collective-permute-start | bytes 1572872 | tf_op jit(solution)/shard_map/ppermute | solution.py:371
  22.0 2.8 %collective-permute-done.3.refs_1_ = bf16[64,2048]{1,0:T(8,128)(2,1)S(1)} collective-permute-done((bf16[64,2048]{1,0:T(8,128)(2,1)S(1)}, bf16[64,2048]{1,0:T(8,128)(2,1)S(1)}, u32[]{:S(2)}, u32[]{:S(2)}) %collective-permute-start.3) | collective-permute-done | bytes 262176 | tf_op jit(solution)/shard_map/ppermute | solution.py:371
  26.4 1.8 %join.4.refs_0_.refs_5_ = bf16[128,2048]{1,0:T(8,128)(2,1)} custom-call(bf16[64,2048]{1,0:T(8,128)(2,1)} %copy-done.15, bf16[64,2048]{1,0:T(8,128)(2,1)} %copy-done.18), custom_call_target="tpu_custom_call" | custom-call | bytes 1048576 | tf_op jit(solution)/shard_map/join/pallas_call | solution.py:86
  28.2 2.4 %collective-permute-done.8.refs_0_ = bf16[64,2048]{1,0:T(8,128)(2,1)S(1)} collective-permute-done((bf16[64,2048]{1,0:T(8,128)(2,1)S(1)}, bf16[64,2048]{1,0:T(8,128)(2,1)S(1)}, u32[]{:S(2)}, u32[]{:S(2)}) %collective-permute-start.8) | collective-permute-done | bytes 262176 | tf_op jit(solution)/shard_map/ppermute | solution.py:371
  33.1 1.5 %collective-permute-start.5 = (bf16[128,2048]{1,0:T(8,128)(2,1)}, bf16[128,2048]{1,0:T(8,128)(2,1)}, u32[]{:S(2)}, u32[]{:S(2)}) collective-permute-start(bf16[128,2048]{1,0:T(8,128)(2,1)} %join.4.refs_0_.refs_5_), channel_id=1, source_target_pairs={{0,2},{2,0},{1,3},{3,1},{4,6},{6,4},{5,7},{7,5},{8,10},{10,8},{9,1... | collective-permute-start | bytes 1572872 | tf_op jit(solution)/shard_map/ppermute | solution.py:371
  34.6 3.6 %collective-permute-done.18.refs_1_.refs_12_ = bf16[256,512]{1,0:T(8,128)(2,1)S(1)} collective-permute-done((bf16[256,512]{1,0:T(8,128)(2,1)}, bf16[256,512]{1,0:T(8,128)(2,1)S(1)}, u32[]{:S(2)}, u32[]{:S(2)}) %collective-permute-start.18) | collective-permute-done | bytes 262176 | tf_op jit(solution)/shard_map/ppermute | solution.py:371
  39.4 4.8 %collective-permute-done.17.refs_0_.refs_11_ = bf16[256,512]{1,0:T(8,128)(2,1)} collective-permute-done((bf16[256,512]{1,0:T(8,128)(2,1)}, bf16[256,512]{1,0:T(8,128)(2,1)}, u32[]{:S(2)}, u32[]{:S(2)}) %collective-permute-start.17) | collective-permute-done | bytes 262176 | tf_op jit(solution)/shard_map/ppermute | solution.py:371
  44.2 4.9 %collective-permute-done.19.refs_2_.refs_13_ = bf16[256,512]{1,0:T(8,128)(2,1)} collective-permute-done((bf16[256,512]{1,0:T(8,128)(2,1)S(1)}, bf16[256,512]{1,0:T(8,128)(2,1)}, u32[]{:S(2)}, u32[]{:S(2)}) %collective-permute-start.19) | collective-permute-done | bytes 262176 | tf_op jit(solution)/shard_map/ppermute | solution.py:371
  49.1 2.0 %join.7 = bf16[768,512]{1,0:T(8,128)(2,1)} custom-call(bf16[256,512]{1,0:T(8,128)(2,1)} %collective-permute-done.17.refs_0_.refs_11_, bf16[256,512]{1,0:T(8,128)(2,1)} %copy-done.11, bf16[256,512]{1,0:T(8,128)(2,1)} %collective-permute-done.19.refs_2_.refs_13_), custom_call_target="tpu_custom_call" | custom-call | bytes 1572864 | tf_op jit(solution)/shard_map/join/pallas_call | solution.py:86
  51.2 2.0 %join.6.refs_4_.refs_9_ = bf16[192,2048]{1,0:T(8,128)(2,1)} custom-call(bf16[64,2048]{1,0:T(8,128)(2,1)} %copy-done.12, bf16[64,2048]{1,0:T(8,128)(2,1)} %copy-done.13, bf16[64,2048]{1,0:T(8,128)(2,1)} %copy-done.14), custom_call_target="tpu_custom_call" | custom-call | bytes 1572864 | tf_op jit(solution)/shard_map/join/pallas_call | solution.py:86
  56.5 3.0 %copy-done.5 = bf16[3,2048,512]{2,1,0:T(8,128)(2,1)S(1)} copy-done((bf16[3,2048,512]{2,1,0:T(8,128)(2,1)S(1)}, bf16[3,2048,512]{2,1,0:T(8,128)(2,1)}, u32[]{:S(2)}) %copy-start.5) | copy-done | bytes 6291480
  59.4 5.7 %project.1.refs_8_ = bf16[3,768,512]{2,1,0:T(8,128)(2,1)S(1)} custom-call(bf16[256,2048]{1,0:T(8,128)(2,1)S(1)} %copy-done.1, bf16[128,2048]{1,0:T(8,128)(2,1)S(1)} %copy-done, bf16[128,2048]{1,0:T(8,128)(2,1)S(1)} %collective-permute-done.12.refs_2_, bf16[128,2048]{1,0:T(8,128)(2,1)S(1)} %collective-permute-done.4.refs_3_, ...), custom_call_target="tpu_custom_call" | custom-call | flops 4831838208 | bytes 11796480 | tf_op jit(solution)/shard_map/project/pallas_call | solution.py:127
  66.6 5.8 %collective-permute-done.20.refs_14_ = bf16[768,512]{1,0:T(8,128)(2,1)} collective-permute-done((bf16[768,512]{1,0:T(8,128)(2,1)}, bf16[768,512]{1,0:T(8,128)(2,1)}, u32[]{:S(2)}, u32[]{:S(2)}) %collective-permute-start.20) | collective-permute-done | bytes 786464 | tf_op jit(solution)/shard_map/ppermute | solution.py:371
  72.4 4.8 %all-to-all-start = ((bf16[8,256,256]{2,1,0:T(8,128)(2,1)}), bf16[8,256,256]{2,1,0:T(8,128)(2,1)S(1)}, u32[]{:S(2)}, u32[]{:S(2)}) async-start(bf16[8,256,256]{2,1,0:T(8,128)(2,1)} %get-tuple-element.40), calls=%async_computation | async-start | bytes 2097152 | tf_op jit(solution)/shard_map/all_to_all | solution.py:423
  83.4 29.1 %attention.1 = (bf16[3,2048,512]{2,1,0:T(8,128)(2,1)}, bf16[2048,512]{1,0:T(8,128)(2,1)}, bf16[2,256,512]{2,1,0:T(8,128)(2,1)}, f32[2,256,512]{2,1,0:T(8,128)}) custom-call(s32[16,2]{1,0:T(8,128)} %copy.12.cols_ref, s32[16]{0:T(128)} %select_reduce_fusion.2.count_ref, s32[16]{0:T(128)} %get-tuple-element.45.home_ref, s32[4]{0:T(128)} %pad_add_fusion.place_ref, ...), custom_call_target="tpu_custom_call" | custom-call | flops 10000000000 | bytes 31457280 | tf_op jit(solution)/shard_map/attention/pallas_call | solution.py:278
  112.8 3.1 %convolution_convert_fusion = bf16[512,256]{1,0:T(8,128)(2,1)} fusion(bf16[2048,512]{1,0:T(8,128)(2,1)} %get-tuple-element.38, bf16[2048,256]{1,0:T(8,128)(2,1)S(1)} %bitcast.13), kind=kOutput, calls=%fused_computation | convolution fusion | flops 537001984 | bytes 3407872 | tf_op jit(solution)/shard_map/dot_general | solution.py:25
  116.1 2.2 %collective-permute-start.22 = (bf16[256,512]{1,0:T(8,128)(2,1)S(1)}, bf16[256,512]{1,0:T(8,128)(2,1)S(1)}, u32[]{:S(2)}, u32[]{:S(2)}) collective-permute-start(bf16[256,512]{1,0:T(8,128)(2,1)S(1)} %fusion.2), channel_id=1, source_target_pairs={{0,2},{2,0},{1,3},{3,1},{4,6},{6,4},{5,7},{7,5},{8,10},{10,8},{9,1... | collective-permute-start | bytes 786440 | tf_op jit(solution)/shard_map/ppermute | solution.py:371
  118.3 6.6 %weight_grad.1 = bf16[3,256,512]{2,1,0:T(8,128)(2,1)} custom-call(s32[1]{0:T(128)} %bitcast.1.chunk_ref, bf16[256,2048]{1,0:T(8,128)(2,1)} %refs_0_.3, bf16[128,2048]{1,0:T(8,128)(2,1)} %join.5.refs_1_, bf16[128,2048]{1,0:T(8,128)(2,1)} %copy-done.3, bf16[128,2048]{1,0:T(8,128)(2,1)} %copy-done.2, bf16[128,2048]{1,0:T(8,128)(2,1)} %copy-done.4, ...), custom_call_target="tpu_custom_call" | custom-call | flops 1610612736 | bytes 6291456 | tf_op jit(solution)/shard_map/weight_grad/pallas_call | solution.py:337
  (100 shorter events, 19.7 us)
Async XLA Ops:
  1.6 11.6 %collective-permute-start.2 = (bf16[64,2048]{1,0:T(8,128)(2,1)S(1)}, bf16[64,2048]{1,0:T(8,128)(2,1)S(1)}, u32[]{:S(2)}, u32[]{:S(2)}) collective-permute-start(bf16[64,2048]{1,0:T(8,128)(2,1)S(1)} %constant_dynamic-slice_fusion), channel_id=1, source_target_pairs={{0,4},{4,0},{1,5},{5,1},{2,6},{6,2},{3,7},{7,3},{8,12},{12,8},{9,1... | collective-permute-start | bytes 786440 | tf_op jit(solution)/shard_map/ppermute | solution.py:371
  4.6 13.3 %collective-permute-start.1 = (bf16[64,2048]{1,0:T(8,128)(2,1)S(1)}, bf16[64,2048]{1,0:T(8,128)(2,1)S(1)}, u32[]{:S(2)}, u32[]{:S(2)}) collective-permute-start(bf16[64,2048]{1,0:T(8,128)(2,1)S(1)} %constant_dynamic-slice_fusion), channel_id=1, source_target_pairs={{0,8},{8,0},{16,24},{24,16},{1,9},{9,1},{17,25},{25,17},{2,10},{10... | collective-permute-start | bytes 786440 | tf_op jit(solution)/shard_map/ppermute | solution.py:371
  6.2 15.8 %collective-permute-start = (bf16[64,2048]{1,0:T(8,128)(2,1)S(1)}, bf16[64,2048]{1,0:T(8,128)(2,1)S(1)}, u32[]{:S(2)}, u32[]{:S(2)}) collective-permute-start(bf16[64,2048]{1,0:T(8,128)(2,1)S(1)} %constant_dynamic-slice_fusion), channel_id=1, source_target_pairs={{0,16},{8,24},{16,0},{24,8},{1,17},{9,25},{17,1},{25,9},{2,18},{10... | collective-permute-start | bytes 786440 | tf_op jit(solution)/shard_map/ppermute | solution.py:371
  17.9 6.9 %collective-permute-start.3 = (bf16[64,2048]{1,0:T(8,128)(2,1)S(1)}, bf16[64,2048]{1,0:T(8,128)(2,1)S(1)}, u32[]{:S(2)}, u32[]{:S(2)}) collective-permute-start(bf16[64,2048]{1,0:T(8,128)(2,1)S(1)} %collective-permute-done.1.refs_1_), channel_id=1, source_target_pairs={{0,4},{4,0},{1,5},{5,1},{2,6},{6,2},{3,7},{7,3},{8,12},{12,8},{9,1... | collective-permute-start | bytes 786440 | tf_op jit(solution)/shard_map/ppermute | solution.py:371
  20.4 12.7 %collective-permute-start.4 = (bf16[128,2048]{1,0:T(8,128)(2,1)}, bf16[128,2048]{1,0:T(8,128)(2,1)S(1)}, u32[]{:S(2)}, u32[]{:S(2)}) collective-permute-start(bf16[128,2048]{1,0:T(8,128)(2,1)} %join.5.refs_1_), channel_id=1, source_target_pairs={{0,2},{2,0},{1,3},{3,1},{4,6},{6,4},{5,7},{7,5},{8,10},{10,8},{9,1... | collective-permute-start | bytes 1572872 | tf_op jit(solution)/shard_map/ppermute | solution.py:371
  22.0 8.7 %collective-permute-start.8 = (bf16[64,2048]{1,0:T(8,128)(2,1)S(1)}, bf16[64,2048]{1,0:T(8,128)(2,1)S(1)}, u32[]{:S(2)}, u32[]{:S(2)}) collective-permute-start(bf16[64,2048]{1,0:T(8,128)(2,1)S(1)} %collective-permute-done.refs_0_), channel_id=1, source_target_pairs={{0,8},{8,0},{16,24},{24,16},{1,9},{9,1},{17,25},{25,17},{2,10},{10... | collective-permute-start | bytes 786440 | tf_op jit(solution)/shard_map/ppermute | solution.py:371
  24.7 6.8 %collective-permute-start.9 = (bf16[64,2048]{1,0:T(8,128)(2,1)S(1)}, bf16[64,2048]{1,0:T(8,128)(2,1)S(1)}, u32[]{:S(2)}, u32[]{:S(2)}) collective-permute-start(bf16[64,2048]{1,0:T(8,128)(2,1)S(1)} %collective-permute-done.refs_0_), channel_id=1, source_target_pairs={{0,4},{4,0},{1,5},{5,1},{2,6},{6,2},{3,7},{7,3},{8,12},{12,8},{9,1... | collective-permute-start | bytes 786440 | tf_op jit(solution)/shard_map/ppermute | solution.py:371
  25.4 12.8 %collective-permute-start.18 = (bf16[256,512]{1,0:T(8,128)(2,1)}, bf16[256,512]{1,0:T(8,128)(2,1)S(1)}, u32[]{:S(2)}, u32[]{:S(2)}) collective-permute-start(bf16[256,512]{1,0:T(8,128)(2,1)} %get-tuple-element.35), channel_id=1, source_target_pairs={{0,16},{8,24},{16,0},{24,8},{1,17},{9,25},{17,1},{25,9},{2,18},{10... | collective-permute-start | bytes 786440 | tf_op jit(solution)/shard_map/ppermute | solution.py:371
  31.6 6.7 %collective-permute-start.10 = (bf16[64,2048]{1,0:T(8,128)(2,1)S(1)}, bf16[64,2048]{1,0:T(8,128)(2,1)S(1)}, u32[]{:S(2)}, u32[]{:S(2)}) collective-permute-start(bf16[64,2048]{1,0:T(8,128)(2,1)S(1)} %collective-permute-done.8.refs_0_), channel_id=1, source_target_pairs={{0,4},{4,0},{1,5},{5,1},{2,6},{6,2},{3,7},{7,3},{8,12},{12,8},{9,1... | collective-permute-start | bytes 786440 | tf_op jit(solution)/shard_map/ppermute | solution.py:371
  33.1 20.1 %collective-permute-start.5 = (bf16[128,2048]{1,0:T(8,128)(2,1)}, bf16[128,2048]{1,0:T(8,128)(2,1)}, u32[]{:S(2)}, u32[]{:S(2)}) collective-permute-start(bf16[128,2048]{1,0:T(8,128)(2,1)} %join.4.refs_0_.refs_5_), channel_id=1, source_target_pairs={{0,2},{2,0},{1,3},{3,1},{4,6},{6,4},{5,7},{7,5},{8,10},{10,8},{9,1... | collective-permute-start | bytes 1572872 | tf_op jit(solution)/shard_map/ppermute | solution.py:371
  34.6 9.6 %collective-permute-start.17 = (bf16[256,512]{1,0:T(8,128)(2,1)}, bf16[256,512]{1,0:T(8,128)(2,1)}, u32[]{:S(2)}, u32[]{:S(2)}) collective-permute-start(bf16[256,512]{1,0:T(8,128)(2,1)} %get-tuple-element.35), channel_id=1, source_target_pairs={{0,8},{8,0},{16,24},{24,16},{1,9},{9,1},{17,25},{25,17},{2,10},{10... | collective-permute-start | bytes 786440 | tf_op jit(solution)/shard_map/ppermute | solution.py:371
  38.3 10.9 %collective-permute-start.19 = (bf16[256,512]{1,0:T(8,128)(2,1)S(1)}, bf16[256,512]{1,0:T(8,128)(2,1)}, u32[]{:S(2)}, u32[]{:S(2)}) collective-permute-start(bf16[256,512]{1,0:T(8,128)(2,1)S(1)} %collective-permute-done.18.refs_1_.refs_12_), channel_id=1, source_target_pairs={{0,8},{8,0},{16,24},{24,16},{1,9},{9,1},{17,25},{25,17},{2,10},{10... | collective-permute-start | bytes 786440 | tf_op jit(solution)/shard_map/ppermute | solution.py:371
  38.3 14.9 %collective-permute-start.16 = (bf16[256,512]{1,0:T(8,128)(2,1)}, bf16[256,512]{1,0:T(8,128)(2,1)}, u32[]{:S(2)}, u32[]{:S(2)}) collective-permute-start(bf16[256,512]{1,0:T(8,128)(2,1)} %get-tuple-element.35), channel_id=1, source_target_pairs={{0,4},{4,0},{1,5},{5,1},{2,6},{6,2},{3,7},{7,3},{8,12},{12,8},{9,1... | collective-permute-start | bytes 786440 | tf_op jit(solution)/shard_map/ppermute | solution.py:371
  39.4 17.0 %collective-permute-start.12 = (bf16[128,2048]{1,0:T(8,128)(2,1)}, bf16[128,2048]{1,0:T(8,128)(2,1)S(1)}, u32[]{:S(2)}, u32[]{:S(2)}) collective-permute-start(bf16[128,2048]{1,0:T(8,128)(2,1)} %join.5.refs_1_), channel_id=1, source_target_pairs={{0,1},{1,0},{2,3},{3,2},{4,5},{5,4},{6,7},{7,6},{8,9},{9,8},{10,11... | collective-permute-start | bytes 1572872 | tf_op jit(solution)/shard_map/ppermute | solution.py:371
  44.2 12.2 %collective-permute-start.13 = (bf16[128,2048]{1,0:T(8,128)(2,1)S(1)}, bf16[128,2048]{1,0:T(8,128)(2,1)S(1)}, u32[]{:S(2)}, u32[]{:S(2)}) collective-permute-start(bf16[128,2048]{1,0:T(8,128)(2,1)S(1)} %collective-permute-done.4.refs_3_), channel_id=1, source_target_pairs={{0,1},{1,0},{2,3},{3,2},{4,5},{5,4},{6,7},{7,6},{8,9},{9,8},{10,11... | collective-permute-start | bytes 1572872 | tf_op jit(solution)/shard_map/ppermute | solution.py:371
  53.2 19.2 %collective-permute-start.20 = (bf16[768,512]{1,0:T(8,128)(2,1)}, bf16[768,512]{1,0:T(8,128)(2,1)}, u32[]{:S(2)}, u32[]{:S(2)}) collective-permute-start(bf16[768,512]{1,0:T(8,128)(2,1)} %join.7), channel_id=1, source_target_pairs={{0,4},{4,0},{1,5},{5,1},{2,6},{6,2},{3,7},{7,3},{8,12},{12,8},{9,1... | collective-permute-start | bytes 2359304 | tf_op jit(solution)/shard_map/ppermute | solution.py:371
  54.1 23.1 %collective-permute-start.11 = (bf16[192,2048]{1,0:T(8,128)(2,1)}, bf16[192,2048]{1,0:T(8,128)(2,1)}, u32[]{:S(2)}, u32[]{:S(2)}) collective-permute-start(bf16[192,2048]{1,0:T(8,128)(2,1)} %join.6.refs_4_.refs_9_), channel_id=1, source_target_pairs={{0,2},{2,0},{1,3},{3,1},{4,6},{6,4},{5,7},{7,5},{8,10},{10,8},{9,1... | collective-permute-start | bytes 2359304 | tf_op jit(solution)/shard_map/ppermute | solution.py:371
  72.4 40.4 %all-to-all-start = ((bf16[8,256,256]{2,1,0:T(8,128)(2,1)}), bf16[8,256,256]{2,1,0:T(8,128)(2,1)S(1)}, u32[]{:S(2)}, u32[]{:S(2)}) async-start(bf16[8,256,256]{2,1,0:T(8,128)(2,1)} %get-tuple-element.40), calls=%async_computation | async-start | bytes 2097152 | tf_op jit(solution)/shard_map/all_to_all | solution.py:423
  77.2 5.3 %collective-permute-start.14 = (bf16[192,2048]{1,0:T(8,128)(2,1)S(1)}, bf16[192,2048]{1,0:T(8,128)(2,1)S(1)}, u32[]{:S(2)}, u32[]{:S(2)}) collective-permute-start(bf16[192,2048]{1,0:T(8,128)(2,1)S(1)} %copy-done.7), channel_id=1, source_target_pairs={{0,1},{1,0},{2,3},{3,2},{4,5},{5,4},{6,7},{7,6},{8,9},{9,8},{10,11... | collective-permute-start | bytes 2359304 | tf_op jit(solution)/shard_map/ppermute | solution.py:371
  77.3 5.2 %collective-permute-start.15 = (bf16[192,2048]{1,0:T(8,128)(2,1)}, bf16[192,2048]{1,0:T(8,128)(2,1)}, u32[]{:S(2)}, u32[]{:S(2)}) collective-permute-start(bf16[192,2048]{1,0:T(8,128)(2,1)} %collective-permute-done.11.refs_6_.refs_11_), channel_id=1, source_target_pairs={{0,1},{1,0},{2,3},{3,2},{4,5},{5,4},{6,7},{7,6},{8,9},{9,8},{10,11... | collective-permute-start | bytes 2359304 | tf_op jit(solution)/shard_map/ppermute | solution.py:371
  77.8 3.7 %collective-permute-start.6 = (bf16[128,2048]{1,0:T(8,128)(2,1)S(1)}, bf16[128,2048]{1,0:T(8,128)(2,1)}, u32[]{:S(2)}, u32[]{:S(2)}) collective-permute-start(bf16[128,2048]{1,0:T(8,128)(2,1)S(1)} %copy-done.8), channel_id=1, source_target_pairs={{0,1},{1,0},{2,3},{3,2},{4,5},{5,4},{6,7},{7,6},{8,9},{9,8},{10,11... | collective-permute-start | bytes 1572872 | tf_op jit(solution)/shard_map/ppermute | solution.py:371
  77.9 4.6 %collective-permute-start.7 = (bf16[128,2048]{1,0:T(8,128)(2,1)}, bf16[128,2048]{1,0:T(8,128)(2,1)}, u32[]{:S(2)}, u32[]{:S(2)}) collective-permute-start(bf16[128,2048]{1,0:T(8,128)(2,1)} %collective-permute-done.5.refs_2_.refs_7_), channel_id=1, source_target_pairs={{0,1},{1,0},{2,3},{3,2},{4,5},{5,4},{6,7},{7,6},{8,9},{9,8},{10,11... | collective-permute-start | bytes 1572872 | tf_op jit(solution)/shard_map/ppermute | solution.py:371
  112.6 3.4 %collective-permute-start.21 = (bf16[2,256,512]{2,1,0:T(8,128)(2,1)}, bf16[2,256,512]{2,1,0:T(8,128)(2,1)S(1)}, u32[]{:S(2)}, u32[]{:S(2)}) collective-permute-start(bf16[2,256,512]{2,1,0:T(8,128)(2,1)} %get-tuple-element.42), channel_id=1, source_target_pairs={{0,1},{1,0},{2,3},{3,2},{4,5},{5,4},{6,7},{7,6},{8,9},{9,8},{10,11... | collective-permute-start | bytes 1572872 | tf_op jit(solution)/shard_map/ppermute | solution.py:371
  116.1 8.9 %collective-permute-start.22 = (bf16[256,512]{1,0:T(8,128)(2,1)S(1)}, bf16[256,512]{1,0:T(8,128)(2,1)S(1)}, u32[]{:S(2)}, u32[]{:S(2)}) collective-permute-start(bf16[256,512]{1,0:T(8,128)(2,1)S(1)} %fusion.2), channel_id=1, source_target_pairs={{0,2},{2,0},{1,3},{3,1},{4,6},{6,4},{5,7},{7,5},{8,10},{10,8},{9,1... | collective-permute-start | bytes 786440 | tf_op jit(solution)/shard_map/ppermute | solution.py:371
  (23 other events, 261.3 us)
